TPU v7x, 32 devices: a whole 2x2x4 slice. The times are simulated.
32 devices in a mesh: section: 2 (over y), dp: 2 (over x), tensor: 8 (over z, core).
Axes of the slice: x: 2, y: 2, z: 4, core: 2. Of those that a mesh axis runs over, the one named last changes fastest.
Arguments:
- incoming: bfloat16 [2, 512, 12288], P('section', 'tensor', 'dp'), may hold values from -24 to 24, as said below
- norm_gain: float32 [2, 12288], P('section', 'dp'), may hold values from 0.1 to 1.9
- norm_shift: float32 [2, 12288], P('section', 'dp'), may hold values from -3 to 3
- up_weight: bfloat16 [2, 12288, 24576], P('section', 'dp', 'tensor'), may hold values from -0.0546875 to 0.0546875
- up_bias: float32 [2, 24576], P('section', 'tensor'), may hold values from -4 to 4
- down_weight: bfloat16 [2, 24576, 12288], P('section', 'tensor', 'dp'), may hold values from -0.0390625 to 0.0390625
- down_bias: float32 [2, 12288], P('section', 'dp'), may hold values from -3 to 3
Outputs:
- rotated: bfloat16 [2, 512, 12288], P('section', 'tensor', 'dp')
Inputs may be any that keep to these rules, and one draw needn't show every extreme that they name: `incoming`: token rows and feature columns carry different scales.
All inputs are finite; a program needn't handle non-finite values.
Results may differ from a plain program's by a relative error of at most 0.004.
Values may be sent and summed in bfloat16 or wider, within the bound.
No kernel may reach another device: no remote copies, remote signals or barrier semaphores. Data moves between devices by JAX's collectives and lax.ppermute only.
A program may use at most 192 MiB of HBM per device.

v0:
```python
import jax
import jax.numpy as jnp
from jax import lax
from jax.sharding import PartitionSpec as P

D = 12288


def from_behind(block, axis, distance):
    devices = range(lax.axis_size(axis))
    route = [((i - distance) % len(devices), i) for i in devices]
    return lax.ppermute(block, axis, route)


def per_device(incoming, norm_gain, norm_shift, up_weight, up_bias, down_weight, down_bias):
    x = incoming[0].astype(jnp.float32)
    gain = norm_gain[0]
    shift = norm_shift[0]
    up_w = up_weight[0]
    up_b = up_bias[0]
    down_w = down_weight[0]
    down_b = down_bias[0]
    total, square = lax.psum((jnp.sum(x, axis=1), jnp.sum(x * x, axis=1)), "dp")
    mean = total / D
    var = square / D - mean * mean
    normed = ((x - mean[:, None]) * lax.rsqrt(var + 1e-05)[:, None] * gain + shift).astype(
        jnp.bfloat16
    )
    partial_value = jnp.dot(
        lax.all_gather(normed, "tensor", axis=0, tiled=True),
        up_w,
        preferred_element_type=jnp.float32,
    )
    share = lax.psum_scatter(partial_value, "dp", scatter_dimension=0, tiled=True)
    act = jax.nn.gelu(share + up_b, approximate=True).astype(jnp.bfloat16)
    terms = jnp.dot(
        lax.all_gather(act, "dp", axis=0, tiled=True), down_w, preferred_element_type=jnp.float32
    )
    summed = lax.psum_scatter(terms, "tensor", scatter_dimension=0, tiled=True)
    result = (summed + down_b + x).astype(jnp.bfloat16)
    moved = from_behind(result, "section", 1)
    return moved[None]


def solution(mesh):
    placed = (
        P("section", "tensor", "dp"),
        P("section", "dp"),
        P("section", "dp"),
        P("section", "dp", "tensor"),
        P("section", "tensor"),
        P("section", "tensor", "dp"),
        P("section", "dp"),
    )
    return jax.shard_map(
        per_device,
        mesh=mesh,
        in_specs=placed,
        out_specs=P("section", "tensor", "dp"),
        check_vma=False,
    )
```

profile of v0, /device:TPU:0, one launch (start us, length us, event | category | flops | bytes accessed | tf_op | source)
XLA Modules:
  0.0 419.4 jit_solution(15745174504196099781)
XLA Ops:
  6.5 1.4 fusion.19
  7.9 1.3 convert_reduce_fusion
  9.3 5.8 %all-reduce = (f32[64]{0:T(128)S(1)}, f32[64]{0:T(128)S(1)}) all-reduce(f32[64]{0:T(128)S(1)} %fusion.19, f32[64]{0:T(128)S(1)} %convert_reduce_fusion), channel_id=1, replica_groups=mesh['section'=2,'dp'=2,'tensor'=8] {'dp'}, use_global_device_ids=true, to_apply=%region_3.0 | all-reduce | flops 128 | bytes 1024 | tf_op jit(solution)/shard_map/psum | solution.py:23
  15.1 2.4 fusion.18
  17.5 0.0 all-gather.3.cloned.1.call-update
  17.5 0.0 reduce-scatter.3.cloned.1.call-start
  17.6 66.7 %all-gather.3.cloned.1.call-done = bf16[512,6144]{1,0:T(8,128)(2,1)} async-done(((bf16[64,6144]{1,0:T(8,128)(2,1)}), bf16[512,6144]{1,0:T(8,128)(2,1)}) %all-gather.3.cloned.1.call-update) | async-done | bytes 6291472 | tf_op jit(solution)/shard_map/all_gather | solution.py:30
  84.3 26.9 %fusion.2 = f32[512,3072]{1,0:T(8,128)} fusion(bf16[512,6144]{1,0:T(8,128)(2,1)} %all-gather.3.cloned.1.call-done, bf16[1,6144,3072]{2,1,0:T(8,128)(2,1)} %param.10), kind=kOutput, calls=%fused_computation.2 | convolution fusion | flops 19327352832 | bytes 50331648 | tf_op jit(solution)/shard_map/dot_general | solution.py:29
  111.2 0.0 reduce-scatter.3.cloned.1.call-update
  111.2 0.0 all-gather.5.cloned.1.call-start
  111.3 75.8 %reduce-scatter.3.cloned.1.call-done = f32[256,3072]{1,0:T(8,128)} async-done(((f32[512,3072]{1,0:T(8,128)}), f32[256,3072]{1,0:T(8,128)}) %reduce-scatter.3.cloned.1.call-update) | async-done | bytes 3145744 | tf_op jit(solution)/shard_map/reduce_scatter | solution.py:34
  187.1 0.0 copy-done.2
  187.1 4.1 fusion.11
  191.2 0.0 all-gather.5.cloned.1.call-update
  191.2 0.0 reduce-scatter.5.cloned.1.call-start
  191.3 45.0 %all-gather.5.cloned.1.call-done = bf16[512,3072]{1,0:T(8,128)(2,1)} async-done(((bf16[256,3072]{1,0:T(8,128)(2,1)}), bf16[512,3072]{1,0:T(8,128)(2,1)}) %all-gather.5.cloned.1.call-update) | async-done | bytes 3145744 | tf_op jit(solution)/shard_map/all_gather | solution.py:37
  236.3 27.4 %fusion = f32[512,6144]{1,0:T(8,128)} fusion(bf16[512,3072]{1,0:T(8,128)(2,1)} %all-gather.5.cloned.1.call-done, bf16[1,3072,6144]{2,1,0:T(8,128)(2,1)} %param.12), kind=kOutput, calls=%fused_computation | convolution fusion | flops 19327352832 | bytes 53477376 | tf_op jit(solution)/shard_map/dot_general | solution.py:36
  263.8 0.0 reduce-scatter.5.cloned.1.call-update
  263.8 129.4 %reduce-scatter.5.cloned.1.call-done = f32[64,6144]{1,0:T(8,128)} async-done(((f32[512,6144]{1,0:T(8,128)}), f32[64,6144]{1,0:T(8,128)}) %reduce-scatter.5.cloned.1.call-update) | async-done | bytes 1572880 | tf_op jit(solution)/shard_map/reduce_scatter | solution.py:39
  393.2 0.0 copy-done
  393.2 1.6 fusion.20
  394.8 1.5 collective-permute-start
  396.3 15.7 %collective-permute-done = bf16[64,6144]{1,0:T(8,128)(2,1)S(1)} collective-permute-done((bf16[64,6144]{1,0:T(8,128)(2,1)S(1)}, bf16[64,6144]{1,0:T(8,128)(2,1)S(1)}, u32[]{:S(2)}, u32[]{:S(2)}) %collective-permute-start) | collective-permute-done | bytes 786464 | tf_op jit(solution)/shard_map/ppermute | solution.py:12
  412.0 0.9 copy.9
  (6 shorter events, 0.0 us)
Async XLA Ops:
  6.5 77.7 %all-gather.3.cloned.1.call-start = ((), (), s32[]{:S(2)}) async-start(), calls=%async_computation.2 | async-start | bytes 7077888 | tf_op jit(solution)/shard_map/all_gather | solution.py:30
  17.5 169.6 %reduce-scatter.3.cloned.1.call-start = ((), (), s32[]{:S(2)}) async-start(), calls=%async_computation.3 | async-start | bytes 9437184 | tf_op jit(solution)/shard_map/reduce_scatter | solution.py:34
  111.2 75.9 %copy-start.2 = (f32[1,3072]{1,0:T(1,128)S(1)}, f32[1,3072]{1,0:T(1,128)}, u32[]{:S(2)}) copy-start(f32[1,3072]{1,0:T(1,128)} %param.11) | copy-start | bytes 36868
  111.2 125.1 %all-gather.5.cloned.1.call-start = ((), (), s32[]{:S(2)}) async-start(), calls=%async_computation.4 | async-start | bytes 4718592 | tf_op jit(solution)/shard_map/all_gather | solution.py:37
  191.2 201.9 %reduce-scatter.5.cloned.1.call-start = ((), (), s32[]{:S(2)}) async-start(), calls=%async_computation.5 | async-start | bytes 14155776 | tf_op jit(solution)/shard_map/reduce_scatter | solution.py:39
  263.8 129.4 %copy-start = (bf16[1,64,6144]{2,1,0:T(8,128)(2,1)S(1)}, bf16[1,64,6144]{2,1,0:T(8,128)(2,1)}, u32[]{:S(2)}) copy-start(bf16[1,64,6144]{2,1,0:T(8,128)(2,1)} %param.7) | copy-start | bytes 2359300
  263.8 129.4 %copy-start.1 = (f32[1,6144]{1,0:T(1,128)S(1)}, f32[1,6144]{1,0:T(1,128)}, u32[]{:S(2)}) copy-start(f32[1,6144]{1,0:T(1,128)} %param.13) | copy-start | bytes 73732
  394.8 17.2 %collective-permute-start = (bf16[64,6144]{1,0:T(8,128)(2,1)S(1)}, bf16[64,6144]{1,0:T(8,128)(2,1)S(1)}, u32[]{:S(2)}, u32[]{:S(2)}) collective-permute-start(bf16[64,6144]{1,0:T(8,128)(2,1)S(1)} %fusion.20), channel_id=1, source_target_pairs={{16,0},{0,16},{17,1},{1,17},{18,2},{2,18},{19,3},{3,19},{20,4},{4,... | collective-permute-start | bytes 2359304 | tf_op jit(solution)/shard_map/ppermute | solution.py:12
Sparse Core Ops, SparseCore 0:
  17.7 66.5 all-gather.2
  111.3 75.6 reduce-scatter.2
  191.4 44.9 all-gather.4
  263.9 129.2 reduce-scatter.4
where the time goes:
time: 420 us; the launch traced here: 419 us
  waiting for transfers between devices  333 us (79%)
  matrix products  54.4 us (13%)
  between operations  13.1 us (3%)
  other arithmetic  10.8 us (3%)
  blocking collectives  5.84 us (1%)
    reduce_scatter x1, waiting for transfers between devices, per_device(): summed = lax.psum_scatter(terms, 'tensor', scatter_dimension=0, tiled=True)  129 us
    reduce_scatter x1, waiting for transfers between devices, per_device(): lax.psum_scatter(partial_value, 'dp', scatter_dimension=0, tiled=True)  75.8 us
    all_gather x1, waiting for transfers between devices, per_device(): lax.all_gather(normed, 'tensor', axis=0, tiled=True)  66.7 us
    all_gather x1, waiting for transfers between devices, per_device(): lax.all_gather(act, 'dp', axis=0, tiled=True)  45 us
    dot_general x1, matrix products, per_device(): jnp.dot(lax.all_gather(act, 'dp', axis=0, tiled=True), down_w, preferred_...  27.4 us
    dot_general x1, matrix products, per_device(): jnp.dot(lax.all_gather(normed, 'tensor', axis=0, tiled=True), up_w, prefe...  26.9 us
    ppermute x1, waiting for transfers between devices, from_behind(): return lax.ppermute(block, axis, route)  15.7 us
  transfers between devices with their start and end apart: 5, of which 5 were waited for; matrix products, arithmetic and copies ran while one was open for 0% of the time, Pallas kernels for 0%

commit v1 on v0

v1 whole, which is shorter than its diff:
```python
import jax
import jax.numpy as jnp
from jax import lax
from jax.sharding import PartitionSpec as P

F32 = jnp.float32
BF16 = jnp.bfloat16


def ring_order(n):
    return list(range(0, n, 2)) + list(range(1, n, 2))[::-1]


def make_per_device(width, n_section, n_dp, n_tensor):
    chips = n_tensor // 2
    order = ring_order(chips)
    along = [
        (order[i] * 2 + c, order[(i + 1) % chips] * 2 + c) for i in range(chips) for c in range(2)
    ]
    swap = [(i, i ^ 1) for i in range(n_tensor)]

    def forward(block):
        return lax.ppermute(block, "tensor", along)

    def sibling(block):
        return lax.ppermute(block, "tensor", swap)

    def across(partial_value):
        if n_dp == 1:
            return partial_value
        total = partial_value
        sent = partial_value.astype(BF16)
        for hop in range(1, n_dp):
            route = [(i, (i + hop) % n_dp) for i in range(n_dp)]
            total = total + lax.ppermute(sent, "dp", route).astype(F32)
        return total

    def per_device(incoming, norm_gain, norm_shift, up_weight, up_bias, down_weight, down_bias):
        x = incoming[0].astype(F32)
        up_w = up_weight[0]
        down_w = down_weight[0]
        rows = x.shape[0]
        total, square = lax.psum((jnp.sum(x, axis=1), jnp.sum(x * x, axis=1)), "dp")
        mean = total / width
        var = square / width - mean * mean
        normed = (
            (x - mean[:, None]) * lax.rsqrt(var + 1e-05)[:, None] * norm_gain[0] + norm_shift[0]
        ).astype(BF16)

        parts = []
        block = normed
        for step in range(chips):
            coming = forward(block) if step < chips - 1 else None
            both = jnp.concatenate([block, sibling(block)], axis=0)
            pre = across(jnp.dot(both, up_w, preferred_element_type=F32))
            act = jax.nn.gelu(pre + up_bias[0], approximate=True).astype(BF16)
            parts.append(jnp.dot(act, down_w, preferred_element_type=F32))
            block = coming

        running = None
        for step in list(range(1, chips)) + [0]:
            part = parts[step]
            summed = part[:rows] + sibling(part[rows:].astype(BF16)).astype(F32)
            if running is not None:
                summed = summed + running.astype(F32)
            if step:
                running = forward(summed.astype(BF16))
        result = (summed + down_bias[0] + x).astype(BF16)
        moved = lax.ppermute(
            result, "section", [(i, (i + 1) % n_section) for i in range(n_section)]
        )
        return moved[None]

    return per_device


def solution(mesh):
    placed = (
        P("section", "tensor", "dp"),
        P("section", "dp"),
        P("section", "dp"),
        P("section", "dp", "tensor"),
        P("section", "tensor"),
        P("section", "tensor", "dp"),
        P("section", "dp"),
    )

    def run(*args):
        width = args[0].shape[2]
        body = make_per_device(
            width, mesh.shape["section"], mesh.shape["dp"], mesh.shape["tensor"]
        )
        return jax.shard_map(
            body,
            mesh=mesh,
            in_specs=placed,
            out_specs=P("section", "tensor", "dp"),
            check_vma=False,
        )(*args)

    return run
```

time: 420 us -> 243 us (0.58)
  waiting for transfers between devices: 333 us -> 81.5 us
  matrix products: 54.4 us -> 122 us
  starting transfers between devices: 1.67 us -> 23.9 us
  between operations: 13.1 us -> 0.19 us
  other arithmetic: 10.8 us -> 6.49 us
    reduce_scatter x2 -> x0, waiting for transfers between devices: 205 us -> none  [the longest x1 129 us: per_device(): summed = lax.psum_scatter(terms, 'tensor', scatter_dimension=0, tiled=True)]
    all_gather x2 -> x0, waiting for transfers between devices: 112 us -> none  [the longest x1 66.7 us: per_device(): lax.all_gather(normed, 'tensor', axis=0, tiled=True)]
    dot_general x2 -> x8, matrix products: 54.4 us -> 122 us  [the longest x4 61.5 us: per_device(): pre = across(jnp.dot(both, up_w, preferred_element_type=F32))]
    ppermute x1 -> x19, waiting for transfers between devices: 15.7 us -> 81.5 us  [the longest x6 33.2 us: forward(): return lax.ppermute(block, 'tensor', along)]
    ppermute x1 -> x19, starting transfers between devices: 1.54 us -> 23.9 us  [the longest x6 14.5 us: forward(): return lax.ppermute(block, 'tensor', along)]
    convert_element_type x3 -> x5, other arithmetic: 8.1 us -> 3.67 us  [the longest x3 2.92 us: per_device(): running = forward(summed.astype(BF16))]
  transfers between devices with their start and end apart: 5 -> 19, of which waited for: 5 -> 6; matrix products, arithmetic and copies ran while one was open for 0% -> 52% of each run, Pallas kernels for 0% -> 0%
where the time goes in v1:
time: 243 us
  matrix products  122 us (50%)
  waiting for transfers between devices  81.5 us (34%)
  starting transfers between devices  23.9 us (10%)
  other arithmetic  6.49 us (3%)
  blocking collectives  5.85 us (2%)
  local copies, waits for them, and re-layouts  3 us (1%)
    dot_general x4, matrix products, per_device(): pre = across(jnp.dot(both, up_w, preferred_element_type=F32))  61.5 us
    dot_general x4, matrix products, per_device(): parts.append(jnp.dot(act, down_w, preferred_element_type=F32))  60.7 us
    ppermute x6, waiting for transfers between devices, forward(): return lax.ppermute(block, 'tensor', along)  33.2 us
    ppermute x4, waiting for transfers between devices, across(): total = total + lax.ppermute(sent, 'dp', route).astype(F32)  31.2 us
    ppermute x1, waiting for transfers between devices, per_device(): lax.ppermute(result, 'section', [(i, (i + 1) % n_section) for i in range(...  17.1 us
    ppermute x6, starting transfers between devices, forward(): return lax.ppermute(block, 'tensor', along)  14.5 us
    ppermute x4, starting transfers between devices, across(): total = total + lax.ppermute(sent, 'dp', route).astype(F32)  6.22 us
    psum x1, blocking collectives, per_device(): total, square = lax.psum((jnp.sum(x, axis=1), jnp.sum(x * x, axis=1)), 'dp')  5.85 us
  transfers between devices with their start and end apart: 19, of which 6 were waited for; matrix products, arithmetic and copies ran while one was open for 52% of the time, Pallas kernels for 0%

profile of v1, /device:TPU:0, one launch (start us, length us, event | category | flops | bytes accessed | tf_op | source)
XLA Modules:
  0.0 243.2 jit_solution(2728294454484391214)
XLA Ops:
  2.8 5.8 %all-reduce = (f32[64]{0:T(128)S(1)}, f32[64]{0:T(128)S(1)}) all-reduce(f32[64]{0:T(128)S(1)} %fusion.23, f32[64]{0:T(128)S(1)} %convert_reduce_fusion), channel_id=1, replica_groups=mesh['section'=2,'dp'=2,'tensor'=8] {'dp'}, use_global_device_ids=true, to_apply=%region_3.0 | all-reduce | flops 128 | bytes 1024 | tf_op jit(solution)/shard_map/psum | solution.py:43
  9.0 3.2 %collective-permute-start.3 = (bf16[64,6144]{1,0:T(8,128)(2,1)S(1)}, bf16[64,6144]{1,0:T(8,128)(2,1)S(1)}, u32[]{:S(2)}, u32[]{:S(2)}) collective-permute-start(bf16[64,6144]{1,0:T(8,128)(2,1)S(1)} %fusion.22), channel_id=1, source_target_pairs={{0,4},{1,5},{4,6},{5,7},{6,2},{7,3},{2,0},{3,1},{8,12},{9,13},{12,... | collective-permute-start | bytes 2359304 | tf_op jit(solution)/shard_map/ppermute | solution.py:23
  12.2 15.7 %collective-permute-done.3 = bf16[64,6144]{1,0:T(8,128)(2,1)S(1)} collective-permute-done((bf16[64,6144]{1,0:T(8,128)(2,1)S(1)}, bf16[64,6144]{1,0:T(8,128)(2,1)S(1)}, u32[]{:S(2)}, u32[]{:S(2)}) %collective-permute-start.3) | collective-permute-done | bytes 786464 | tf_op jit(solution)/shard_map/ppermute | solution.py:23
  28.4 3.4 %collective-permute-start.4 = (bf16[64,6144]{1,0:T(8,128)(2,1)S(1)}, bf16[64,6144]{1,0:T(8,128)(2,1)}, u32[]{:S(2)}, u32[]{:S(2)}) collective-permute-start(bf16[64,6144]{1,0:T(8,128)(2,1)S(1)} %collective-permute-done.3), channel_id=1, source_target_pairs={{0,4},{1,5},{4,6},{5,7},{6,2},{7,3},{2,0},{3,1},{8,12},{9,13},{12,... | collective-permute-start | bytes 2359304 | tf_op jit(solution)/shard_map/ppermute | solution.py:23
  31.8 14.4 %fusion.123 = (bf16[128,3072]{1,0:T(8,128)(2,1)S(1)}, f32[128,3072]{1,0:T(8,128)S(1)}) fusion(bf16[1,6144,3072]{2,1,0:T(8,128)(2,1)} %param.10, bf16[64,6144]{1,0:T(8,128)(2,1)S(1)} %collective-permute-done.12, bf16[64,6144]{1,0:T(8,128)(2,1)S(1)} %collective-permute-done.3), kind=kOutput, calls=%fused_computation.135 | convolution fusion | flops 4835377152 | bytes 41680896 | tf_op jit(solution)/shard_map/dot_general | solution.py:55
  47.7 15.3 %fusion.120 = (bf16[128,3072]{1,0:T(8,128)(2,1)}, f32[128,3072]{1,0:T(8,128)}) fusion(bf16[1,6144,3072]{2,1,0:T(8,128)(2,1)} %param.10, bf16[64,6144]{1,0:T(8,128)(2,1)S(1)} %collective-permute-done, bf16[64,6144]{1,0:T(8,128)(2,1)S(1)} %fusion.22), kind=kOutput, calls=%fused_computation.132 | convolution fusion | flops 4835377152 | bytes 41680896 | tf_op jit(solution)/shard_map/dot_general | solution.py:55
  63.6 1.8 collective-permute-start.5
  66.4 15.0 %fusion = f32[128,6144]{1,0:T(8,128)S(1)} fusion(bf16[1,3072,6144]{2,1,0:T(8,128)(2,1)} %param.12, f32[128,3072]{1,0:T(8,128)S(1)} %get-tuple-element.16, bf16[128,3072]{1,0:T(8,128)(2,1)} %copy-done.2, f32[3072]{0:T(1024)S(1)} %bitcast.51), kind=kOutput, calls=%fused_computation | convolution fusion | flops 4836556800 | bytes 43266048 | tf_op jit(solution)/shard_map/dot_general | solution.py:57
  81.7 15.7 %fusion.122 = (bf16[128,3072]{1,0:T(8,128)(2,1)}, f32[128,3072]{1,0:T(8,128)S(1)}) fusion(bf16[1,6144,3072]{2,1,0:T(8,128)(2,1)} %param.10, bf16[64,6144]{1,0:T(8,128)(2,1)} %collective-permute-done.9, bf16[64,6144]{1,0:T(8,128)(2,1)} %collective-permute-done.4), kind=kOutput, calls=%fused_computation.134 | convolution fusion | flops 4835377152 | bytes 41680896 | tf_op jit(solution)/shard_map/dot_general | solution.py:55
  97.4 2.4 collective-permute-start.10
  100.1 2.2 collective-permute-start.15
  102.3 15.8 %collective-permute-done.10 = bf16[128,3072]{1,0:T(8,128)(2,1)S(1)} collective-permute-done((bf16[128,3072]{1,0:T(8,128)(2,1)}, bf16[128,3072]{1,0:T(8,128)(2,1)S(1)}, u32[]{:S(2)}, u32[]{:S(2)}) %collective-permute-start.10) | collective-permute-done | bytes 786464 | tf_op jit(solution)/shard_map/ppermute | solution.py:35
  119.0 15.0 %fusion.2 = f32[128,6144]{1,0:T(8,128)S(1)} fusion(bf16[1,3072,6144]{2,1,0:T(8,128)(2,1)} %param.12, f32[128,3072]{1,0:T(8,128)S(1)} %get-tuple-element.14, bf16[128,3072]{1,0:T(8,128)(2,1)} %copy-done.3, f32[3072]{0:T(1024)S(1)} %bitcast.52), kind=kOutput, calls=%fused_computation.2 | convolution fusion | flops 4836556800 | bytes 43266048 | tf_op jit(solution)/shard_map/dot_general | solution.py:57
  134.2 16.1 %fusion.121 = (bf16[128,3072]{1,0:T(8,128)(2,1)}, f32[128,3072]{1,0:T(8,128)}) fusion(bf16[1,6144,3072]{2,1,0:T(8,128)(2,1)} %param.10, bf16[64,6144]{1,0:T(8,128)(2,1)} %collective-permute-done.6, bf16[64,6144]{1,0:T(8,128)(2,1)S(1)} %collective-permute-done.5), kind=kOutput, calls=%fused_computation.133 | convolution fusion | flops 4835377152 | bytes 41680896 | tf_op jit(solution)/shard_map/dot_general | solution.py:55
  150.3 1.7 collective-permute-start.7
  153.2 2.0 collective-permute-start.16
  155.2 15.3 %collective-permute-done.7 = bf16[128,3072]{1,0:T(8,128)(2,1)S(1)} collective-permute-done((bf16[128,3072]{1,0:T(8,128)(2,1)}, bf16[128,3072]{1,0:T(8,128)(2,1)S(1)}, u32[]{:S(2)}, u32[]{:S(2)}) %collective-permute-start.7) | collective-permute-done | bytes 786464 | tf_op jit(solution)/shard_map/ppermute | solution.py:35
  170.4 15.3 %fusion.4 = f32[128,6144]{1,0:T(8,128)S(1)} fusion(bf16[1,3072,6144]{2,1,0:T(8,128)(2,1)} %param.12, f32[128,3072]{1,0:T(8,128)} %get-tuple-element.12, bf16[128,3072]{1,0:T(8,128)(2,1)S(1)} %collective-permute-done.7, f32[3072]{0:T(1024)S(1)} %bitcast.53), kind=kOutput, calls=%fused_computation.4 | convolution fusion | flops 4836556800 | bytes 43266048 | tf_op jit(solution)/shard_map/dot_general | solution.py:57
  185.9 15.4 %fusion.6 = f32[128,6144]{1,0:T(8,128)S(1)} fusion(bf16[1,3072,6144]{2,1,0:T(8,128)(2,1)} %param.12, f32[128,3072]{1,0:T(8,128)} %get-tuple-element.10, bf16[128,3072]{1,0:T(8,128)(2,1)} %collective-permute-done.1, f32[3072]{0:T(1024)S(1)} %bitcast.54), kind=kOutput, calls=%fused_computation.6 | convolution fusion | flops 4836556800 | bytes 43266048 | tf_op jit(solution)/shard_map/dot_general | solution.py:57
  202.0 1.7 fusion.61
  203.7 2.0 collective-permute-start.17
  205.7 17.5 %collective-permute-done.17 = bf16[64,6144]{1,0:T(8,128)(2,1)S(1)} collective-permute-done((bf16[64,6144]{1,0:T(8,128)(2,1)S(1)}, bf16[64,6144]{1,0:T(8,128)(2,1)S(1)}, u32[]{:S(2)}, u32[]{:S(2)}) %collective-permute-start.17) | collective-permute-done | bytes 786464 | tf_op jit(solution)/shard_map/ppermute | solution.py:23
  223.6 1.6 collective-permute-start.18
  225.2 17.1 %collective-permute-done.18 = bf16[64,6144]{1,0:T(8,128)(2,1)S(1)} collective-permute-done((bf16[64,6144]{1,0:T(8,128)(2,1)S(1)}, bf16[64,6144]{1,0:T(8,128)(2,1)S(1)}, u32[]{:S(2)}, u32[]{:S(2)}) %collective-permute-start.18) | collective-permute-done | bytes 786464 | tf_op jit(solution)/shard_map/ppermute | solution.py:69
  (50 shorter events, 11.6 us)
Async XLA Ops:
  0.0 8.7 %copy-start = (bf16[1,64,6144]{2,1,0:T(8,128)(2,1)S(1)}, bf16[1,64,6144]{2,1,0:T(8,128)(2,1)}, u32[]{:S(2)}) copy-start(bf16[1,64,6144]{2,1,0:T(8,128)(2,1)} %param.7) | copy-start | bytes 2359300
  0.0 8.7 %copy-start.6 = (f32[1,6144]{1,0:T(1,128)S(1)}, f32[1,6144]{1,0:T(1,128)}, u32[]{:S(2)}) copy-start(f32[1,6144]{1,0:T(1,128)} %param.8) | copy-start | bytes 73732
  0.0 8.7 %copy-start.5 = (f32[1,6144]{1,0:T(1,128)S(1)}, f32[1,6144]{1,0:T(1,128)}, u32[]{:S(2)}) copy-start(f32[1,6144]{1,0:T(1,128)} %param.9) | copy-start | bytes 73732
  9.0 18.8 %collective-permute-start.3 = (bf16[64,6144]{1,0:T(8,128)(2,1)S(1)}, bf16[64,6144]{1,0:T(8,128)(2,1)S(1)}, u32[]{:S(2)}, u32[]{:S(2)}) collective-permute-start(bf16[64,6144]{1,0:T(8,128)(2,1)S(1)} %fusion.22), channel_id=1, source_target_pairs={{0,4},{1,5},{4,6},{5,7},{6,2},{7,3},{2,0},{3,1},{8,12},{9,13},{12,... | collective-permute-start | bytes 2359304 | tf_op jit(solution)/shard_map/ppermute | solution.py:23
  27.9 3.9 %collective-permute-start.12 = (bf16[64,6144]{1,0:T(8,128)(2,1)S(1)}, bf16[64,6144]{1,0:T(8,128)(2,1)S(1)}, u32[]{:S(2)}, u32[]{:S(2)}) collective-permute-start(bf16[64,6144]{1,0:T(8,128)(2,1)S(1)} %collective-permute-done.3), channel_id=1, source_target_pairs={{0,1},{1,0},{2,3},{3,2},{4,5},{5,4},{6,7},{7,6},{8,9},{9,8},{10,11... | collective-permute-start | bytes 2359304 | tf_op jit(solution)/shard_map/ppermute | solution.py:26
  27.9 19.8 %collective-permute-start = (bf16[64,6144]{1,0:T(8,128)(2,1)S(1)}, bf16[64,6144]{1,0:T(8,128)(2,1)S(1)}, u32[]{:S(2)}, u32[]{:S(2)}) collective-permute-start(bf16[64,6144]{1,0:T(8,128)(2,1)S(1)} %fusion.22), channel_id=1, source_target_pairs={{0,1},{1,0},{2,3},{3,2},{4,5},{5,4},{6,7},{7,6},{8,9},{9,8},{10,11... | collective-permute-start | bytes 2359304 | tf_op jit(solution)/shard_map/ppermute | solution.py:26
  28.4 35.2 %collective-permute-start.4 = (bf16[64,6144]{1,0:T(8,128)(2,1)S(1)}, bf16[64,6144]{1,0:T(8,128)(2,1)}, u32[]{:S(2)}, u32[]{:S(2)}) collective-permute-start(bf16[64,6144]{1,0:T(8,128)(2,1)S(1)} %collective-permute-done.3), channel_id=1, source_target_pairs={{0,4},{1,5},{4,6},{5,7},{6,2},{7,3},{2,0},{3,1},{8,12},{9,13},{12,... | collective-permute-start | bytes 2359304 | tf_op jit(solution)/shard_map/ppermute | solution.py:23
  46.2 20.2 %copy-start.1 = (f32[1,3072]{1,0:T(1,128)S(1)}, f32[1,3072]{1,0:T(1,128)}, u32[]{:S(2)}) copy-start(f32[1,3072]{1,0:T(1,128)} %param.11) | copy-start | bytes 36868
  46.2 19.3 %collective-permute-start.13 = (bf16[128,3072]{1,0:T(8,128)(2,1)S(1)}, bf16[128,3072]{1,0:T(8,128)(2,1)S(1)}, u32[]{:S(2)}, u32[]{:S(2)}) collective-permute-start(bf16[128,3072]{1,0:T(8,128)(2,1)S(1)} %get-tuple-element.15), channel_id=1, source_target_pairs={{0,8},{8,0},{1,9},{9,1},{2,10},{10,2},{3,11},{11,3},{4,12},{12,4},... | collective-permute-start | bytes 2359304 | tf_op jit(solution)/shard_map/ppermute | solution.py:35
  63.0 122.8 %collective-permute-start.1 = (bf16[128,3072]{1,0:T(8,128)(2,1)}, bf16[128,3072]{1,0:T(8,128)(2,1)}, u32[]{:S(2)}, u32[]{:S(2)}) collective-permute-start(bf16[128,3072]{1,0:T(8,128)(2,1)} %get-tuple-element.9), channel_id=1, source_target_pairs={{0,8},{8,0},{1,9},{9,1},{2,10},{10,2},{3,11},{11,3},{4,12},{12,4},... | collective-permute-start | bytes 2359304 | tf_op jit(solution)/shard_map/ppermute | solution.py:35
  63.6 18.1 %collective-permute-start.9 = (bf16[64,6144]{1,0:T(8,128)(2,1)}, bf16[64,6144]{1,0:T(8,128)(2,1)}, u32[]{:S(2)}, u32[]{:S(2)}) collective-permute-start(bf16[64,6144]{1,0:T(8,128)(2,1)} %collective-permute-done.4), channel_id=1, source_target_pairs={{0,1},{1,0},{2,3},{3,2},{4,5},{5,4},{6,7},{7,6},{8,9},{9,8},{10,11... | collective-permute-start | bytes 2359304 | tf_op jit(solution)/shard_map/ppermute | solution.py:26
  63.6 36.2 %collective-permute-start.5 = (bf16[64,6144]{1,0:T(8,128)(2,1)}, bf16[64,6144]{1,0:T(8,128)(2,1)S(1)}, u32[]{:S(2)}, u32[]{:S(2)}) collective-permute-start(bf16[64,6144]{1,0:T(8,128)(2,1)} %collective-permute-done.4), channel_id=1, source_target_pairs={{0,4},{1,5},{4,6},{5,7},{6,2},{7,3},{2,0},{3,1},{8,12},{9,13},{12,... | collective-permute-start | bytes 2359304 | tf_op jit(solution)/shard_map/ppermute | solution.py:23
  81.5 18.5 %collective-permute-start.14 = (bf16[64,6144]{1,0:T(8,128)(2,1)S(1)}, bf16[64,6144]{1,0:T(8,128)(2,1)S(1)}, u32[]{:S(2)}, u32[]{:S(2)}) collective-permute-start(bf16[64,6144]{1,0:T(8,128)(2,1)S(1)} %slice.68), channel_id=1, source_target_pairs={{0,1},{1,0},{2,3},{3,2},{4,5},{5,4},{6,7},{7,6},{8,9},{9,8},{10,11... | collective-permute-start | bytes 2359304 | tf_op jit(solution)/shard_map/ppermute | solution.py:26
  97.4 20.8 %collective-permute-start.10 = (bf16[128,3072]{1,0:T(8,128)(2,1)}, bf16[128,3072]{1,0:T(8,128)(2,1)S(1)}, u32[]{:S(2)}, u32[]{:S(2)}) collective-permute-start(bf16[128,3072]{1,0:T(8,128)(2,1)} %get-tuple-element.13), channel_id=1, source_target_pairs={{0,8},{8,0},{1,9},{9,1},{2,10},{10,2},{3,11},{11,3},{4,12},{12,4},... | collective-permute-start | bytes 2359304 | tf_op jit(solution)/shard_map/ppermute | solution.py:35
  99.8 34.5 %collective-permute-start.6 = (bf16[64,6144]{1,0:T(8,128)(2,1)S(1)}, bf16[64,6144]{1,0:T(8,128)(2,1)}, u32[]{:S(2)}, u32[]{:S(2)}) collective-permute-start(bf16[64,6144]{1,0:T(8,128)(2,1)S(1)} %collective-permute-done.5), channel_id=1, source_target_pairs={{0,1},{1,0},{2,3},{3,2},{4,5},{5,4},{6,7},{7,6},{8,9},{9,8},{10,11... | collective-permute-start | bytes 2359304 | tf_op jit(solution)/shard_map/ppermute | solution.py:26
  100.1 52.0 %collective-permute-start.15 = (bf16[64,6144]{1,0:T(8,128)(2,1)S(1)}, bf16[64,6144]{1,0:T(8,128)(2,1)S(1)}, u32[]{:S(2)}, u32[]{:S(2)}) collective-permute-start(bf16[64,6144]{1,0:T(8,128)(2,1)S(1)} %fusion.57), channel_id=1, source_target_pairs={{0,4},{1,5},{4,6},{5,7},{6,2},{7,3},{2,0},{3,1},{8,12},{9,13},{12,... | collective-permute-start | bytes 2359304 | tf_op jit(solution)/shard_map/ppermute | solution.py:23
  134.1 17.9 %collective-permute-start.11 = (bf16[64,6144]{1,0:T(8,128)(2,1)S(1)}, bf16[64,6144]{1,0:T(8,128)(2,1)S(1)}, u32[]{:S(2)}, u32[]{:S(2)}) collective-permute-start(bf16[64,6144]{1,0:T(8,128)(2,1)S(1)} %slice.69), channel_id=1, source_target_pairs={{0,1},{1,0},{2,3},{3,2},{4,5},{5,4},{6,7},{7,6},{8,9},{9,8},{10,11... | collective-permute-start | bytes 2359304 | tf_op jit(solution)/shard_map/ppermute | solution.py:26
  150.3 20.1 %collective-permute-start.7 = (bf16[128,3072]{1,0:T(8,128)(2,1)}, bf16[128,3072]{1,0:T(8,128)(2,1)S(1)}, u32[]{:S(2)}, u32[]{:S(2)}) collective-permute-start(bf16[128,3072]{1,0:T(8,128)(2,1)} %get-tuple-element.11), channel_id=1, source_target_pairs={{0,8},{8,0},{1,9},{9,1},{2,10},{10,2},{3,11},{11,3},{4,12},{12,4},... | collective-permute-start | bytes 2359304 | tf_op jit(solution)/shard_map/ppermute | solution.py:35
  153.2 48.8 %collective-permute-start.16 = (bf16[64,6144]{1,0:T(8,128)(2,1)}, bf16[64,6144]{1,0:T(8,128)(2,1)}, u32[]{:S(2)}, u32[]{:S(2)}) collective-permute-start(bf16[64,6144]{1,0:T(8,128)(2,1)} %fusion.59), channel_id=1, source_target_pairs={{0,4},{1,5},{4,6},{5,7},{6,2},{7,3},{2,0},{3,1},{8,12},{9,13},{12,... | collective-permute-start | bytes 2359304 | tf_op jit(solution)/shard_map/ppermute | solution.py:23
  185.8 16.2 %collective-permute-start.8 = (bf16[64,6144]{1,0:T(8,128)(2,1)S(1)}, bf16[64,6144]{1,0:T(8,128)(2,1)}, u32[]{:S(2)}, u32[]{:S(2)}) collective-permute-start(bf16[64,6144]{1,0:T(8,128)(2,1)S(1)} %slice.70), channel_id=1, source_target_pairs={{0,1},{1,0},{2,3},{3,2},{4,5},{5,4},{6,7},{7,6},{8,9},{9,8},{10,11... | collective-permute-start | bytes 2359304 | tf_op jit(solution)/shard_map/ppermute | solution.py:26
  201.4 21.8 %copy-start.4 = (f32[1,6144]{1,0:T(1,128)S(1)}, f32[1,6144]{1,0:T(1,128)}, u32[]{:S(2)}) copy-start(f32[1,6144]{1,0:T(1,128)} %param.13) | copy-start | bytes 73732
  201.4 4.2 %collective-permute-start.2 = (bf16[64,6144]{1,0:T(8,128)(2,1)S(1)}, bf16[64,6144]{1,0:T(8,128)(2,1)S(1)}, u32[]{:S(2)}, u32[]{:S(2)}) collective-permute-start(bf16[64,6144]{1,0:T(8,128)(2,1)S(1)} %slice.71), channel_id=1, source_target_pairs={{0,1},{1,0},{2,3},{3,2},{4,5},{5,4},{6,7},{7,6},{8,9},{9,8},{10,11... | collective-permute-start | bytes 2359304 | tf_op jit(solution)/shard_map/ppermute | solution.py:26
  203.7 19.5 %collective-permute-start.17 = (bf16[64,6144]{1,0:T(8,128)(2,1)S(1)}, bf16[64,6144]{1,0:T(8,128)(2,1)S(1)}, u32[]{:S(2)}, u32[]{:S(2)}) collective-permute-start(bf16[64,6144]{1,0:T(8,128)(2,1)S(1)} %fusion.61), channel_id=1, source_target_pairs={{0,4},{1,5},{4,6},{5,7},{6,2},{7,3},{2,0},{3,1},{8,12},{9,13},{12,... | collective-permute-start | bytes 2359304 | tf_op jit(solution)/shard_map/ppermute | solution.py:23
  223.6 18.7 %collective-permute-start.18 = (bf16[64,6144]{1,0:T(8,128)(2,1)S(1)}, bf16[64,6144]{1,0:T(8,128)(2,1)S(1)}, u32[]{:S(2)}, u32[]{:S(2)}) collective-permute-start(bf16[64,6144]{1,0:T(8,128)(2,1)S(1)} %fusion.24), channel_id=1, source_target_pairs={{0,16},{16,0},{1,17},{17,1},{2,18},{18,2},{3,19},{19,3},{4,20},{20... | collective-permute-start | bytes 2359304 | tf_op jit(solution)/shard_map/ppermute | solution.py:69
  (2 other events, 1.8 us)

commit v2 on v1

v2 whole, which is shorter than its diff:
```python
import functools

import jax
import jax.numpy as jnp
from jax import lax
from jax.experimental import pallas as pl
from jax.experimental.pallas import tpu as pltpu
from jax.sharding import PartitionSpec as P

F32 = jnp.float32
BF16 = jnp.bfloat16
MIB = 1024 * 1024
LONG = pl.CostEstimate(flops=20_000_000_000, bytes_accessed=80_000_000, transcendentals=0)


def ring_order(n):
    return list(range(0, n, 2)) + list(range(1, n, 2))[::-1]


def pick_tile(extent, most):
    tile = min(extent, most)
    while extent % tile:
        tile //= 2
    return tile


def sums_kernel(x_ref, out_ref):
    x = x_ref[0].astype(F32)
    total = jnp.sum(x, axis=1, keepdims=True)
    square = jnp.sum(x * x, axis=1, keepdims=True)
    lane = lax.broadcasted_iota(jnp.int32, out_ref.shape, 1)
    out_ref[...] = jnp.where(lane == 0, total, square)


def row_sums(incoming):
    rows = incoming.shape[1]
    return pl.pallas_call(
        sums_kernel,
        out_shape=jax.ShapeDtypeStruct((rows, 128), F32),
        compiler_params=pltpu.CompilerParams(vmem_limit_bytes=16 * MIB),
    )(incoming)


def up_kernel(width, n_dp, n_tensor, at_ref, a_ref, b_ref, sums_ref, gain_ref, shift_ref, w_ref, *rest):
    wide_ref, sent_ref, normed_ref = rest[-3:]
    rows = a_ref.shape[0]

    @pl.when(pl.program_id(0) == 0)
    def _():
        for half, block_ref in enumerate((a_ref, b_ref)):
            sums = jnp.zeros((rows, 128), F32)
            for k in range(n_dp):
                start = pl.multiple_of((at_ref[half] + k * n_tensor) * rows, rows)
                sums = sums + sums_ref[pl.ds(start, rows), :]
            mean = sums[:, 0:1] / width
            var = sums[:, 1:2] / width - mean * mean
            scale = lax.rsqrt(var + 1e-05)
            x = block_ref[...].astype(F32)
            normed_ref[half * rows : (half + 1) * rows, :] = (
                (x - mean) * scale * gain_ref[...] + shift_ref[...]
            ).astype(BF16)

    product = jnp.dot(normed_ref[...], w_ref[0], preferred_element_type=F32)
    wide_ref[...] = product
    sent_ref[...] = product.astype(BF16)


def up_product(width, n_dp, n_tensor, at, a, b, sums, gain, shift, weight, after):
    rows, depth = a.shape
    columns = weight.shape[2]
    tile = pick_tile(columns, 256)
    whole = lambda shape: pl.BlockSpec(shape, lambda j, at: (0,) * len(shape))
    out = pl.BlockSpec((2 * rows, tile), lambda j, at: (0, j))
    return pl.pallas_call(
        functools.partial(up_kernel, width, n_dp, n_tensor),
        out_shape=(
            jax.ShapeDtypeStruct((2 * rows, columns), F32),
            jax.ShapeDtypeStruct((2 * rows, columns), BF16),
        ),
        grid_spec=pltpu.PrefetchScalarGridSpec(
            num_scalar_prefetch=1,
            grid=(columns // tile,),
            in_specs=[
                whole(a.shape),
                whole(b.shape),
                whole(sums.shape),
                whole(gain.shape),
                whole(shift.shape),
                pl.BlockSpec((1, depth, tile), lambda j, at: (0, 0, j)),
            ]
            + [pl.BlockSpec(memory_space=pl.ANY)] * len(after),
            out_specs=[out, out],
            scratch_shapes=[pltpu.VMEM((2 * rows, depth), BF16)],
        ),
        compiler_params=pltpu.CompilerParams(vmem_limit_bytes=28 * MIB),
        cost_estimate=LONG,
    )(at, a, b, sums, gain, shift, weight, *after)


def down_kernel(own_ref, other_ref, bias_ref, w_ref, *rest):
    mine_ref, theirs_ref, total_ref = rest[-3:]
    rows = mine_ref.shape[0]
    step = pl.program_id(0)
    pre = own_ref[...] + other_ref[...].astype(F32) + bias_ref[...]
    act = jax.nn.gelu(pre, approximate=True).astype(BF16)
    product = jnp.dot(act, w_ref[0], preferred_element_type=F32)

    @pl.when(step == 0)
    def _():
        total_ref[...] = product

    @pl.when(step > 0)
    def _():
        total_ref[...] += product

    @pl.when(step == pl.num_programs(0) - 1)
    def _():
        mine_ref[...] = total_ref[:rows, :]
        theirs_ref[...] = total_ref[rows:, :].astype(BF16)


def down_product(own, other, bias, weight, after):
    rows = own.shape[0] // 2
    depth, columns = weight.shape[1:]
    tile = pick_tile(depth, 256)
    return pl.pallas_call(
        down_kernel,
        out_shape=(
            jax.ShapeDtypeStruct((rows, columns), F32),
            jax.ShapeDtypeStruct((rows, columns), BF16),
        ),
        grid=(depth // tile,),
        in_specs=[
            pl.BlockSpec((2 * rows, tile), lambda k: (0, k)),
            pl.BlockSpec((2 * rows, tile), lambda k: (0, k)),
            pl.BlockSpec((1, tile), lambda k: (0, k)),
            pl.BlockSpec((1, tile, columns), lambda k: (0, k, 0)),
        ]
        + [pl.BlockSpec(memory_space=pl.ANY)] * len(after),
        out_specs=[pl.BlockSpec((rows, columns), lambda k: (0, 0))] * 2,
        scratch_shapes=[pltpu.VMEM((2 * rows, columns), F32)],
        compiler_params=pltpu.CompilerParams(vmem_limit_bytes=28 * MIB),
        cost_estimate=LONG,
    )(own, other, bias, weight, *after)


def make_per_device(width, n_section, n_dp, n_tensor):
    chips = n_tensor // 2
    order = ring_order(chips)
    along = [
        (order[i] * 2 + c, order[(i + 1) % chips] * 2 + c) for i in range(chips) for c in range(2)
    ]
    swap = [(i, i ^ 1) for i in range(n_tensor)]
    source = [
        [
            [order[(order.index(t // 2) - k) % chips] * 2 + (t % 2 ^ half) for half in range(2)]
            for t in range(n_tensor)
        ]
        for k in range(chips)
    ]

    def forward(block):
        return lax.ppermute(block, "tensor", along)

    def sibling(block):
        return lax.ppermute(block, "tensor", swap)

    def from_others(sent):
        total = None
        for hop in range(1, n_dp):
            route = [(i, (i + hop) % n_dp) for i in range(n_dp)]
            got = lax.ppermute(sent, "dp", route)
            total = got if total is None else total.astype(F32) + got.astype(F32)
        return total

    def per_device(incoming, norm_gain, norm_shift, up_weight, up_bias, down_weight, down_bias):
        rows = incoming.shape[1]
        raw = incoming[0]
        me = lax.axis_index("tensor")
        at = jnp.asarray(source, jnp.int32)[:, me]
        sums = lax.all_gather(row_sums(incoming), ("dp", "tensor"), axis=0, tiled=True)

        blocks, siblings = [raw], [sibling(raw)]

        pres, parts = {}, {}
        last = ()

        def up(k):
            nonlocal last
            coming = forward(blocks[k]) if k < chips - 1 else None
            wide, sent = up_product(
                width, n_dp, n_tensor, at[k], blocks[k], siblings[k], sums,
                norm_gain, norm_shift, up_weight, last,
            )
            if coming is not None:
                coming, wide = lax.optimization_barrier((coming, wide))
                blocks.append(coming)
                siblings.append(sibling(coming))
            pres[k] = (wide, from_others(sent))
            last = (wide,)

        def down(k):
            nonlocal last
            mine, theirs = down_product(*pres[k], up_bias, down_weight, last)
            last = (mine,)
            if k == 1:
                first = (mine + sibling(theirs).astype(F32)).astype(BF16)
                running.append(forward(first))
                last = (first,)
            else:
                parts[k] = (mine, sibling(theirs))

        running = []
        up(0)
        if chips > 1:
            up(1)
        for k in range(2, chips):
            up(k)
            down(k - 1)
        if chips > 1:
            down(chips - 1)
        down(0)

        for k in list(range(2, chips)) + [0]:
            mine, got = parts[k]
            summed = mine + got.astype(F32)
            if running:
                summed = summed + running[-1].astype(F32)
            if k:
                running.append(forward(summed.astype(BF16)))
        result = (summed + down_bias[0] + raw.astype(F32)).astype(BF16)
        moved = lax.ppermute(
            result, "section", [(i, (i + 1) % n_section) for i in range(n_section)]
        )
        return moved[None]

    return per_device


def solution(mesh):
    placed = (
        P("section", "tensor", "dp"),
        P("section", "dp"),
        P("section", "dp"),
        P("section", "dp", "tensor"),
        P("section", "tensor"),
        P("section", "tensor", "dp"),
        P("section", "dp"),
    )

    def run(*args):
        body = make_per_device(
            args[0].shape[2], mesh.shape["section"], mesh.shape["dp"], mesh.shape["tensor"]
        )
        return jax.shard_map(
            body,
            mesh=mesh,
            in_specs=placed,
            out_specs=P("section", "tensor", "dp"),
            check_vma=False,
        )(*args)

    return run
```

time: 243 us -> 260 us (1.070)
  Pallas kernels: 0 us -> 149 us
  matrix products: 122 us -> 0 us
  waiting for transfers between devices: 81.5 us -> 52.8 us
  blocking collectives: 5.85 us -> 33.7 us
  starting transfers between devices: 23.9 us -> 15.2 us
  other arithmetic: 6.49 us -> 1.12 us
    pallas_call x0 -> x9, Pallas kernels: none -> 149 us  [the longest x4 76 us: down_product(): pl.pallas_call(down_kernel, out_shape=(jax.ShapeDtypeStruct((rows, column...]
    dot_general x8 -> x0, matrix products: 122 us -> none  [the longest x4 61.5 us: per_device(): pre = across(jnp.dot(both, up_w, preferred_element_type=F32))]
    all_gather x0 -> x1, blocking collectives: none -> 33.7 us  [per_device(): lax.all_gather(row_sums(incoming), ('dp', 'tensor'), axis=0, tiled=True)]
    ppermute x4, waiting for transfers between devices: 31.2 us -> 14.1 us  [from_others(): got = lax.ppermute(sent, 'dp', route)]
    ppermute x6, waiting for transfers between devices: 33.2 us -> 18 us  [forward(): return lax.ppermute(block, 'tensor', along)]
    ppermute x6, starting transfers between devices: 14.5 us -> 6.64 us  [forward(): return lax.ppermute(block, 'tensor', along)]
    psum x1 -> x0, blocking collectives: 5.85 us -> none  [per_device(): total, square = lax.psum((jnp.sum(x, axis=1), jnp.sum(x * x, axis=1)), 'dp')]
    ppermute x8, waiting for transfers between devices: 0.02 us -> 3.29 us  [sibling(): return lax.ppermute(block, 'tensor', swap)]
  transfers between devices with their start and end apart: 19 -> 19, of which waited for: 6 -> 7; matrix products, arithmetic and copies ran while one was open for 52% -> 1% of each run, Pallas kernels for 0% -> 51%
where the time goes in v2:
time: 260 us; the launch traced here: 258 us
  Pallas kernels  149 us (57%)
  waiting for transfers between devices  52.8 us (20%)
  blocking collectives  33.7 us (13%)
  starting transfers between devices  15.2 us (6%)
  local copies, waits for them, and re-layouts  5.42 us (2%)
    pallas_call x4, Pallas kernels, down_product(): pl.pallas_call(down_kernel, out_shape=(jax.ShapeDtypeStruct((rows, column...  76 us
    pallas_call x4, Pallas kernels, up_product(): pl.pallas_call(functools.partial(up_kernel, width, n_dp, n_tensor), out_s...  73.1 us
    all_gather x1, blocking collectives, per_device(): lax.all_gather(row_sums(incoming), ('dp', 'tensor'), axis=0, tiled=True)  33.7 us
    ppermute x6, waiting for transfers between devices, forward(): return lax.ppermute(block, 'tensor', along)  18 us
    ppermute x1, waiting for transfers between devices, per_device(): lax.ppermute(result, 'section', [(i, (i + 1) % n_section) for i in range(...  17.3 us
    ppermute x4, waiting for transfers between devices, from_others(): got = lax.ppermute(sent, 'dp', route)  14.1 us
    ppermute x6, starting transfers between devices, forward(): return lax.ppermute(block, 'tensor', along)  6.64 us
  transfers between devices with their start and end apart: 19, of which 7 were waited for; matrix products, arithmetic and copies ran while one was open for 1% of the time, Pallas kernels for 51%

profile of v2, /device:TPU:0, one launch (start us, length us, event | category | flops | bytes accessed | tf_op | source)
XLA Modules:
  0.0 257.9 jit_solution(18282900026286158999)
XLA Ops:
  0.5 3.6 %collective-permute-start = (bf16[64,6144]{1,0:T(8,128)(2,1)}, bf16[64,6144]{1,0:T(8,128)(2,1)S(1)}, u32[]{:S(2)}, u32[]{:S(2)}) collective-permute-start(bf16[64,6144]{1,0:T(8,128)(2,1)} %bitcast.13), channel_id=1, source_target_pairs={{0,4},{1,5},{4,6},{5,7},{6,2},{7,3},{2,0},{3,1},{8,12},{9,13},{12,... | collective-permute-start | bytes 2359304 | tf_op jit(solution)/shard_map/ppermute | solution.py:163
  4.0 1.2 copy-done
  5.5 0.7 fusion.2
  6.3 33.7 %all_gather.3.sums_ref = f32[1024,128]{1,0:T(8,128)S(1)} all-gather(f32[64,128]{1,0:T(8,128)S(1)} %shard_map.82), channel_id=1, replica_groups=mesh['section'=2,'dp'=2,'tensor'=8] {'dp','tensor'}, dimensions={0}, use_global_device_ids=true | all-gather | bytes 557056 | tf_op jit(solution)/shard_map/all_gather | solution.py:181
  40.0 1.1 copy-done.1
  42.6 18.3 %shard_map.83 = (f32[128,3072]{1,0:T(8,128)S(1)}, bf16[128,3072]{1,0:T(8,128)(2,1)S(1)}) custom-call(s32[2]{0:T(128)S(1)} %get-tuple-element.51.at_ref, bf16[64,6144]{1,0:T(8,128)(2,1)S(1)} %bitcast.14, bf16[64,6144]{1,0:T(8,128)(2,1)S(1)} %collective-permute-done.1.b_ref, f32[1024,128]{1,0:T(8,128)S(1)} %all_gather.3.sums_ref, f32[1,6144]{1,0:T(1,128)S(1)} %copy-done.3, ...), custom_call_target="tpu_custom_call" | custom-call | flops 20000000000 | bytes 80000000 | tf_op jit(solution)/shard_map/pallas_call | solution.py:74
  61.3 1.9 collective-permute-done.4.b_ref
  63.2 18.3 %shard_map.84 = (f32[128,3072]{1,0:T(8,128)S(1)}, bf16[128,3072]{1,0:T(8,128)(2,1)S(1)}) custom-call(s32[2]{0:T(128)S(1)} %get-tuple-element.50.at_ref, bf16[64,6144]{1,0:T(8,128)(2,1)S(1)} %collective-permute-done.a_ref, bf16[64,6144]{1,0:T(8,128)(2,1)S(1)} %collective-permute-done.4.b_ref, f32[1024,128]{1,0:T(8,128)S(1)} %all_gather.3.sums_ref, ...), custom_call_target="tpu_custom_call" | custom-call | flops 20000000000 | bytes 80000000 | tf_op jit(solution)/shard_map/pallas_call | solution.py:74
  82.1 1.7 collective-permute-start.8
  83.9 18.3 %shard_map.85 = (f32[128,3072]{1,0:T(8,128)S(1)}, bf16[128,3072]{1,0:T(8,128)(2,1)S(1)}) custom-call(s32[2]{0:T(128)S(1)} %get-tuple-element.52.at_ref, bf16[64,6144]{1,0:T(8,128)(2,1)S(1)} %collective-permute-done.3.a_ref, bf16[64,6144]{1,0:T(8,128)(2,1)S(1)} %collective-permute-done.6.b_ref, f32[1024,128]{1,0:T(8,128)S(1)} %all_gather.3.sums_ref, ...), custom_call_target="tpu_custom_call" | custom-call | flops 20000000000 | bytes 80000000 | tf_op jit(solution)/shard_map/pallas_call | solution.py:74
  102.2 19.0 %shard_map.86 = (f32[64,6144]{1,0:T(8,128)S(1)}, bf16[64,6144]{1,0:T(8,128)(2,1)S(1)}) custom-call(f32[128,3072]{1,0:T(8,128)S(1)} %get-tuple-element.33.rest_0_.own_ref, bf16[128,3072]{1,0:T(8,128)(2,1)S(1)} %collective-permute-done.8.other_ref, f32[1,3072]{1,0:T(1,128)S(1)} %copy-done.7, bf16[1,3072,6144]{2,1,0:T(8,128)(2,1)} %w_ref.15, ...), custom_call_target="tpu_custom_call" | custom-call | flops 20000000000 | bytes 80000000 | tf_op jit(solution)/shard_map/pallas_call | solution.py:126
  121.7 1.7 collective-permute-start.2
  124.5 1.1 collective-permute-done.7.b_ref
  125.6 18.3 %shard_map.87 = (f32[128,3072]{1,0:T(8,128)S(1)}, bf16[128,3072]{1,0:T(8,128)(2,1)S(1)}) custom-call(s32[2]{0:T(128)S(1)} %get-tuple-element.49.at_ref, bf16[64,6144]{1,0:T(8,128)(2,1)S(1)} %collective-permute-done.5.a_ref, bf16[64,6144]{1,0:T(8,128)(2,1)S(1)} %collective-permute-done.7.b_ref, f32[1024,128]{1,0:T(8,128)S(1)} %all_gather.3.sums_ref, ...), custom_call_target="tpu_custom_call" | custom-call | flops 20000000000 | bytes 80000000 | tf_op jit(solution)/shard_map/pallas_call | solution.py:74
  143.9 0.9 collective-permute-start.10
  144.8 14.1 %collective-permute-done.11.other_ref = bf16[128,3072]{1,0:T(8,128)(2,1)S(1)} collective-permute-done((bf16[128,3072]{1,0:T(8,128)(2,1)S(1)}, bf16[128,3072]{1,0:T(8,128)(2,1)S(1)}, u32[]{:S(2)}, u32[]{:S(2)}) %collective-permute-start.11) | collective-permute-done | bytes 786464 | tf_op jit(solution)/shard_map/ppermute | solution.py:172
  158.9 19.0 %shard_map.88 = (f32[64,6144]{1,0:T(8,128)S(1)}, bf16[64,6144]{1,0:T(8,128)(2,1)S(1)}) custom-call(f32[128,3072]{1,0:T(8,128)S(1)} %get-tuple-element.37.rest_0_.own_ref, bf16[128,3072]{1,0:T(8,128)(2,1)S(1)} %collective-permute-done.11.other_ref, f32[1,3072]{1,0:T(1,128)S(1)} %copy-done.7, bf16[1,3072,6144]{2,1,0:T(8,128)(2,1)} %w_ref.15, ...), custom_call_target="tpu_custom_call" | custom-call | flops 20000000000 | bytes 80000000 | tf_op jit(solution)/shard_map/pallas_call | solution.py:126
  178.0 19.0 %shard_map.89 = (f32[64,6144]{1,0:T(8,128)S(1)}, bf16[64,6144]{1,0:T(8,128)(2,1)S(1)}) custom-call(f32[128,3072]{1,0:T(8,128)S(1)} %get-tuple-element.40.rest_0_.own_ref, bf16[128,3072]{1,0:T(8,128)(2,1)S(1)} %collective-permute-done.10.other_ref, f32[1,3072]{1,0:T(1,128)S(1)} %copy-done.7, bf16[1,3072,6144]{2,1,0:T(8,128)(2,1)} %w_ref.15, ...), custom_call_target="tpu_custom_call" | custom-call | flops 20000000000 | bytes 80000000 | tf_op jit(solution)/shard_map/pallas_call | solution.py:126
  198.3 19.0 %shard_map.90 = (f32[64,6144]{1,0:T(8,128)S(1)}, bf16[64,6144]{1,0:T(8,128)(2,1)S(1)}) custom-call(f32[128,3072]{1,0:T(8,128)S(1)} %get-tuple-element.28.rest_0_.own_ref, bf16[128,3072]{1,0:T(8,128)(2,1)S(1)} %collective-permute-done.2.other_ref, f32[1,3072]{1,0:T(1,128)S(1)} %copy-done.7, bf16[1,3072,6144]{2,1,0:T(8,128)(2,1)} %w_ref.15, ...), custom_call_target="tpu_custom_call" | custom-call | flops 20000000000 | bytes 80000000 | tf_op jit(solution)/shard_map/pallas_call | solution.py:126
  217.7 1.8 collective-permute-start.17
  219.7 18.0 %collective-permute-done.17 = bf16[64,6144]{1,0:T(8,128)(2,1)S(1)} collective-permute-done((bf16[64,6144]{1,0:T(8,128)(2,1)S(1)}, bf16[64,6144]{1,0:T(8,128)(2,1)S(1)}, u32[]{:S(2)}, u32[]{:S(2)}) %collective-permute-start.17) | collective-permute-done | bytes 786464 | tf_op jit(solution)/shard_map/ppermute | solution.py:163
  238.1 1.6 collective-permute-start.18
  239.7 17.3 %collective-permute-done.18 = bf16[64,6144]{1,0:T(8,128)(2,1)S(1)} collective-permute-done((bf16[64,6144]{1,0:T(8,128)(2,1)S(1)}, bf16[64,6144]{1,0:T(8,128)(2,1)S(1)}, u32[]{:S(2)}, u32[]{:S(2)}) %collective-permute-start.18) | collective-permute-done | bytes 786464 | tf_op jit(solution)/shard_map/ppermute | solution.py:232
  257.0 0.9 copy.10
  (48 shorter events, 7.2 us)
Async XLA Ops:
  0.0 40.0 %collective-permute-start.1 = (bf16[64,6144]{1,0:T(8,128)(2,1)}, bf16[64,6144]{1,0:T(8,128)(2,1)S(1)}, u32[]{:S(2)}, u32[]{:S(2)}) collective-permute-start(bf16[64,6144]{1,0:T(8,128)(2,1)} %bitcast.12), channel_id=1, source_target_pairs={{0,1},{1,0},{2,3},{3,2},{4,5},{5,4},{6,7},{7,6},{8,9},{9,8},{10,11... | collective-permute-start | bytes 2359304 | tf_op jit(solution)/shard_map/ppermute | solution.py:166
  0.5 60.4 %collective-permute-start = (bf16[64,6144]{1,0:T(8,128)(2,1)}, bf16[64,6144]{1,0:T(8,128)(2,1)S(1)}, u32[]{:S(2)}, u32[]{:S(2)}) collective-permute-start(bf16[64,6144]{1,0:T(8,128)(2,1)} %bitcast.13), channel_id=1, source_target_pairs={{0,4},{1,5},{4,6},{5,7},{6,2},{7,3},{2,0},{3,1},{8,12},{9,13},{12,... | collective-permute-start | bytes 2359304 | tf_op jit(solution)/shard_map/ppermute | solution.py:163
  60.9 2.4 collective-permute-start.4
  61.3 20.2 %collective-permute-start.3 = (bf16[64,6144]{1,0:T(8,128)(2,1)S(1)}, bf16[64,6144]{1,0:T(8,128)(2,1)S(1)}, u32[]{:S(2)}, u32[]{:S(2)}) collective-permute-start(bf16[64,6144]{1,0:T(8,128)(2,1)S(1)} %collective-permute-done.a_ref), channel_id=1, source_target_pairs={{0,4},{1,5},{4,6},{5,7},{6,2},{7,3},{2,0},{3,1},{8,12},{9,13},{12,... | collective-permute-start | bytes 2359304 | tf_op jit(solution)/shard_map/ppermute | solution.py:163
  81.5 2.4 collective-permute-start.6
  82.0 20.2 %collective-permute-start.5 = (bf16[64,6144]{1,0:T(8,128)(2,1)S(1)}, bf16[64,6144]{1,0:T(8,128)(2,1)S(1)}, u32[]{:S(2)}, u32[]{:S(2)}) collective-permute-start(bf16[64,6144]{1,0:T(8,128)(2,1)S(1)} %collective-permute-done.3.a_ref), channel_id=1, source_target_pairs={{0,4},{1,5},{4,6},{5,7},{6,2},{7,3},{2,0},{3,1},{8,12},{9,13},{12,... | collective-permute-start | bytes 2359304 | tf_op jit(solution)/shard_map/ppermute | solution.py:163
  82.1 20.1 %collective-permute-start.8 = (bf16[128,3072]{1,0:T(8,128)(2,1)S(1)}, bf16[128,3072]{1,0:T(8,128)(2,1)S(1)}, u32[]{:S(2)}, u32[]{:S(2)}) collective-permute-start(bf16[128,3072]{1,0:T(8,128)(2,1)S(1)} %get-tuple-element.36), channel_id=1, source_target_pairs={{0,8},{8,0},{1,9},{9,1},{2,10},{10,2},{3,11},{11,3},{4,12},{12,4},... | collective-permute-start | bytes 2359304 | tf_op jit(solution)/shard_map/ppermute | solution.py:172
  83.9 18.3 %copy-start.7 = (f32[1,3072]{1,0:T(1,128)S(1)}, f32[1,3072]{1,0:T(1,128)}, u32[]{:S(2)}) copy-start(f32[1,3072]{1,0:T(1,128)} %bias_ref.7) | copy-start | bytes 36868
  121.2 2.4 collective-permute-start.9
  121.7 76.6 %collective-permute-start.2 = (bf16[128,3072]{1,0:T(8,128)(2,1)S(1)}, bf16[128,3072]{1,0:T(8,128)(2,1)S(1)}, u32[]{:S(2)}, u32[]{:S(2)}) collective-permute-start(bf16[128,3072]{1,0:T(8,128)(2,1)S(1)} %get-tuple-element.29), channel_id=1, source_target_pairs={{0,8},{8,0},{1,9},{9,1},{2,10},{10,2},{3,11},{11,3},{4,12},{12,4},... | collective-permute-start | bytes 2359304 | tf_op jit(solution)/shard_map/ppermute | solution.py:172
  123.3 2.3 collective-permute-start.7
  123.3 35.6 %collective-permute-start.11 = (bf16[128,3072]{1,0:T(8,128)(2,1)S(1)}, bf16[128,3072]{1,0:T(8,128)(2,1)S(1)}, u32[]{:S(2)}, u32[]{:S(2)}) collective-permute-start(bf16[128,3072]{1,0:T(8,128)(2,1)S(1)} %get-tuple-element.42), channel_id=1, source_target_pairs={{0,8},{8,0},{1,9},{9,1},{2,10},{10,2},{3,11},{11,3},{4,12},{12,4},... | collective-permute-start | bytes 2359304 | tf_op jit(solution)/shard_map/ppermute | solution.py:172
  123.7 1.9 copy-start.4
  123.7 1.9 copy-start.6
  123.9 73.7 %collective-permute-start.15 = (bf16[64,6144]{1,0:T(8,128)(2,1)S(1)}, bf16[64,6144]{1,0:T(8,128)(2,1)S(1)}, u32[]{:S(2)}, u32[]{:S(2)}) collective-permute-start(bf16[64,6144]{1,0:T(8,128)(2,1)S(1)} %add_convert_fusion.3.rest_0_), channel_id=1, source_target_pairs={{0,4},{1,5},{4,6},{5,7},{6,2},{7,3},{2,0},{3,1},{8,12},{9,13},{12,... | collective-permute-start | bytes 2359304 | tf_op jit(solution)/shard_map/ppermute | solution.py:163
  143.9 34.1 %collective-permute-start.10 = (bf16[128,3072]{1,0:T(8,128)(2,1)S(1)}, bf16[128,3072]{1,0:T(8,128)(2,1)S(1)}, u32[]{:S(2)}, u32[]{:S(2)}) collective-permute-start(bf16[128,3072]{1,0:T(8,128)(2,1)S(1)} %get-tuple-element.41), channel_id=1, source_target_pairs={{0,8},{8,0},{1,9},{9,1},{2,10},{10,2},{3,11},{11,3},{4,12},{12,4},... | collective-permute-start | bytes 2359304 | tf_op jit(solution)/shard_map/ppermute | solution.py:172
  177.9 19.7 %collective-permute-start.14 = (bf16[64,6144]{1,0:T(8,128)(2,1)S(1)}, bf16[64,6144]{1,0:T(8,128)(2,1)S(1)}, u32[]{:S(2)}, u32[]{:S(2)}) collective-permute-start(bf16[64,6144]{1,0:T(8,128)(2,1)S(1)} %get-tuple-element.48), channel_id=1, source_target_pairs={{0,1},{1,0},{2,3},{3,2},{4,5},{5,4},{6,7},{7,6},{8,9},{9,8},{10,11... | collective-permute-start | bytes 2359304 | tf_op jit(solution)/shard_map/ppermute | solution.py:166
  197.0 20.4 %collective-permute-start.13 = (bf16[64,6144]{1,0:T(8,128)(2,1)S(1)}, bf16[64,6144]{1,0:T(8,128)(2,1)S(1)}, u32[]{:S(2)}, u32[]{:S(2)}) collective-permute-start(bf16[64,6144]{1,0:T(8,128)(2,1)S(1)} %get-tuple-element.47), channel_id=1, source_target_pairs={{0,1},{1,0},{2,3},{3,2},{4,5},{5,4},{6,7},{7,6},{8,9},{9,8},{10,11... | collective-permute-start | bytes 2359304 | tf_op jit(solution)/shard_map/ppermute | solution.py:166
  197.8 19.6 %collective-permute-start.16 = (bf16[64,6144]{1,0:T(8,128)(2,1)S(1)}, bf16[64,6144]{1,0:T(8,128)(2,1)S(1)}, u32[]{:S(2)}, u32[]{:S(2)}) collective-permute-start(bf16[64,6144]{1,0:T(8,128)(2,1)S(1)} %add_convert_fusion.2), channel_id=1, source_target_pairs={{0,4},{1,5},{4,6},{5,7},{6,2},{7,3},{2,0},{3,1},{8,12},{9,13},{12,... | collective-permute-start | bytes 2359304 | tf_op jit(solution)/shard_map/ppermute | solution.py:163
  217.3 20.4 %copy-start.2 = (bf16[1,64,6144]{2,1,0:T(8,128)(2,1)S(1)}, bf16[1,64,6144]{2,1,0:T(8,128)(2,1)}, u32[]{:S(2)}) copy-start(bf16[1,64,6144]{2,1,0:T(8,128)(2,1)} %x_ref.1) | copy-start | bytes 2359300
  217.3 20.4 %copy-start.8 = (f32[1,6144]{1,0:T(1,128)S(1)}, f32[1,6144]{1,0:T(1,128)}, u32[]{:S(2)}) copy-start(f32[1,6144]{1,0:T(1,128)} %param.14) | copy-start | bytes 73732
  217.3 2.4 collective-permute-start.12
  217.7 20.0 %collective-permute-start.17 = (bf16[64,6144]{1,0:T(8,128)(2,1)S(1)}, bf16[64,6144]{1,0:T(8,128)(2,1)S(1)}, u32[]{:S(2)}, u32[]{:S(2)}) collective-permute-start(bf16[64,6144]{1,0:T(8,128)(2,1)S(1)} %add_convert_fusion.1), channel_id=1, source_target_pairs={{0,4},{1,5},{4,6},{5,7},{6,2},{7,3},{2,0},{3,1},{8,12},{9,13},{12,... | collective-permute-start | bytes 2359304 | tf_op jit(solution)/shard_map/ppermute | solution.py:163
  238.1 18.9 %collective-permute-start.18 = (bf16[64,6144]{1,0:T(8,128)(2,1)S(1)}, bf16[64,6144]{1,0:T(8,128)(2,1)S(1)}, u32[]{:S(2)}, u32[]{:S(2)}) collective-permute-start(bf16[64,6144]{1,0:T(8,128)(2,1)S(1)} %add_convert_fusion), channel_id=1, source_target_pairs={{0,16},{16,0},{1,17},{17,1},{2,18},{18,2},{3,19},{19,3},{4,20},{20... | collective-permute-start | bytes 2359304 | tf_op jit(solution)/shard_map/ppermute | solution.py:232
  (4 other events, 3.8 us)

commit v3 on v1

v3 whole, which is shorter than its diff:
```python
import jax
import jax.numpy as jnp
from jax import lax
from jax.sharding import PartitionSpec as P

F32 = jnp.float32
BF16 = jnp.bfloat16


def ring_order(n):
    return list(range(0, n, 2)) + list(range(1, n, 2))[::-1]


def make_per_device(width, n_section, n_dp, n_tensor):
    chips = n_tensor // 2
    order = ring_order(chips)
    along = [
        (order[i] * 2 + c, order[(i + 1) % chips] * 2 + c) for i in range(chips) for c in range(2)
    ]
    swap = [(i, i ^ 1) for i in range(n_tensor)]
    turn = [(i, (i + 1) % n_section) for i in range(n_section)]
    along_and_turn = [
        (s * n_tensor + a, t * n_tensor + b) for s, t in turn for a, b in along
    ]

    def forward(block):
        return lax.ppermute(block, "tensor", along)

    def sibling(block):
        return lax.ppermute(block, "tensor", swap)

    def from_others(sent):
        total = None
        for hop in range(1, n_dp):
            route = [(i, (i + hop) % n_dp) for i in range(n_dp)]
            got = lax.ppermute(sent, "dp", route)
            total = got if total is None else total.astype(F32) + got.astype(F32)
        return total

    def per_device(incoming, norm_gain, norm_shift, up_weight, up_bias, down_weight, down_bias):
        rows = incoming.shape[1]
        x = incoming[0].astype(F32)
        sums = jnp.stack(
            lax.reduce(
                (x, x * x), (F32(0), F32(0)), lambda a, b: (a[0] + b[0], a[1] + b[1]), (1,)
            )
        )
        total, square = sums + from_others(sums)
        mean = total / width
        var = square / width - mean * mean
        normed = (
            (x - mean[:, None]) * lax.rsqrt(var + 1e-05)[:, None] * norm_gain[0] + norm_shift[0]
        ).astype(BF16)

        blocks, pres = [(normed, sibling(normed))], []

        def tie(values, done):
            return lax.optimization_barrier((values, done))[0]

        def up(k):
            block = blocks[k][0]
            coming = forward(block) if k < chips - 1 else None
            both = jnp.concatenate(blocks[k], axis=0)
            pre = jnp.dot(both, up_weight[0], preferred_element_type=F32)
            other = from_others(pre.astype(BF16))
            if coming is not None:
                coming = tie(coming, pre)
                blocks.append((coming, sibling(coming)))
            pres.append((pre, other))
            return pre

        def act(k, done):
            pre, other = pres[k]
            if done is not None:
                other = tie(other, done)
            return jax.nn.gelu(pre + other.astype(F32) + up_bias[0], approximate=True).astype(BF16)

        def send(k, value):
            if k < chips - 1:
                return forward(value)
            return lax.ppermute(value, ("section", "tensor"), along_and_turn)

        up(0)
        residual = lax.ppermute(incoming[0], "section", turn)
        for k in range(1, chips):
            if k == 1:
                blocks[1] = tie(blocks[1], residual)
                up(1)
                done = (pres[1][0], pres[0][1])
                if chips > 2:
                    blocks[2] = tie(blocks[2], done)
                    done = up(2)
                both = jnp.concatenate([act(1, done), act(0, None)], axis=0)
                part = jnp.dot(both, down_weight[0], preferred_element_type=F32)
                if chips > 2:
                    part = tie(part, pres[2][1])
                got = sibling(part[rows : 2 * rows].astype(BF16))
                summed = (part[:rows] + got.astype(F32)).astype(BF16)
                running = send(1, summed)
                own = part[2 * rows : 3 * rows] + sibling(part[3 * rows :].astype(BF16)).astype(F32)
                own = lax.ppermute((own + down_bias[0]).astype(BF16), "section", turn)
                continue
            if k + 1 < chips:
                blocks[k + 1] = tie(blocks[k + 1], summed)
                done = (up(k + 1), running, own)
            else:
                done = summed
            part = jnp.dot(act(k, done), down_weight[0], preferred_element_type=F32)
            part = tie(part, pres[k + 1][1] if k + 1 < chips else running)
            got = sibling(part[rows:].astype(BF16))
            summed = (part[:rows] + got.astype(F32) + running.astype(F32)).astype(BF16)
            running = send(k, summed)
        result = running.astype(F32) + own.astype(F32) + residual.astype(F32)
        return result.astype(BF16)[None]

    return per_device


def solution(mesh):
    placed = (
        P("section", "tensor", "dp"),
        P("section", "dp"),
        P("section", "dp"),
        P("section", "dp", "tensor"),
        P("section", "tensor"),
        P("section", "tensor", "dp"),
        P("section", "dp"),
    )

    def run(*args):
        body = make_per_device(
            args[0].shape[2], mesh.shape["section"], mesh.shape["dp"], mesh.shape["tensor"]
        )
        return jax.shard_map(
            body,
            mesh=mesh,
            in_specs=placed,
            out_specs=P("section", "tensor", "dp"),
            check_vma=False,
        )(*args)

    return run
```

time: 243 us -> 191 us (0.79)
  waiting for transfers between devices: 81.5 us -> 42.6 us
  matrix products: 122 us -> 109 us
  blocking collectives: 5.85 us -> 0 us
  other arithmetic: 6.49 us -> 10.6 us
    ppermute x5 -> x8, waiting for transfers between devices: 48.4 us -> 22.3 us  [the longest x1 18 us: send(): return lax.ppermute(value, ('section', 'tensor'), along_and_turn)]
    ppermute x6 -> x5, waiting for transfers between devices: 33.2 us -> 10 us  [forward(): return lax.ppermute(block, 'tensor', along)]
    dot_general x8 -> x7, matrix products: 122 us -> 109 us  [the longest x4 60.1 us: up(): pre = jnp.dot(both, up_weight[0], preferred_element_type=F32)]
    ppermute x8, waiting for transfers between devices: 0.02 us -> 10.3 us  [sibling(): return lax.ppermute(block, 'tensor', swap)]
    psum x1 -> x0, blocking collectives: 5.85 us -> none  [per_device(): total, square = lax.psum((jnp.sum(x, axis=1), jnp.sum(x * x, axis=1)), 'dp')]
    ppermute x5 -> x8, starting transfers between devices: 7.79 us -> 13.6 us  [the longest x5 8.01 us: from_others(): got = lax.ppermute(sent, 'dp', route)]
    another operation x0 -> x3, other arithmetic: none -> 4.92 us  [the longest x1 3.37 us: run(): jax.shard_map(body, mesh=mesh, in_specs=placed, out_specs=P('section', 't...]
    ppermute x6 -> x5, starting transfers between devices: 14.5 us -> 11.7 us  [forward(): return lax.ppermute(block, 'tensor', along)]
  transfers between devices with their start and end apart: 19 -> 21, of which waited for: 6 -> 14; matrix products, arithmetic and copies ran while one was open for 52% -> 60% of each run, Pallas kernels for 0% -> 0%
where the time goes in v3:
time: 191 us
  matrix products  109 us (57%)
  waiting for transfers between devices  42.6 us (22%)
  starting transfers between devices  26.1 us (14%)
  other arithmetic  10.6 us (6%)
  local copies, waits for them, and re-layouts  2.05 us (1%)
    dot_general x4, matrix products, up(): pre = jnp.dot(both, up_weight[0], preferred_element_type=F32)  60.1 us
    dot_general x2, matrix products, per_device(): part = jnp.dot(act(k, done), down_weight[0], preferred_element_type=F32)  30 us
    dot_general x1, matrix products, per_device(): part = jnp.dot(both, down_weight[0], preferred_element_type=F32)  18.8 us
    ppermute x1, waiting for transfers between devices, send(): return lax.ppermute(value, ('section', 'tensor'), along_and_turn)  18 us
    ppermute x5, starting transfers between devices, forward(): return lax.ppermute(block, 'tensor', along)  11.7 us
    ppermute x8, waiting for transfers between devices, sibling(): return lax.ppermute(block, 'tensor', swap)  10.3 us
    ppermute x5, waiting for transfers between devices, forward(): return lax.ppermute(block, 'tensor', along)  10 us
    ppermute x5, starting transfers between devices, from_others(): got = lax.ppermute(sent, 'dp', route)  8.01 us
  transfers between devices with their start and end apart: 21, of which 14 were waited for; matrix products, arithmetic and copies ran while one was open for 60% of the time, Pallas kernels for 0%

profile of v3, /device:TPU:0, one launch (start us, length us, event | category | flops | bytes accessed | tf_op | source)
XLA Modules:
  0.0 190.5 jit_solution(7914606540500615338)
XLA Ops:
  1.6 3.0 %collective-permute-start = (f32[2,64]{1,0:T(2,128)S(1)}, f32[2,64]{1,0:T(2,128)S(1)}, u32[]{:S(2)}, u32[]{:S(2)}) collective-permute-start(f32[2,64]{1,0:T(2,128)S(1)} %pad_maximum_fusion), channel_id=1, source_target_pairs={{0,8},{8,0},{1,9},{9,1},{2,10},{10,2},{3,11},{11,3},{4,12},{12,4},... | collective-permute-start | bytes 1544 | tf_op jit(solution)/shard_map/ppermute | solution.py:36
  4.6 1.5 collective-permute-done
  7.7 2.1 %collective-permute-start.4 = (bf16[64,6144]{1,0:T(8,128)(2,1)S(1)}, bf16[64,6144]{1,0:T(8,128)(2,1)S(1)}, u32[]{:S(2)}, u32[]{:S(2)}) collective-permute-start(bf16[64,6144]{1,0:T(8,128)(2,1)S(1)} %bitcast.45), channel_id=1, source_target_pairs={{0,16},{16,0},{1,17},{17,1},{2,18},{18,2},{3,19},{19,3},{4,20},{20... | collective-permute-start | bytes 2359304 | tf_op jit(solution)/shard_map/ppermute | solution.py:84
  9.9 2.6 %collective-permute-start.1 = (bf16[64,6144]{1,0:T(8,128)(2,1)S(1)}, bf16[64,6144]{1,0:T(8,128)(2,1)S(1)}, u32[]{:S(2)}, u32[]{:S(2)}) collective-permute-start(bf16[64,6144]{1,0:T(8,128)(2,1)S(1)} %fusion.17), channel_id=1, source_target_pairs={{0,4},{1,5},{4,6},{5,7},{6,2},{7,3},{2,0},{3,1},{8,12},{9,13},{12,... | collective-permute-start | bytes 2359304 | tf_op jit(solution)/shard_map/ppermute | solution.py:27
  12.5 14.4 %fusion.96 = (bf16[128,3072]{1,0:T(8,128)(2,1)S(1)}, f32[128,3072]{1,0:T(8,128)S(1)}) fusion(bf16[1,6144,3072]{2,1,0:T(8,128)(2,1)} %param.10, bf16[64,6144]{1,0:T(8,128)(2,1)S(1)} %collective-permute-done.2, bf16[64,6144]{1,0:T(8,128)(2,1)S(1)} %fusion.17), kind=kOutput, calls=%fused_computation.110 | convolution fusion | flops 4835377152 | bytes 41680896 | tf_op jit(solution)/shard_map/dot_general | solution.py:64
  26.8 2.7 %collective-permute-done.1 = bf16[64,6144]{1,0:T(8,128)(2,1)S(1)} collective-permute-done((bf16[64,6144]{1,0:T(8,128)(2,1)S(1)}, bf16[64,6144]{1,0:T(8,128)(2,1)S(1)}, u32[]{:S(2)}, u32[]{:S(2)}) %collective-permute-start.1) | collective-permute-done | bytes 786464 | tf_op jit(solution)/shard_map/ppermute | solution.py:27
  31.9 3.4 %collective-permute-start.5 = (bf16[64,6144]{1,0:T(8,128)(2,1)S(1)}, bf16[64,6144]{1,0:T(8,128)(2,1)}, u32[]{:S(2)}, u32[]{:S(2)}) collective-permute-start(bf16[64,6144]{1,0:T(8,128)(2,1)S(1)} %collective-permute-done.1), channel_id=1, source_target_pairs={{0,4},{1,5},{4,6},{5,7},{6,2},{7,3},{2,0},{3,1},{8,12},{9,13},{12,... | collective-permute-start | bytes 2359304 | tf_op jit(solution)/shard_map/ppermute | solution.py:27
  35.2 14.4 %fusion.95 = (bf16[128,3072]{1,0:T(8,128)(2,1)S(1)}, f32[128,3072]{1,0:T(8,128)S(1)}) fusion(bf16[1,6144,3072]{2,1,0:T(8,128)(2,1)} %param.10, bf16[64,6144]{1,0:T(8,128)(2,1)S(1)} %collective-permute-done.3, bf16[64,6144]{1,0:T(8,128)(2,1)S(1)} %collective-permute-done.1), kind=kOutput, calls=%fused_computation.109 | convolution fusion | flops 4835377152 | bytes 41680896 | tf_op jit(solution)/shard_map/dot_general | solution.py:64
  49.6 2.7 %collective-permute-done.5 = bf16[64,6144]{1,0:T(8,128)(2,1)} collective-permute-done((bf16[64,6144]{1,0:T(8,128)(2,1)S(1)}, bf16[64,6144]{1,0:T(8,128)(2,1)}, u32[]{:S(2)}, u32[]{:S(2)}) %collective-permute-start.5) | collective-permute-done | bytes 786464 | tf_op jit(solution)/shard_map/ppermute | solution.py:27
  55.7 3.5 %collective-permute-start.8 = (bf16[64,6144]{1,0:T(8,128)(2,1)}, bf16[64,6144]{1,0:T(8,128)(2,1)}, u32[]{:S(2)}, u32[]{:S(2)}) collective-permute-start(bf16[64,6144]{1,0:T(8,128)(2,1)} %collective-permute-done.5), channel_id=1, source_target_pairs={{0,4},{1,5},{4,6},{5,7},{6,2},{7,3},{2,0},{3,1},{8,12},{9,13},{12,... | collective-permute-start | bytes 2359304 | tf_op jit(solution)/shard_map/ppermute | solution.py:27
  59.2 15.7 %fusion.97 = (bf16[128,3072]{1,0:T(8,128)(2,1)}, f32[128,3072]{1,0:T(8,128)S(1)}) fusion(bf16[1,6144,3072]{2,1,0:T(8,128)(2,1)} %param.10, bf16[64,6144]{1,0:T(8,128)(2,1)} %copy-done.5, bf16[64,6144]{1,0:T(8,128)(2,1)} %collective-permute-done.5), kind=kOutput, calls=%fused_computation.111 | convolution fusion | flops 4835377152 | bytes 41680896 | tf_op jit(solution)/shard_map/dot_general | solution.py:64
  76.4 2.2 %fusion.25 = (bf16[128,3072]{1,0:T(8,128)(2,1)S(1)}, bf16[128,3072]{1,0:T(8,128)(2,1)}) fusion(f32[128,3072]{1,0:T(8,128)S(1)} %get-tuple-element.46, bf16[128,3072]{1,0:T(8,128)(2,1)S(1)} %collective-permute-done.10, f32[3072]{0:T(1024)S(1)} %bitcast.46, f32[128,3072]{1,0:T(8,128)S(1)} %get-tuple-element.48, bf16[128,3072]{1,0:T(8,128)(2,1)S(1)} %collective-permute-done.7), kind=kLoop, calls=%fused_computation.31 | loop fusion | flops 9437184 | bytes 6303744 | tf_op jit(solution)/shard_map/convert_element_type | solution.py:76
  78.6 18.8 %fusion.4 = f32[256,6144]{1,0:T(8,128)} fusion(bf16[1,3072,6144]{2,1,0:T(8,128)(2,1)} %param.12, bf16[128,3072]{1,0:T(8,128)(2,1)} %get-tuple-element.44, bf16[128,3072]{1,0:T(8,128)(2,1)S(1)} %get-tuple-element.43), kind=kOutput, calls=%fused_computation.4 | convolution fusion | flops 9666822144 | bytes 45613056 | tf_op jit(solution)/shard_map/dot_general | solution.py:94
  97.4 3.4 %convert.10 = bf16[256,6144]{1,0:T(8,128)(2,1)S(1)} convert(f32[256,6144]{1,0:T(8,128)} %fusion.4) | non-fusion elementwise | flops 1572864 | bytes 9437184 | tf_op jit(solution)/shard_map/convert.3 | solution.py:134
  101.5 1.7 collective-permute-done.12
  103.2 2.2 %collective-permute-done.15 = bf16[64,6144]{1,0:T(8,128)(2,1)S(1)} collective-permute-done((bf16[64,6144]{1,0:T(8,128)(2,1)S(1)}, bf16[64,6144]{1,0:T(8,128)(2,1)S(1)}, u32[]{:S(2)}, u32[]{:S(2)}) %collective-permute-start.15) | collective-permute-done | bytes 786464 | tf_op jit(solution)/shard_map/ppermute | solution.py:30
  108.4 15.7 %fusion.98 = (bf16[128,3072]{1,0:T(8,128)(2,1)}, f32[128,3072]{1,0:T(8,128)S(1)}) fusion(bf16[1,6144,3072]{2,1,0:T(8,128)(2,1)} %param.10, bf16[64,6144]{1,0:T(8,128)(2,1)} %copy-done.4, bf16[64,6144]{1,0:T(8,128)(2,1)} %collective-permute-done.8), kind=kOutput, calls=%fused_computation.112 | convolution fusion | flops 4835377152 | bytes 41680896 | tf_op jit(solution)/shard_map/dot_general | solution.py:64
  127.2 15.0 %fusion.2 = f32[128,6144]{1,0:T(8,128)S(1)} fusion(bf16[1,3072,6144]{2,1,0:T(8,128)(2,1)} %param.12, f32[128,3072]{1,0:T(8,128)S(1)} %get-tuple-element.50, bf16[128,3072]{1,0:T(8,128)(2,1)} %collective-permute-done.11, f32[3072]{0:T(1024)S(1)} %bitcast.47), kind=kOutput, calls=%fused_computation.2 | convolution fusion | flops 4836556800 | bytes 43266048 | tf_op jit(solution)/shard_map/dot_general | solution.py:108
  143.6 2.3 %collective-permute-done.17 = bf16[64,6144]{1,0:T(8,128)(2,1)S(1)} collective-permute-done((bf16[64,6144]{1,0:T(8,128)(2,1)S(1)}, bf16[64,6144]{1,0:T(8,128)(2,1)S(1)}, u32[]{:S(2)}, u32[]{:S(2)}) %collective-permute-start.17) | collective-permute-done | bytes 786464 | tf_op jit(solution)/shard_map/ppermute | solution.py:30
  147.2 15.0 %fusion = f32[128,6144]{1,0:T(8,128)S(1)} fusion(bf16[1,3072,6144]{2,1,0:T(8,128)(2,1)} %param.12, f32[128,3072]{1,0:T(8,128)S(1)} %get-tuple-element.52, bf16[128,3072]{1,0:T(8,128)(2,1)} %collective-permute-done.13, f32[3072]{0:T(1024)S(1)} %bitcast.48), kind=kOutput, calls=%fused_computation | convolution fusion | flops 4836556800 | bytes 43266048 | tf_op jit(solution)/shard_map/dot_general | solution.py:108
  162.3 3.5 %collective-permute-done.18 = bf16[64,6144]{1,0:T(8,128)(2,1)S(1)} collective-permute-done((bf16[64,6144]{1,0:T(8,128)(2,1)S(1)}, bf16[64,6144]{1,0:T(8,128)(2,1)S(1)}, u32[]{:S(2)}, u32[]{:S(2)}) %collective-permute-start.18) | collective-permute-done | bytes 786464 | tf_op jit(solution)/shard_map/ppermute | solution.py:27
  165.9 2.3 %collective-permute-done.19 = bf16[64,6144]{1,0:T(8,128)(2,1)S(1)} collective-permute-done((bf16[64,6144]{1,0:T(8,128)(2,1)S(1)}, bf16[64,6144]{1,0:T(8,128)(2,1)S(1)}, u32[]{:S(2)}, u32[]{:S(2)}) %collective-permute-start.19) | collective-permute-done | bytes 786464 | tf_op jit(solution)/shard_map/ppermute | solution.py:30
  168.4 2.9 %collective-permute-start.20 = (bf16[64,6144]{1,0:T(8,128)(2,1)S(1)}, bf16[64,6144]{1,0:T(8,128)(2,1)S(1)}, u32[]{:S(2)}, u32[]{:S(2)}) collective-permute-start(bf16[64,6144]{1,0:T(8,128)(2,1)S(1)} %add_convert_fusion.1), channel_id=1, source_target_pairs={{0,20},{1,21},{4,22},{5,23},{6,18},{7,19},{2,16},{3,17},{16,4},{17... | collective-permute-start | bytes 2359304 | tf_op jit(solution)/shard_map/ppermute | solution.py:81
  171.4 18.0 %collective-permute-done.20 = bf16[64,6144]{1,0:T(8,128)(2,1)S(1)} collective-permute-done((bf16[64,6144]{1,0:T(8,128)(2,1)S(1)}, bf16[64,6144]{1,0:T(8,128)(2,1)S(1)}, u32[]{:S(2)}, u32[]{:S(2)}) %collective-permute-start.20) | collective-permute-done | bytes 786464 | tf_op jit(solution)/shard_map/ppermute | solution.py:81
  (56 shorter events, 21.4 us)
Async XLA Ops:
  0.0 7.7 %copy-start.1 = (bf16[1,64,6144]{2,1,0:T(8,128)(2,1)S(1)}, bf16[1,64,6144]{2,1,0:T(8,128)(2,1)}, u32[]{:S(2)}) copy-start(bf16[1,64,6144]{2,1,0:T(8,128)(2,1)} %param.7) | copy-start | bytes 2359300
  1.6 4.5 %collective-permute-start = (f32[2,64]{1,0:T(2,128)S(1)}, f32[2,64]{1,0:T(2,128)S(1)}, u32[]{:S(2)}, u32[]{:S(2)}) collective-permute-start(f32[2,64]{1,0:T(2,128)S(1)} %pad_maximum_fusion), channel_id=1, source_target_pairs={{0,8},{8,0},{1,9},{9,1},{2,10},{10,2},{3,11},{11,3},{4,12},{12,4},... | collective-permute-start | bytes 1544 | tf_op jit(solution)/shard_map/ppermute | solution.py:36
  7.7 4.8 %collective-permute-start.2 = (bf16[64,6144]{1,0:T(8,128)(2,1)S(1)}, bf16[64,6144]{1,0:T(8,128)(2,1)S(1)}, u32[]{:S(2)}, u32[]{:S(2)}) collective-permute-start(bf16[64,6144]{1,0:T(8,128)(2,1)S(1)} %fusion.17), channel_id=1, source_target_pairs={{0,1},{1,0},{2,3},{3,2},{4,5},{5,4},{6,7},{7,6},{8,9},{9,8},{10,11... | collective-permute-start | bytes 2359304 | tf_op jit(solution)/shard_map/ppermute | solution.py:30
  7.7 23.3 %collective-permute-start.4 = (bf16[64,6144]{1,0:T(8,128)(2,1)S(1)}, bf16[64,6144]{1,0:T(8,128)(2,1)S(1)}, u32[]{:S(2)}, u32[]{:S(2)}) collective-permute-start(bf16[64,6144]{1,0:T(8,128)(2,1)S(1)} %bitcast.45), channel_id=1, source_target_pairs={{0,16},{16,0},{1,17},{17,1},{2,18},{18,2},{3,19},{19,3},{4,20},{20... | collective-permute-start | bytes 2359304 | tf_op jit(solution)/shard_map/ppermute | solution.py:84
  9.9 19.7 %collective-permute-start.1 = (bf16[64,6144]{1,0:T(8,128)(2,1)S(1)}, bf16[64,6144]{1,0:T(8,128)(2,1)S(1)}, u32[]{:S(2)}, u32[]{:S(2)}) collective-permute-start(bf16[64,6144]{1,0:T(8,128)(2,1)S(1)} %fusion.17), channel_id=1, source_target_pairs={{0,4},{1,5},{4,6},{5,7},{6,2},{7,3},{2,0},{3,1},{8,12},{9,13},{12,... | collective-permute-start | bytes 2359304 | tf_op jit(solution)/shard_map/ppermute | solution.py:27
  29.6 2.3 %collective-permute-start.3 = (bf16[64,6144]{1,0:T(8,128)(2,1)S(1)}, bf16[64,6144]{1,0:T(8,128)(2,1)S(1)}, u32[]{:S(2)}, u32[]{:S(2)}) collective-permute-start(bf16[64,6144]{1,0:T(8,128)(2,1)S(1)} %collective-permute-done.1), channel_id=1, source_target_pairs={{0,1},{1,0},{2,3},{3,2},{4,5},{5,4},{6,7},{7,6},{8,9},{9,8},{10,11... | collective-permute-start | bytes 2359304 | tf_op jit(solution)/shard_map/ppermute | solution.py:30
  29.6 24.3 %collective-permute-start.7 = (bf16[128,3072]{1,0:T(8,128)(2,1)S(1)}, bf16[128,3072]{1,0:T(8,128)(2,1)S(1)}, u32[]{:S(2)}, u32[]{:S(2)}) collective-permute-start(bf16[128,3072]{1,0:T(8,128)(2,1)S(1)} %get-tuple-element.47), channel_id=1, source_target_pairs={{0,8},{8,0},{1,9},{9,1},{2,10},{10,2},{3,11},{11,3},{4,12},{12,4},... | collective-permute-start | bytes 2359304 | tf_op jit(solution)/shard_map/ppermute | solution.py:36
  31.9 20.5 %collective-permute-start.5 = (bf16[64,6144]{1,0:T(8,128)(2,1)S(1)}, bf16[64,6144]{1,0:T(8,128)(2,1)}, u32[]{:S(2)}, u32[]{:S(2)}) collective-permute-start(bf16[64,6144]{1,0:T(8,128)(2,1)S(1)} %collective-permute-done.1), channel_id=1, source_target_pairs={{0,4},{1,5},{4,6},{5,7},{6,2},{7,3},{2,0},{3,1},{8,12},{9,13},{12,... | collective-permute-start | bytes 2359304 | tf_op jit(solution)/shard_map/ppermute | solution.py:27
  52.3 2.5 %collective-permute-start.6 = (bf16[64,6144]{1,0:T(8,128)(2,1)}, bf16[64,6144]{1,0:T(8,128)(2,1)S(1)}, u32[]{:S(2)}, u32[]{:S(2)}) collective-permute-start(bf16[64,6144]{1,0:T(8,128)(2,1)} %collective-permute-done.5), channel_id=1, source_target_pairs={{0,1},{1,0},{2,3},{3,2},{4,5},{5,4},{6,7},{7,6},{8,9},{9,8},{10,11... | collective-permute-start | bytes 2359304 | tf_op jit(solution)/shard_map/ppermute | solution.py:30
  52.3 24.1 %copy-start.6 = (f32[1,3072]{1,0:T(1,128)S(1)}, f32[1,3072]{1,0:T(1,128)}, u32[]{:S(2)}) copy-start(f32[1,3072]{1,0:T(1,128)} %param.11) | copy-start | bytes 36868
  52.3 22.6 %collective-permute-start.10 = (bf16[128,3072]{1,0:T(8,128)(2,1)S(1)}, bf16[128,3072]{1,0:T(8,128)(2,1)S(1)}, u32[]{:S(2)}, u32[]{:S(2)}) collective-permute-start(bf16[128,3072]{1,0:T(8,128)(2,1)S(1)} %get-tuple-element.45), channel_id=1, source_target_pairs={{0,8},{8,0},{1,9},{9,1},{2,10},{10,2},{3,11},{11,3},{4,12},{12,4},... | collective-permute-start | bytes 2359304 | tf_op jit(solution)/shard_map/ppermute | solution.py:36
  55.7 45.7 %collective-permute-start.8 = (bf16[64,6144]{1,0:T(8,128)(2,1)}, bf16[64,6144]{1,0:T(8,128)(2,1)}, u32[]{:S(2)}, u32[]{:S(2)}) collective-permute-start(bf16[64,6144]{1,0:T(8,128)(2,1)} %collective-permute-done.5), channel_id=1, source_target_pairs={{0,4},{1,5},{4,6},{5,7},{6,2},{7,3},{2,0},{3,1},{8,12},{9,13},{12,... | collective-permute-start | bytes 2359304 | tf_op jit(solution)/shard_map/ppermute | solution.py:27
  74.9 22.5 %collective-permute-start.11 = (bf16[128,3072]{1,0:T(8,128)(2,1)}, bf16[128,3072]{1,0:T(8,128)(2,1)}, u32[]{:S(2)}, u32[]{:S(2)}) collective-permute-start(bf16[128,3072]{1,0:T(8,128)(2,1)} %get-tuple-element.49), channel_id=1, source_target_pairs={{0,8},{8,0},{1,9},{9,1},{2,10},{10,2},{3,11},{11,3},{4,12},{12,4},... | collective-permute-start | bytes 2359304 | tf_op jit(solution)/shard_map/ppermute | solution.py:36
  97.4 8.1 %copy-start = (f32[256,6144]{1,0:T(8,128)S(1)}, f32[256,6144]{1,0:T(8,128)}, u32[]{:S(2)}) copy-start(f32[256,6144]{1,0:T(8,128)} %fusion.4) | copy-start | bytes 18874372
  100.9 2.4 %collective-permute-start.12 = (bf16[64,6144]{1,0:T(8,128)(2,1)S(1)}, bf16[64,6144]{1,0:T(8,128)(2,1)S(1)}, u32[]{:S(2)}, u32[]{:S(2)}) collective-permute-start(bf16[64,6144]{1,0:T(8,128)(2,1)S(1)} %get-tuple-element.41), channel_id=1, source_target_pairs={{0,1},{1,0},{2,3},{3,2},{4,5},{5,4},{6,7},{7,6},{8,9},{9,8},{10,11... | collective-permute-start | bytes 2359304 | tf_op jit(solution)/shard_map/ppermute | solution.py:30
  100.9 4.5 %collective-permute-start.15 = (bf16[64,6144]{1,0:T(8,128)(2,1)S(1)}, bf16[64,6144]{1,0:T(8,128)(2,1)S(1)}, u32[]{:S(2)}, u32[]{:S(2)}) collective-permute-start(bf16[64,6144]{1,0:T(8,128)(2,1)S(1)} %get-tuple-element.42), channel_id=1, source_target_pairs={{0,1},{1,0},{2,3},{3,2},{4,5},{5,4},{6,7},{7,6},{8,9},{9,8},{10,11... | collective-permute-start | bytes 2359304 | tf_op jit(solution)/shard_map/ppermute | solution.py:30
  101.4 5.5 %collective-permute-start.9 = (bf16[64,6144]{1,0:T(8,128)(2,1)}, bf16[64,6144]{1,0:T(8,128)(2,1)S(1)}, u32[]{:S(2)}, u32[]{:S(2)}) collective-permute-start(bf16[64,6144]{1,0:T(8,128)(2,1)} %collective-permute-done.8), channel_id=1, source_target_pairs={{0,1},{1,0},{2,3},{3,2},{4,5},{5,4},{6,7},{7,6},{8,9},{9,8},{10,11... | collective-permute-start | bytes 2359304 | tf_op jit(solution)/shard_map/ppermute | solution.py:30
  105.8 19.9 %collective-permute-start.14 = (bf16[64,6144]{1,0:T(8,128)(2,1)S(1)}, bf16[64,6144]{1,0:T(8,128)(2,1)S(1)}, u32[]{:S(2)}, u32[]{:S(2)}) collective-permute-start(bf16[64,6144]{1,0:T(8,128)(2,1)S(1)} %get-tuple-element.39), channel_id=1, source_target_pairs={{0,4},{1,5},{4,6},{5,7},{6,2},{7,3},{2,0},{3,1},{8,12},{9,13},{12,... | collective-permute-start | bytes 2359304 | tf_op jit(solution)/shard_map/ppermute | solution.py:27
  107.9 19.3 %collective-permute-start.16 = (bf16[64,6144]{1,0:T(8,128)(2,1)S(1)}, bf16[64,6144]{1,0:T(8,128)(2,1)S(1)}, u32[]{:S(2)}, u32[]{:S(2)}) collective-permute-start(bf16[64,6144]{1,0:T(8,128)(2,1)S(1)} %get-tuple-element.40), channel_id=1, source_target_pairs={{0,16},{16,0},{1,17},{17,1},{2,18},{18,2},{3,19},{19,3},{4,20},{20... | collective-permute-start | bytes 2359304 | tf_op jit(solution)/shard_map/ppermute | solution.py:101
  124.1 19.3 %collective-permute-start.13 = (bf16[128,3072]{1,0:T(8,128)(2,1)}, bf16[128,3072]{1,0:T(8,128)(2,1)}, u32[]{:S(2)}, u32[]{:S(2)}) collective-permute-start(bf16[128,3072]{1,0:T(8,128)(2,1)} %get-tuple-element.51), channel_id=1, source_target_pairs={{0,8},{8,0},{1,9},{9,1},{2,10},{10,2},{3,11},{11,3},{4,12},{12,4},... | collective-permute-start | bytes 2359304 | tf_op jit(solution)/shard_map/ppermute | solution.py:36
  143.5 2.4 %collective-permute-start.17 = (bf16[64,6144]{1,0:T(8,128)(2,1)S(1)}, bf16[64,6144]{1,0:T(8,128)(2,1)S(1)}, u32[]{:S(2)}, u32[]{:S(2)}) collective-permute-start(bf16[64,6144]{1,0:T(8,128)(2,1)S(1)} %slice.47), channel_id=1, source_target_pairs={{0,1},{1,0},{2,3},{3,2},{4,5},{5,4},{6,7},{7,6},{8,9},{9,8},{10,11... | collective-permute-start | bytes 2359304 | tf_op jit(solution)/shard_map/ppermute | solution.py:30
  146.1 19.6 %collective-permute-start.18 = (bf16[64,6144]{1,0:T(8,128)(2,1)S(1)}, bf16[64,6144]{1,0:T(8,128)(2,1)S(1)}, u32[]{:S(2)}, u32[]{:S(2)}) collective-permute-start(bf16[64,6144]{1,0:T(8,128)(2,1)S(1)} %add_convert_fusion.2), channel_id=1, source_target_pairs={{0,4},{1,5},{4,6},{5,7},{6,2},{7,3},{2,0},{3,1},{8,12},{9,13},{12,... | collective-permute-start | bytes 2359304 | tf_op jit(solution)/shard_map/ppermute | solution.py:27
  165.9 2.4 %collective-permute-start.19 = (bf16[64,6144]{1,0:T(8,128)(2,1)S(1)}, bf16[64,6144]{1,0:T(8,128)(2,1)S(1)}, u32[]{:S(2)}, u32[]{:S(2)}) collective-permute-start(bf16[64,6144]{1,0:T(8,128)(2,1)S(1)} %slice.46), channel_id=1, source_target_pairs={{0,1},{1,0},{2,3},{3,2},{4,5},{5,4},{6,7},{7,6},{8,9},{9,8},{10,11... | collective-permute-start | bytes 2359304 | tf_op jit(solution)/shard_map/ppermute | solution.py:30
  168.4 20.9 %collective-permute-start.20 = (bf16[64,6144]{1,0:T(8,128)(2,1)S(1)}, bf16[64,6144]{1,0:T(8,128)(2,1)S(1)}, u32[]{:S(2)}, u32[]{:S(2)}) collective-permute-start(bf16[64,6144]{1,0:T(8,128)(2,1)S(1)} %add_convert_fusion.1), channel_id=1, source_target_pairs={{0,20},{1,21},{4,22},{5,23},{6,18},{7,19},{2,16},{3,17},{16,4},{17... | collective-permute-start | bytes 2359304 | tf_op jit(solution)/shard_map/ppermute | solution.py:81
  (5 other events, 11.7 us)

commit v4 on v3

--- a/solution.py
+++ b/solution.py
@@ -64,7 +64,7 @@
             pre = jnp.dot(both, up_weight[0], preferred_element_type=F32)
             other = from_others(pre.astype(BF16))
             if coming is not None:
-                coming = tie(coming, pre)
+                coming = tie(coming, (pre, pres[0][1]) if k == 1 else pre)
                 blocks.append((coming, sibling(coming)))
             pres.append((pre, other))
             return pre
@@ -81,34 +81,35 @@
             return lax.ppermute(value, ("section", "tensor"), along_and_turn)
 
         up(0)
-        residual = lax.ppermute(incoming[0], "section", turn)
+        residual = lax.ppermute(tie(incoming[0], pres[0][0]), "section", turn)
         for k in range(1, chips):
             if k == 1:
-                blocks[1] = tie(blocks[1], residual)
                 up(1)
-                done = (pres[1][0], pres[0][1])
+                done = (pres[1][0], pres[0][1], residual)
                 if chips > 2:
                     blocks[2] = tie(blocks[2], done)
                     done = up(2)
                 both = jnp.concatenate([act(1, done), act(0, None)], axis=0)
                 part = jnp.dot(both, down_weight[0], preferred_element_type=F32)
+                theirs = part[rows : 2 * rows].astype(BF16)
                 if chips > 2:
-                    part = tie(part, pres[2][1])
-                got = sibling(part[rows : 2 * rows].astype(BF16))
-                summed = (part[:rows] + got.astype(F32)).astype(BF16)
+                    theirs = tie(theirs, pres[2][1])
+                summed = (part[:rows] + sibling(theirs).astype(F32)).astype(BF16)
                 running = send(1, summed)
-                own = part[2 * rows : 3 * rows] + sibling(part[3 * rows :].astype(BF16)).astype(F32)
+                theirs = tie(part[3 * rows :].astype(BF16), summed)
+                own = part[2 * rows : 3 * rows] + sibling(theirs).astype(F32)
                 own = lax.ppermute((own + down_bias[0]).astype(BF16), "section", turn)
                 continue
             if k + 1 < chips:
                 blocks[k + 1] = tie(blocks[k + 1], summed)
-                done = (up(k + 1), running, own)
+                done = (up(k + 1), running)
             else:
                 done = summed
             part = jnp.dot(act(k, done), down_weight[0], preferred_element_type=F32)
-            part = tie(part, pres[k + 1][1] if k + 1 < chips else running)
-            got = sibling(part[rows:].astype(BF16))
-            summed = (part[:rows] + got.astype(F32) + running.astype(F32)).astype(BF16)
+            theirs = part[rows:].astype(BF16)
+            theirs = tie(theirs, pres[k + 1][1] if k + 1 < chips else (running, own))
+            summed = part[:rows] + sibling(theirs).astype(F32) + running.astype(F32)
+            summed = summed.astype(BF16)
             running = send(k, summed)
         result = running.astype(F32) + own.astype(F32) + residual.astype(F32)
         return result.astype(BF16)[None]

time: 191 us -> 187 us (0.979)
  waiting for transfers between devices: 42.6 us -> 38.4 us
  starting transfers between devices: 26.1 us -> 23.4 us
    ppermute x8, waiting for transfers between devices: 10.3 us -> 5.29 us  [sibling(): return lax.ppermute(block, 'tensor', swap)]
    convert_element_type x3 -> x4, other arithmetic: 0.85 us -> 4.87 us  [the longest x1 1.87 us: per_device(): own = lax.ppermute((own + down_bias[0]).astype(BF16), 'section', turn)]
    another operation x1 -> x0, other arithmetic: 3.37 us -> none  [run(): jax.shard_map(body, mesh=mesh, in_specs=placed, out_specs=P('section', 't...]
    ppermute x5, waiting for transfers between devices: 2.82 us -> 5.96 us  [from_others(): got = lax.ppermute(sent, 'dp', route)]
    ppermute x5, waiting for transfers between devices: 10 us -> 7.59 us  [forward(): return lax.ppermute(block, 'tensor', along)]
    ppermute x5, starting transfers between devices: 11.7 us -> 9.72 us  [forward(): return lax.ppermute(block, 'tensor', along)]
  transfers between devices with their start and end apart: 21 -> 21, of which waited for: 14 -> 12; matrix products, arithmetic and copies ran while one was open for 60% -> 64% of each run, Pallas kernels for 0% -> 0%
where the time goes in v4:
time: 187 us
  matrix products  110 us (59%)
  waiting for transfers between devices  38.4 us (21%)
  starting transfers between devices  23.4 us (13%)
  other arithmetic  11.6 us (6%)
  local copies, waits for them, and re-layouts  3.48 us (2%)
    dot_general x4, matrix products, up(): pre = jnp.dot(both, up_weight[0], preferred_element_type=F32)  60.4 us
    dot_general x2, matrix products, per_device(): part = jnp.dot(act(k, done), down_weight[0], preferred_element_type=F32)  30 us
    dot_general x1, matrix products, per_device(): part = jnp.dot(both, down_weight[0], preferred_element_type=F32)  19.5 us
    ppermute x1, waiting for transfers between devices, send(): return lax.ppermute(value, ('section', 'tensor'), along_and_turn)  18 us
    ppermute x5, starting transfers between devices, forward(): return lax.ppermute(block, 'tensor', along)  9.72 us
    ppermute x5, starting transfers between devices, from_others(): got = lax.ppermute(sent, 'dp', route)  8.01 us
    ppermute x5, waiting for transfers between devices, forward(): return lax.ppermute(block, 'tensor', along)  7.59 us
    ppermute x5, waiting for transfers between devices, from_others(): got = lax.ppermute(sent, 'dp', route)  5.96 us
  transfers between devices with their start and end apart: 21, of which 12 were waited for; matrix products, arithmetic and copies ran while one was open for 64% of the time, Pallas kernels for 0%

profile of v4, /device:TPU:0, one launch (start us, length us, event | category | flops | bytes accessed | tf_op | source)
XLA Modules:
  0.0 186.9 jit_solution(18153512998831042603)
XLA Ops:
  1.5 3.0 %collective-permute-start = (f32[2,64]{1,0:T(2,128)S(1)}, f32[2,64]{1,0:T(2,128)S(1)}, u32[]{:S(2)}, u32[]{:S(2)}) collective-permute-start(f32[2,64]{1,0:T(2,128)S(1)} %pad_maximum_fusion), channel_id=1, source_target_pairs={{0,8},{8,0},{1,9},{9,1},{2,10},{10,2},{3,11},{11,3},{4,12},{12,4},... | collective-permute-start | bytes 1544 | tf_op jit(solution)/shard_map/ppermute | solution.py:36
  4.5 1.5 collective-permute-done
  7.7 3.2 %collective-permute-start.1 = (bf16[64,6144]{1,0:T(8,128)(2,1)S(1)}, bf16[64,6144]{1,0:T(8,128)(2,1)S(1)}, u32[]{:S(2)}, u32[]{:S(2)}) collective-permute-start(bf16[64,6144]{1,0:T(8,128)(2,1)S(1)} %fusion.17), channel_id=1, source_target_pairs={{0,4},{1,5},{4,6},{5,7},{6,2},{7,3},{2,0},{3,1},{8,12},{9,13},{12,... | collective-permute-start | bytes 2359304 | tf_op jit(solution)/shard_map/ppermute | solution.py:27
  10.8 14.4 %fusion.103 = (bf16[128,3072]{1,0:T(8,128)(2,1)S(1)}, f32[128,3072]{1,0:T(8,128)S(1)}) fusion(bf16[1,6144,3072]{2,1,0:T(8,128)(2,1)} %param.10, bf16[64,6144]{1,0:T(8,128)(2,1)S(1)} %collective-permute-done.2, bf16[64,6144]{1,0:T(8,128)(2,1)S(1)} %fusion.17), kind=kOutput, calls=%fused_computation.117 | convolution fusion | flops 4835377152 | bytes 41680896 | tf_op jit(solution)/shard_map/dot_general | solution.py:64
  25.2 3.0 %collective-permute-done.1 = bf16[64,6144]{1,0:T(8,128)(2,1)S(1)} collective-permute-done((bf16[64,6144]{1,0:T(8,128)(2,1)S(1)}, bf16[64,6144]{1,0:T(8,128)(2,1)S(1)}, u32[]{:S(2)}, u32[]{:S(2)}) %collective-permute-start.1) | collective-permute-done | bytes 786464 | tf_op jit(solution)/shard_map/ppermute | solution.py:27
  28.3 3.4 %collective-permute-start.3 = (bf16[64,6144]{1,0:T(8,128)(2,1)S(1)}, bf16[64,6144]{1,0:T(8,128)(2,1)}, u32[]{:S(2)}, u32[]{:S(2)}) collective-permute-start(bf16[64,6144]{1,0:T(8,128)(2,1)S(1)} %collective-permute-done.1), channel_id=1, source_target_pairs={{0,4},{1,5},{4,6},{5,7},{6,2},{7,3},{2,0},{3,1},{8,12},{9,13},{12,... | collective-permute-start | bytes 2359304 | tf_op jit(solution)/shard_map/ppermute | solution.py:27
  31.6 1.5 collective-permute-start.7
  34.7 14.9 %fusion.102 = (bf16[128,3072]{1,0:T(8,128)(2,1)}, f32[128,3072]{1,0:T(8,128)S(1)}) fusion(bf16[1,6144,3072]{2,1,0:T(8,128)(2,1)} %param.10, bf16[64,6144]{1,0:T(8,128)(2,1)S(1)} %collective-permute-done.4, bf16[64,6144]{1,0:T(8,128)(2,1)S(1)} %collective-permute-done.1), kind=kOutput, calls=%fused_computation.116 | convolution fusion | flops 4835377152 | bytes 41680896 | tf_op jit(solution)/shard_map/dot_general | solution.py:64
  49.5 3.0 %collective-permute-done.5 = bf16[128,3072]{1,0:T(8,128)(2,1)S(1)} collective-permute-done((bf16[128,3072]{1,0:T(8,128)(2,1)S(1)}, bf16[128,3072]{1,0:T(8,128)(2,1)S(1)}, u32[]{:S(2)}, u32[]{:S(2)}) %collective-permute-start.5) | collective-permute-done | bytes 786464 | tf_op jit(solution)/shard_map/ppermute | solution.py:36
  56.6 15.7 %fusion.105 = (bf16[128,3072]{1,0:T(8,128)(2,1)}, f32[128,3072]{1,0:T(8,128)S(1)}) fusion(bf16[1,6144,3072]{2,1,0:T(8,128)(2,1)} %param.10, bf16[64,6144]{1,0:T(8,128)(2,1)} %copy-done.3, bf16[64,6144]{1,0:T(8,128)(2,1)} %collective-permute-done.3), kind=kOutput, calls=%fused_computation.119 | convolution fusion | flops 4835377152 | bytes 41680896 | tf_op jit(solution)/shard_map/dot_general | solution.py:64
  74.2 2.5 %fusion.25 = (bf16[128,3072]{1,0:T(8,128)(2,1)}, bf16[128,3072]{1,0:T(8,128)(2,1)}) fusion(f32[128,3072]{1,0:T(8,128)S(1)} %get-tuple-element.44, bf16[128,3072]{1,0:T(8,128)(2,1)S(1)} %collective-permute-done.10, f32[3072]{0:T(1024)S(1)} %bitcast.48, f32[128,3072]{1,0:T(8,128)S(1)} %get-tuple-element.46, bf16[128,3072]{1,0:T(8,128)(2,1)S(1)} %collective-permute-done.5), kind=kLoop, calls=%fused_computation.31 | loop fusion | flops 9437184 | bytes 6303744 | tf_op jit(solution)/shard_map/convert_element_type | solution.py:76
  76.7 19.5 %fusion.104 = (bf16[256,6144]{1,0:T(8,128)(2,1)}, f32[256,6144]{1,0:T(8,128)}) fusion(bf16[1,3072,6144]{2,1,0:T(8,128)(2,1)} %param.12, bf16[128,3072]{1,0:T(8,128)(2,1)} %get-tuple-element.42, bf16[128,3072]{1,0:T(8,128)(2,1)} %get-tuple-element.41), kind=kOutput, calls=%fused_computation.118 | convolution fusion | flops 9668395008 | bytes 48758784 | tf_op jit(solution)/shard_map/dot_general | solution.py:93
  98.4 2.0 %collective-permute-done.12 = bf16[64,6144]{1,0:T(8,128)(2,1)S(1)} collective-permute-done((bf16[64,6144]{1,0:T(8,128)(2,1)S(1)}, bf16[64,6144]{1,0:T(8,128)(2,1)S(1)}, u32[]{:S(2)}, u32[]{:S(2)}) %collective-permute-start.12) | collective-permute-done | bytes 786464 | tf_op jit(solution)/shard_map/ppermute | solution.py:30
  100.4 1.6 fusion.56
  103.1 15.5 %fusion.106 = (bf16[128,3072]{1,0:T(8,128)(2,1)}, f32[128,3072]{1,0:T(8,128)S(1)}) fusion(bf16[1,6144,3072]{2,1,0:T(8,128)(2,1)} %param.10, bf16[64,6144]{1,0:T(8,128)(2,1)S(1)} %collective-permute-done.9, bf16[64,6144]{1,0:T(8,128)(2,1)} %collective-permute-done.8), kind=kOutput, calls=%fused_computation.120 | convolution fusion | flops 4835377152 | bytes 41680896 | tf_op jit(solution)/shard_map/dot_general | solution.py:64
  119.1 2.7 %collective-permute-done.14 = bf16[64,6144]{1,0:T(8,128)(2,1)S(1)} collective-permute-done((bf16[64,6144]{1,0:T(8,128)(2,1)S(1)}, bf16[64,6144]{1,0:T(8,128)(2,1)S(1)}, u32[]{:S(2)}, u32[]{:S(2)}) %collective-permute-start.14) | collective-permute-done | bytes 786464 | tf_op jit(solution)/shard_map/ppermute | solution.py:27
  122.7 15.0 %fusion.2 = f32[128,6144]{1,0:T(8,128)S(1)} fusion(bf16[1,3072,6144]{2,1,0:T(8,128)(2,1)} %param.12, f32[128,3072]{1,0:T(8,128)S(1)} %get-tuple-element.50, bf16[128,3072]{1,0:T(8,128)(2,1)} %collective-permute-done.11, f32[3072]{0:T(1024)S(1)} %bitcast.49), kind=kOutput, calls=%fused_computation.2 | convolution fusion | flops 4836556800 | bytes 43266048 | tf_op jit(solution)/shard_map/dot_general | solution.py:108
  138.8 1.9 %fusion.51 = bf16[64,6144]{1,0:T(8,128)(2,1)S(1)} fusion(f32[256,6144]{1,0:T(8,128)} %get-tuple-element.48, bf16[64,6144]{1,0:T(8,128)(2,1)} %collective-permute-done.17, f32[6144]{0:T(1024)S(1)} %bitcast.51), kind=kLoop, calls=%fused_computation.58 | loop fusion | flops 1572864 | bytes 3170304 | tf_op jit(solution)/shard_map/convert_element_type | solution.py:101
  144.0 15.0 %fusion = f32[128,6144]{1,0:T(8,128)S(1)} fusion(bf16[1,3072,6144]{2,1,0:T(8,128)(2,1)} %param.12, f32[128,3072]{1,0:T(8,128)S(1)} %get-tuple-element.52, bf16[128,3072]{1,0:T(8,128)(2,1)} %collective-permute-done.13, f32[3072]{0:T(1024)S(1)} %bitcast.50), kind=kOutput, calls=%fused_computation | convolution fusion | flops 4836556800 | bytes 43266048 | tf_op jit(solution)/shard_map/dot_general | solution.py:108
  159.1 1.6 collective-permute-done.18
  160.7 1.8 collective-permute-done.16
  162.5 2.3 %collective-permute-done.19 = bf16[64,6144]{1,0:T(8,128)(2,1)S(1)} collective-permute-done((bf16[64,6144]{1,0:T(8,128)(2,1)S(1)}, bf16[64,6144]{1,0:T(8,128)(2,1)S(1)}, u32[]{:S(2)}, u32[]{:S(2)}) %collective-permute-start.19) | collective-permute-done | bytes 786464 | tf_op jit(solution)/shard_map/ppermute | solution.py:30
  165.1 2.8 %collective-permute-start.20 = (bf16[64,6144]{1,0:T(8,128)(2,1)S(1)}, bf16[64,6144]{1,0:T(8,128)(2,1)S(1)}, u32[]{:S(2)}, u32[]{:S(2)}) collective-permute-start(bf16[64,6144]{1,0:T(8,128)(2,1)S(1)} %fusion.53), channel_id=1, source_target_pairs={{0,20},{1,21},{4,22},{5,23},{6,18},{7,19},{2,16},{3,17},{16,4},{17... | collective-permute-start | bytes 2359304 | tf_op jit(solution)/shard_map/ppermute | solution.py:81
  167.8 18.0 %collective-permute-done.20 = bf16[64,6144]{1,0:T(8,128)(2,1)S(1)} collective-permute-done((bf16[64,6144]{1,0:T(8,128)(2,1)S(1)}, bf16[64,6144]{1,0:T(8,128)(2,1)S(1)}, u32[]{:S(2)}, u32[]{:S(2)}) %collective-permute-start.20) | collective-permute-done | bytes 786464 | tf_op jit(solution)/shard_map/ppermute | solution.py:81
  (52 shorter events, 21.1 us)
Async XLA Ops:
  1.5 4.5 %collective-permute-start = (f32[2,64]{1,0:T(2,128)S(1)}, f32[2,64]{1,0:T(2,128)S(1)}, u32[]{:S(2)}, u32[]{:S(2)}) collective-permute-start(f32[2,64]{1,0:T(2,128)S(1)} %pad_maximum_fusion), channel_id=1, source_target_pairs={{0,8},{8,0},{1,9},{9,1},{2,10},{10,2},{3,11},{11,3},{4,12},{12,4},... | collective-permute-start | bytes 1544 | tf_op jit(solution)/shard_map/ppermute | solution.py:36
  7.6 24.1 %copy-start = (bf16[1,64,6144]{2,1,0:T(8,128)(2,1)S(1)}, bf16[1,64,6144]{2,1,0:T(8,128)(2,1)}, u32[]{:S(2)}) copy-start(bf16[1,64,6144]{2,1,0:T(8,128)(2,1)} %param.7) | copy-start | bytes 2359300
  7.6 3.3 %collective-permute-start.2 = (bf16[64,6144]{1,0:T(8,128)(2,1)S(1)}, bf16[64,6144]{1,0:T(8,128)(2,1)S(1)}, u32[]{:S(2)}, u32[]{:S(2)}) collective-permute-start(bf16[64,6144]{1,0:T(8,128)(2,1)S(1)} %fusion.17), channel_id=1, source_target_pairs={{0,1},{1,0},{2,3},{3,2},{4,5},{5,4},{6,7},{7,6},{8,9},{9,8},{10,11... | collective-permute-start | bytes 2359304 | tf_op jit(solution)/shard_map/ppermute | solution.py:30
  7.7 20.6 %collective-permute-start.1 = (bf16[64,6144]{1,0:T(8,128)(2,1)S(1)}, bf16[64,6144]{1,0:T(8,128)(2,1)S(1)}, u32[]{:S(2)}, u32[]{:S(2)}) collective-permute-start(bf16[64,6144]{1,0:T(8,128)(2,1)S(1)} %fusion.17), channel_id=1, source_target_pairs={{0,4},{1,5},{4,6},{5,7},{6,2},{7,3},{2,0},{3,1},{8,12},{9,13},{12,... | collective-permute-start | bytes 2359304 | tf_op jit(solution)/shard_map/ppermute | solution.py:27
  28.3 6.4 %collective-permute-start.4 = (bf16[64,6144]{1,0:T(8,128)(2,1)S(1)}, bf16[64,6144]{1,0:T(8,128)(2,1)S(1)}, u32[]{:S(2)}, u32[]{:S(2)}) collective-permute-start(bf16[64,6144]{1,0:T(8,128)(2,1)S(1)} %collective-permute-done.1), channel_id=1, source_target_pairs={{0,1},{1,0},{2,3},{3,2},{4,5},{5,4},{6,7},{7,6},{8,9},{9,8},{10,11... | collective-permute-start | bytes 2359304 | tf_op jit(solution)/shard_map/ppermute | solution.py:30
  28.3 21.3 %collective-permute-start.3 = (bf16[64,6144]{1,0:T(8,128)(2,1)S(1)}, bf16[64,6144]{1,0:T(8,128)(2,1)}, u32[]{:S(2)}, u32[]{:S(2)}) collective-permute-start(bf16[64,6144]{1,0:T(8,128)(2,1)S(1)} %collective-permute-done.1), channel_id=1, source_target_pairs={{0,4},{1,5},{4,6},{5,7},{6,2},{7,3},{2,0},{3,1},{8,12},{9,13},{12,... | collective-permute-start | bytes 2359304 | tf_op jit(solution)/shard_map/ppermute | solution.py:27
  31.6 22.4 %collective-permute-start.7 = (bf16[64,6144]{1,0:T(8,128)(2,1)S(1)}, bf16[64,6144]{1,0:T(8,128)(2,1)S(1)}, u32[]{:S(2)}, u32[]{:S(2)}) collective-permute-start(bf16[64,6144]{1,0:T(8,128)(2,1)S(1)} %bitcast.47), channel_id=1, source_target_pairs={{0,16},{16,0},{1,17},{17,1},{2,18},{18,2},{3,19},{19,3},{4,20},{20... | collective-permute-start | bytes 2359304 | tf_op jit(solution)/shard_map/ppermute | solution.py:84
  33.2 19.4 %collective-permute-start.5 = (bf16[128,3072]{1,0:T(8,128)(2,1)S(1)}, bf16[128,3072]{1,0:T(8,128)(2,1)S(1)}, u32[]{:S(2)}, u32[]{:S(2)}) collective-permute-start(bf16[128,3072]{1,0:T(8,128)(2,1)S(1)} %get-tuple-element.45), channel_id=1, source_target_pairs={{0,8},{8,0},{1,9},{9,1},{2,10},{10,2},{3,11},{11,3},{4,12},{12,4},... | collective-permute-start | bytes 2359304 | tf_op jit(solution)/shard_map/ppermute | solution.py:36
  52.6 2.5 %collective-permute-start.6 = (bf16[64,6144]{1,0:T(8,128)(2,1)}, bf16[64,6144]{1,0:T(8,128)(2,1)S(1)}, u32[]{:S(2)}, u32[]{:S(2)}) collective-permute-start(bf16[64,6144]{1,0:T(8,128)(2,1)} %collective-permute-done.3), channel_id=1, source_target_pairs={{0,1},{1,0},{2,3},{3,2},{4,5},{5,4},{6,7},{7,6},{8,9},{9,8},{10,11... | collective-permute-start | bytes 2359304 | tf_op jit(solution)/shard_map/ppermute | solution.py:30
  52.6 21.7 %copy-start.4 = (f32[1,3072]{1,0:T(1,128)S(1)}, f32[1,3072]{1,0:T(1,128)}, u32[]{:S(2)}) copy-start(f32[1,3072]{1,0:T(1,128)} %param.11) | copy-start | bytes 36868
  52.6 20.2 %collective-permute-start.10 = (bf16[128,3072]{1,0:T(8,128)(2,1)}, bf16[128,3072]{1,0:T(8,128)(2,1)S(1)}, u32[]{:S(2)}, u32[]{:S(2)}) collective-permute-start(bf16[128,3072]{1,0:T(8,128)(2,1)} %get-tuple-element.43), channel_id=1, source_target_pairs={{0,8},{8,0},{1,9},{9,1},{2,10},{10,2},{3,11},{11,3},{4,12},{12,4},... | collective-permute-start | bytes 2359304 | tf_op jit(solution)/shard_map/ppermute | solution.py:36
  55.9 41.9 %collective-permute-start.8 = (bf16[64,6144]{1,0:T(8,128)(2,1)}, bf16[64,6144]{1,0:T(8,128)(2,1)}, u32[]{:S(2)}, u32[]{:S(2)}) collective-permute-start(bf16[64,6144]{1,0:T(8,128)(2,1)} %collective-permute-done.3), channel_id=1, source_target_pairs={{0,4},{1,5},{4,6},{5,7},{6,2},{7,3},{2,0},{3,1},{8,12},{9,13},{12,... | collective-permute-start | bytes 2359304 | tf_op jit(solution)/shard_map/ppermute | solution.py:27
  72.7 25.0 %collective-permute-start.11 = (bf16[128,3072]{1,0:T(8,128)(2,1)}, bf16[128,3072]{1,0:T(8,128)(2,1)}, u32[]{:S(2)}, u32[]{:S(2)}) collective-permute-start(bf16[128,3072]{1,0:T(8,128)(2,1)} %get-tuple-element.49), channel_id=1, source_target_pairs={{0,8},{8,0},{1,9},{9,1},{2,10},{10,2},{3,11},{11,3},{4,12},{12,4},... | collective-permute-start | bytes 2359304 | tf_op jit(solution)/shard_map/ppermute | solution.py:36
  97.8 2.6 %collective-permute-start.12 = (bf16[64,6144]{1,0:T(8,128)(2,1)S(1)}, bf16[64,6144]{1,0:T(8,128)(2,1)S(1)}, u32[]{:S(2)}, u32[]{:S(2)}) collective-permute-start(bf16[64,6144]{1,0:T(8,128)(2,1)S(1)} %get-tuple-element.31), channel_id=1, source_target_pairs={{0,1},{1,0},{2,3},{3,2},{4,5},{5,4},{6,7},{7,6},{8,9},{9,8},{10,11... | collective-permute-start | bytes 2359304 | tf_op jit(solution)/shard_map/ppermute | solution.py:30
  97.9 5.2 %collective-permute-start.9 = (bf16[64,6144]{1,0:T(8,128)(2,1)}, bf16[64,6144]{1,0:T(8,128)(2,1)S(1)}, u32[]{:S(2)}, u32[]{:S(2)}) collective-permute-start(bf16[64,6144]{1,0:T(8,128)(2,1)} %collective-permute-done.8), channel_id=1, source_target_pairs={{0,1},{1,0},{2,3},{3,2},{4,5},{5,4},{6,7},{7,6},{8,9},{9,8},{10,11... | collective-permute-start | bytes 2359304 | tf_op jit(solution)/shard_map/ppermute | solution.py:30
  101.9 19.9 %collective-permute-start.14 = (bf16[64,6144]{1,0:T(8,128)(2,1)S(1)}, bf16[64,6144]{1,0:T(8,128)(2,1)S(1)}, u32[]{:S(2)}, u32[]{:S(2)}) collective-permute-start(bf16[64,6144]{1,0:T(8,128)(2,1)S(1)} %fusion.56), channel_id=1, source_target_pairs={{0,4},{1,5},{4,6},{5,7},{6,2},{7,3},{2,0},{3,1},{8,12},{9,13},{12,... | collective-permute-start | bytes 2359304 | tf_op jit(solution)/shard_map/ppermute | solution.py:27
  103.1 35.7 %collective-permute-start.17 = (bf16[64,6144]{1,0:T(8,128)(2,1)S(1)}, bf16[64,6144]{1,0:T(8,128)(2,1)}, u32[]{:S(2)}, u32[]{:S(2)}) collective-permute-start(bf16[64,6144]{1,0:T(8,128)(2,1)S(1)} %get-tuple-element.37), channel_id=1, source_target_pairs={{0,1},{1,0},{2,3},{3,2},{4,5},{5,4},{6,7},{7,6},{8,9},{9,8},{10,11... | collective-permute-start | bytes 2359304 | tf_op jit(solution)/shard_map/ppermute | solution.py:30
  118.5 20.3 %collective-permute-start.13 = (bf16[128,3072]{1,0:T(8,128)(2,1)}, bf16[128,3072]{1,0:T(8,128)(2,1)}, u32[]{:S(2)}, u32[]{:S(2)}) collective-permute-start(bf16[128,3072]{1,0:T(8,128)(2,1)} %get-tuple-element.51), channel_id=1, source_target_pairs={{0,8},{8,0},{1,9},{9,1},{2,10},{10,2},{3,11},{11,3},{4,12},{12,4},... | collective-permute-start | bytes 2359304 | tf_op jit(solution)/shard_map/ppermute | solution.py:36
  138.8 2.7 %collective-permute-start.15 = (bf16[64,6144]{1,0:T(8,128)(2,1)S(1)}, bf16[64,6144]{1,0:T(8,128)(2,1)S(1)}, u32[]{:S(2)}, u32[]{:S(2)}) collective-permute-start(bf16[64,6144]{1,0:T(8,128)(2,1)S(1)} %slice.65), channel_id=1, source_target_pairs={{0,1},{1,0},{2,3},{3,2},{4,5},{5,4},{6,7},{7,6},{8,9},{9,8},{10,11... | collective-permute-start | bytes 2359304 | tf_op jit(solution)/shard_map/ppermute | solution.py:30
  138.8 2.7 %copy-start.2 = (bf16[64,6144]{1,0:T(8,128)(2,1)S(1)}, bf16[64,6144]{1,0:T(8,128)(2,1)}, u32[]{:S(2)}) copy-start(bf16[64,6144]{1,0:T(8,128)(2,1)} %copy-done.1) | copy-start | bytes 2359300
  140.7 20.0 %collective-permute-start.18 = (bf16[64,6144]{1,0:T(8,128)(2,1)S(1)}, bf16[64,6144]{1,0:T(8,128)(2,1)S(1)}, u32[]{:S(2)}, u32[]{:S(2)}) collective-permute-start(bf16[64,6144]{1,0:T(8,128)(2,1)S(1)} %fusion.51), channel_id=1, source_target_pairs={{0,16},{16,0},{1,17},{17,1},{2,18},{18,2},{3,19},{19,3},{4,20},{20... | collective-permute-start | bytes 2359304 | tf_op jit(solution)/shard_map/ppermute | solution.py:101
  142.6 19.9 %collective-permute-start.16 = (bf16[64,6144]{1,0:T(8,128)(2,1)}, bf16[64,6144]{1,0:T(8,128)(2,1)S(1)}, u32[]{:S(2)}, u32[]{:S(2)}) collective-permute-start(bf16[64,6144]{1,0:T(8,128)(2,1)} %fusion.55), channel_id=1, source_target_pairs={{0,4},{1,5},{4,6},{5,7},{6,2},{7,3},{2,0},{3,1},{8,12},{9,13},{12,... | collective-permute-start | bytes 2359304 | tf_op jit(solution)/shard_map/ppermute | solution.py:27
  162.5 2.3 %collective-permute-start.19 = (bf16[64,6144]{1,0:T(8,128)(2,1)S(1)}, bf16[64,6144]{1,0:T(8,128)(2,1)S(1)}, u32[]{:S(2)}, u32[]{:S(2)}) collective-permute-start(bf16[64,6144]{1,0:T(8,128)(2,1)S(1)} %slice.64), channel_id=1, source_target_pairs={{0,1},{1,0},{2,3},{3,2},{4,5},{5,4},{6,7},{7,6},{8,9},{9,8},{10,11... | collective-permute-start | bytes 2359304 | tf_op jit(solution)/shard_map/ppermute | solution.py:30
  165.1 20.7 %collective-permute-start.20 = (bf16[64,6144]{1,0:T(8,128)(2,1)S(1)}, bf16[64,6144]{1,0:T(8,128)(2,1)S(1)}, u32[]{:S(2)}, u32[]{:S(2)}) collective-permute-start(bf16[64,6144]{1,0:T(8,128)(2,1)S(1)} %fusion.53), channel_id=1, source_target_pairs={{0,20},{1,21},{4,22},{5,23},{6,18},{7,19},{2,16},{3,17},{16,4},{17... | collective-permute-start | bytes 2359304 | tf_op jit(solution)/shard_map/ppermute | solution.py:81
  (3 other events, 2.9 us)

commit v5 on v3

v5 whole, which is shorter than its diff:
```python
import jax
import jax.numpy as jnp
from jax import lax
from jax.sharding import PartitionSpec as P

F32 = jnp.float32
BF16 = jnp.bfloat16


def ring_order(n):
    return list(range(0, n, 2)) + list(range(1, n, 2))[::-1]


def make_per_device(width, n_section, n_dp, n_tensor):
    chips = n_tensor // 2
    order = ring_order(chips)
    ahead = chips // 2
    swap = [(i, i ^ 1) for i in range(n_tensor)]
    turn = [(i, (i + 1) % n_section) for i in range(n_section)]

    def hops(way):
        return [
            (order[i] * 2 + c, order[(i + way) % chips] * 2 + c)
            for i in range(chips)
            for c in range(2)
        ]

    def shift(block, way):
        return lax.ppermute(block, "tensor", hops(way))

    def shift_and_turn(block, way):
        route = [(s * n_tensor + a, t * n_tensor + b) for s, t in turn for a, b in hops(way)]
        return lax.ppermute(block, ("section", "tensor"), route)

    def sibling(block):
        return lax.ppermute(block, "tensor", swap)

    def from_others(sent):
        total = None
        for hop in range(1, n_dp):
            route = [(i, (i + hop) % n_dp) for i in range(n_dp)]
            got = lax.ppermute(sent, "dp", route)
            total = got if total is None else total.astype(F32) + got.astype(F32)
        return total

    def per_device(incoming, norm_gain, norm_shift, up_weight, up_bias, down_weight, down_bias):
        rows = incoming.shape[1]
        x = incoming[0].astype(F32)
        sums = jnp.stack(
            lax.reduce(
                (x, x * x), (F32(0), F32(0)), lambda a, b: (a[0] + b[0], a[1] + b[1]), (1,)
            )
        )
        total, square = sums + from_others(sums)
        mean = total / width
        var = square / width - mean * mean
        normed = (
            (x - mean[:, None]) * lax.rsqrt(var + 1e-05)[:, None] * norm_gain[0] + norm_shift[0]
        ).astype(BF16)

        pres = {}

        def tie(values, done):
            return lax.optimization_barrier((values, done))[0]

        def up(offset, block):
            both = jnp.concatenate([block, sibling(block)], axis=0)
            pre = jnp.dot(both, up_weight[0], preferred_element_type=F32)
            pres[offset] = (pre, from_others(pre.astype(BF16)))
            return pre

        def act(offset, done=None):
            pre, other = pres[offset]
            if done is not None:
                other = tie(other, done)
            return jax.nn.gelu(pre + other.astype(F32) + up_bias[0], approximate=True).astype(BF16)

        ups = [(chips - k, 1) for k in range(1, ahead + 1)]
        ups += [(k, -1) for k in range(1, chips - ahead)]
        done = up(0, normed)
        residual = lax.ppermute(tie(incoming[0], done), "section", turn)
        carried, before = {1: normed, -1: normed}, None
        for offset, way in ups:
            block = shift(carried[way], way)
            extra = () if before is None else (pres[before][1], residual)
            block = tie(block, (done, extra))
            carried[way] = block
            before = 0 if before is None else last
            last = offset
            done = up(offset, block)

        along = [(k, 1) for k in range(ahead, 0, -1)]
        against = [(chips - k, -1) for k in range(chips - ahead - 1, 0, -1)]
        downs = [along.pop(0)]
        while along or against:
            downs.append(against.pop(0) if against else along.pop(0))
            if along and len(downs) % 2 == 0:
                downs.append(along.pop(0))

        sums, arrived = {}, []
        own = sent = None
        for place, (offset, way) in enumerate(downs):
            active = act(offset, done)
            if place == 0:
                mine = act(0)
                active = jnp.concatenate(
                    [active[:rows], mine[:rows], active[rows:], mine[rows:]], axis=0
                )
            part = jnp.dot(active, down_weight[0], preferred_element_type=F32)
            half = part.shape[0] // 2
            theirs = part[half:].astype(BF16)
            if place:
                over = pres[downs[place + 1][0]][1] if place + 1 < len(downs) else ()
                theirs = tie(theirs, (sent, over, own))
            got = sibling(theirs)
            summed = part[:rows] + got[:rows].astype(F32)
            if way in sums:
                summed = summed + sums[way].astype(F32)
            summed = summed.astype(BF16)
            if offset == way % chips:
                sent = shift_and_turn(summed, way)
                arrived.append(sent)
            else:
                sent = sums[way] = shift(summed, way)
            done = summed
            if place == 0:
                own = (part[rows:half] + got[rows:].astype(F32) + down_bias[0]).astype(BF16)
                done = (summed, own)
                own = lax.ppermute(own, "section", turn)
        result = own.astype(F32) + residual.astype(F32)
        for value in arrived:
            result = result + value.astype(F32)
        return result.astype(BF16)[None]

    return per_device


def solution(mesh):
    placed = (
        P("section", "tensor", "dp"),
        P("section", "dp"),
        P("section", "dp"),
        P("section", "dp", "tensor"),
        P("section", "tensor"),
        P("section", "tensor", "dp"),
        P("section", "dp"),
    )

    def run(*args):
        body = make_per_device(
            args[0].shape[2], mesh.shape["section"], mesh.shape["dp"], mesh.shape["tensor"]
        )
        return jax.shard_map(
            body,
            mesh=mesh,
            in_specs=placed,
            out_specs=P("section", "tensor", "dp"),
            check_vma=False,
        )(*args)

    return run
```

time: 191 us -> 196 us (1.026)
  local copies, waits for them, and re-layouts: 2.05 us -> 4.34 us
    another operation x1 -> x0, other arithmetic: 3.37 us -> none  [run(): jax.shard_map(body, mesh=mesh, in_specs=placed, out_specs=P('section', 't...]
    slice x3 -> x4, local copies, waits for them, and re-layouts: 0.26 us -> 3.37 us  [the longest x3 2.24 us: per_device(): theirs = part[half:].astype(BF16)]
    convert_element_type x3, other arithmetic: 0.85 us -> 3.87 us  [the longest x1 2.32 us: per_device(): own = (part[rows:half] + got[rows:].astype(F32) + down_bias[0]).astype(BF16)]
    ppermute x5, waiting for transfers between devices: 2.82 us -> 5.02 us  [from_others(): got = lax.ppermute(sent, 'dp', route)]
    ppermute x8 -> x7, waiting for transfers between devices: 10.3 us -> 8.17 us  [sibling(): return lax.ppermute(block, 'tensor', swap)]
  transfers between devices with their start and end apart: 21 -> 20, of which waited for: 14 -> 15; matrix products, arithmetic and copies ran while one was open for 60% -> 48% of each run, Pallas kernels for 0% -> 0%
where the time goes in v5:
time: 196 us
  matrix products  110 us (56%)
  waiting for transfers between devices  44.4 us (23%)
  starting transfers between devices  25.3 us (13%)
  other arithmetic  12 us (6%)
  local copies, waits for them, and re-layouts  4.34 us (2%)
    dot_general x4, matrix products, up(): pre = jnp.dot(both, up_weight[0], preferred_element_type=F32)  61 us
    dot_general x3, matrix products, per_device(): part = jnp.dot(active, down_weight[0], preferred_element_type=F32)  48.7 us
    ppermute x2, waiting for transfers between devices, shift_and_turn(): return lax.ppermute(block, ('section', 'tensor'), route)  21.6 us
    ppermute x5, starting transfers between devices, from_others(): got = lax.ppermute(sent, 'dp', route)  9.16 us
    ppermute x4, starting transfers between devices, shift(): return lax.ppermute(block, 'tensor', hops(way))  8.49 us
    ppermute x7, waiting for transfers between devices, sibling(): return lax.ppermute(block, 'tensor', swap)  8.17 us
    ppermute x4, waiting for transfers between devices, shift(): return lax.ppermute(block, 'tensor', hops(way))  6.36 us
    ppermute x2, starting transfers between devices, shift_and_turn(): return lax.ppermute(block, ('section', 'tensor'), route)  5.36 us
  transfers between devices with their start and end apart: 20, of which 15 were waited for; matrix products, arithmetic and copies ran while one was open for 48% of the time, Pallas kernels for 0%

profile of v5, /device:TPU:0, one launch (start us, length us, event | category | flops | bytes accessed | tf_op | source)
XLA Modules:
  0.0 195.9 jit_solution(9967183811373603552)
XLA Ops:
  1.5 3.0 %collective-permute-start = (f32[2,64]{1,0:T(2,128)S(1)}, f32[2,64]{1,0:T(2,128)S(1)}, u32[]{:S(2)}, u32[]{:S(2)}) collective-permute-start(f32[2,64]{1,0:T(2,128)S(1)} %pad_maximum_fusion), channel_id=1, source_target_pairs={{0,8},{8,0},{1,9},{9,1},{2,10},{10,2},{3,11},{11,3},{4,12},{12,4},... | collective-permute-start | bytes 1544 | tf_op jit(solution)/shard_map/ppermute | solution.py:42
  7.7 3.2 %collective-permute-start.1 = (bf16[64,6144]{1,0:T(8,128)(2,1)S(1)}, bf16[64,6144]{1,0:T(8,128)(2,1)}, u32[]{:S(2)}, u32[]{:S(2)}) collective-permute-start(bf16[64,6144]{1,0:T(8,128)(2,1)S(1)} %fusion.17), channel_id=1, source_target_pairs={{0,4},{1,5},{4,6},{5,7},{6,2},{7,3},{2,0},{3,1},{8,12},{9,13},{12,... | collective-permute-start | bytes 2359304 | tf_op jit(solution)/shard_map/ppermute | solution.py:29
  10.8 14.4 %fusion.106 = (bf16[128,3072]{1,0:T(8,128)(2,1)S(1)}, f32[128,3072]{1,0:T(8,128)S(1)}) fusion(bf16[1,6144,3072]{2,1,0:T(8,128)(2,1)} %param.10, bf16[64,6144]{1,0:T(8,128)(2,1)S(1)} %collective-permute-done.2, bf16[64,6144]{1,0:T(8,128)(2,1)S(1)} %fusion.17), kind=kOutput, calls=%fused_computation.121 | convolution fusion | flops 4835377152 | bytes 41680896 | tf_op jit(solution)/shard_map/dot_general | solution.py:68
  25.2 3.0 %collective-permute-done.1 = bf16[64,6144]{1,0:T(8,128)(2,1)} collective-permute-done((bf16[64,6144]{1,0:T(8,128)(2,1)S(1)}, bf16[64,6144]{1,0:T(8,128)(2,1)}, u32[]{:S(2)}, u32[]{:S(2)}) %collective-permute-start.1) | collective-permute-done | bytes 786464 | tf_op jit(solution)/shard_map/ppermute | solution.py:29
  28.3 3.5 %collective-permute-start.3 = (bf16[64,6144]{1,0:T(8,128)(2,1)}, bf16[64,6144]{1,0:T(8,128)(2,1)S(1)}, u32[]{:S(2)}, u32[]{:S(2)}) collective-permute-start(bf16[64,6144]{1,0:T(8,128)(2,1)} %collective-permute-done.1), channel_id=1, source_target_pairs={{0,4},{1,5},{4,6},{5,7},{6,2},{7,3},{2,0},{3,1},{8,12},{9,13},{12,... | collective-permute-start | bytes 2359304 | tf_op jit(solution)/shard_map/ppermute | solution.py:29
  34.8 15.7 %fusion.108 = (bf16[128,3072]{1,0:T(8,128)(2,1)}, f32[128,3072]{1,0:T(8,128)S(1)}) fusion(bf16[1,6144,3072]{2,1,0:T(8,128)(2,1)} %param.10, bf16[64,6144]{1,0:T(8,128)(2,1)} %collective-permute-done.4, bf16[64,6144]{1,0:T(8,128)(2,1)} %collective-permute-done.1), kind=kOutput, calls=%fused_computation.123 | convolution fusion | flops 4835377152 | bytes 41680896 | tf_op jit(solution)/shard_map/dot_general | solution.py:68
  55.1 15.5 %fusion.107 = (bf16[128,3072]{1,0:T(8,128)(2,1)}, f32[128,3072]{1,0:T(8,128)S(1)}) fusion(bf16[1,6144,3072]{2,1,0:T(8,128)(2,1)} %param.10, bf16[64,6144]{1,0:T(8,128)(2,1)} %collective-permute-done.7, bf16[64,6144]{1,0:T(8,128)(2,1)S(1)} %collective-permute-done.3), kind=kOutput, calls=%fused_computation.122 | convolution fusion | flops 4835377152 | bytes 41680896 | tf_op jit(solution)/shard_map/dot_general | solution.py:68
  70.6 3.0 %collective-permute-done.9 = bf16[64,6144]{1,0:T(8,128)(2,1)} collective-permute-done((bf16[64,6144]{1,0:T(8,128)(2,1)S(1)}, bf16[64,6144]{1,0:T(8,128)(2,1)}, u32[]{:S(2)}, u32[]{:S(2)}) %collective-permute-start.9) | collective-permute-done | bytes 786464 | tf_op jit(solution)/shard_map/ppermute | solution.py:29
  76.1 15.5 %fusion.109 = (bf16[128,3072]{1,0:T(8,128)(2,1)}, f32[128,3072]{1,0:T(8,128)S(1)}) fusion(bf16[1,6144,3072]{2,1,0:T(8,128)(2,1)} %param.10, bf16[64,6144]{1,0:T(8,128)(2,1)S(1)} %collective-permute-done.11, bf16[64,6144]{1,0:T(8,128)(2,1)} %collective-permute-done.9), kind=kOutput, calls=%fused_computation.124 | convolution fusion | flops 4835377152 | bytes 41680896 | tf_op jit(solution)/shard_map/dot_general | solution.py:68
  91.6 2.2 %collective-permute-done.8 = bf16[128,3072]{1,0:T(8,128)(2,1)S(1)} collective-permute-done((bf16[128,3072]{1,0:T(8,128)(2,1)}, bf16[128,3072]{1,0:T(8,128)(2,1)S(1)}, u32[]{:S(2)}, u32[]{:S(2)}) %collective-permute-start.8) | collective-permute-done | bytes 786464 | tf_op jit(solution)/shard_map/ppermute | solution.py:42
  94.8 2.7 %fusion.25 = (bf16[128,3072]{1,0:T(8,128)(2,1)S(1)}, bf16[128,3072]{1,0:T(8,128)(2,1)S(1)}) fusion(f32[128,3072]{1,0:T(8,128)S(1)} %get-tuple-element.38, bf16[128,3072]{1,0:T(8,128)(2,1)} %copy-done.4, f32[3072]{0:T(1024)S(1)} %bitcast.46, f32[128,3072]{1,0:T(8,128)S(1)} %get-tuple-element.36, bf16[128,3072]{1,0:T(8,128)(2,1)} %copy-done.3), kind=kLoop, calls=%fused_computation.32 | loop fusion | flops 9437184 | bytes 6303744 | tf_op jit(solution)/shard_map/convert_element_type | solution.py:76
  98.6 18.8 %fusion.4 = f32[256,6144]{1,0:T(8,128)} fusion(bf16[1,3072,6144]{2,1,0:T(8,128)(2,1)} %param.12, bf16[64,3072]{1,0:T(8,128)(2,1)} %get-tuple-element.43, bf16[64,3072]{1,0:T(8,128)(2,1)} %get-tuple-element.30, bf16[64,3072]{1,0:T(8,128)(2,1)} %get-tuple-element.44, bf16[64,3072]{1,0:T(8,128)(2,1)S(1)} %get-tuple-element.29), kind=kOutput, calls=%fused_computation.4 | convolution fusion | flops 9669967872 | bytes 45613056 | tf_op jit(solution)/shard_map/dot_general | solution.py:109
  117.3 2.1 %slice.89 = bf16[128,6144]{1,0:T(8,128)(2,1)S(1)} slice(f32[256,6144]{1,0:T(8,128)} %fusion.4), slice={[128:256], [0:6144]} | slice | bytes 3145728 | tf_op jit(solution)/shard_map/slice | solution.py:111
  122.9 2.3 %fusion.55 = (bf16[64,6144]{1,0:T(8,128)(2,1)S(1)}, bf16[64,6144]{1,0:T(8,128)(2,1)S(1)}) fusion(f32[256,6144]{1,0:T(8,128)} %fusion.4, bf16[128,6144]{1,0:T(8,128)(2,1)S(1)} %collective-permute-done.12, f32[6144]{0:T(1024)S(1)} %bitcast.49), kind=kLoop, calls=%fused_computation.68 | loop fusion | flops 2752512 | bytes 6316032 | tf_op jit(solution)/shard_map/convert_element_type | solution.py:127
  127.6 15.0 %fusion.2 = f32[128,6144]{1,0:T(8,128)S(1)} fusion(bf16[1,3072,6144]{2,1,0:T(8,128)(2,1)} %param.12, f32[128,3072]{1,0:T(8,128)S(1)} %get-tuple-element.40, bf16[128,3072]{1,0:T(8,128)(2,1)} %copy-done.5, f32[3072]{0:T(1024)S(1)} %bitcast.47), kind=kOutput, calls=%fused_computation.2 | convolution fusion | flops 4836556800 | bytes 43266048 | tf_op jit(solution)/shard_map/dot_general | solution.py:109
  142.7 2.2 %collective-permute-done.13 = bf16[64,6144]{1,0:T(8,128)(2,1)} collective-permute-done((bf16[64,6144]{1,0:T(8,128)(2,1)S(1)}, bf16[64,6144]{1,0:T(8,128)(2,1)}, u32[]{:S(2)}, u32[]{:S(2)}) %collective-permute-start.13) | collective-permute-done | bytes 786464 | tf_op jit(solution)/shard_map/ppermute | solution.py:129
  145.3 2.3 %collective-permute-done.16 = bf16[64,6144]{1,0:T(8,128)(2,1)S(1)} collective-permute-done((bf16[64,6144]{1,0:T(8,128)(2,1)S(1)}, bf16[64,6144]{1,0:T(8,128)(2,1)S(1)}, u32[]{:S(2)}, u32[]{:S(2)}) %collective-permute-start.16) | collective-permute-done | bytes 786464 | tf_op jit(solution)/shard_map/ppermute | solution.py:36
  147.7 2.7 %collective-permute-start.17 = (bf16[64,6144]{1,0:T(8,128)(2,1)S(1)}, bf16[64,6144]{1,0:T(8,128)(2,1)S(1)}, u32[]{:S(2)}, u32[]{:S(2)}) collective-permute-start(bf16[64,6144]{1,0:T(8,128)(2,1)S(1)} %fusion.52), channel_id=1, source_target_pairs={{0,18},{1,19},{4,16},{5,17},{6,20},{7,21},{2,22},{3,23},{16,2},{17... | collective-permute-start | bytes 2359304 | tf_op jit(solution)/shard_map/ppermute | solution.py:33
  150.4 15.0 %fusion = f32[128,6144]{1,0:T(8,128)S(1)} fusion(bf16[1,3072,6144]{2,1,0:T(8,128)(2,1)} %param.12, f32[128,3072]{1,0:T(8,128)S(1)} %get-tuple-element.42, bf16[128,3072]{1,0:T(8,128)(2,1)} %collective-permute-done.15, f32[3072]{0:T(1024)S(1)} %bitcast.48), kind=kOutput, calls=%fused_computation | convolution fusion | flops 4836556800 | bytes 43266048 | tf_op jit(solution)/shard_map/dot_general | solution.py:109
  165.4 3.8 %collective-permute-done.17 = bf16[64,6144]{1,0:T(8,128)(2,1)S(1)} collective-permute-done((bf16[64,6144]{1,0:T(8,128)(2,1)S(1)}, bf16[64,6144]{1,0:T(8,128)(2,1)S(1)}, u32[]{:S(2)}, u32[]{:S(2)}) %collective-permute-start.17) | collective-permute-done | bytes 786464 | tf_op jit(solution)/shard_map/ppermute | solution.py:33
  169.2 2.3 %collective-permute-done.18 = bf16[64,6144]{1,0:T(8,128)(2,1)S(1)} collective-permute-done((bf16[64,6144]{1,0:T(8,128)(2,1)S(1)}, bf16[64,6144]{1,0:T(8,128)(2,1)S(1)}, u32[]{:S(2)}, u32[]{:S(2)}) %collective-permute-start.18) | collective-permute-done | bytes 786464 | tf_op jit(solution)/shard_map/ppermute | solution.py:36
  172.9 2.7 %collective-permute-start.19 = (bf16[64,6144]{1,0:T(8,128)(2,1)S(1)}, bf16[64,6144]{1,0:T(8,128)(2,1)S(1)}, u32[]{:S(2)}, u32[]{:S(2)}) collective-permute-start(bf16[64,6144]{1,0:T(8,128)(2,1)S(1)} %fusion.51), channel_id=1, source_target_pairs={{0,20},{1,21},{4,22},{5,23},{6,18},{7,19},{2,16},{3,17},{16,4},{17... | collective-permute-start | bytes 2359304 | tf_op jit(solution)/shard_map/ppermute | solution.py:33
  175.6 17.8 %collective-permute-done.19 = bf16[64,6144]{1,0:T(8,128)(2,1)S(1)} collective-permute-done((bf16[64,6144]{1,0:T(8,128)(2,1)S(1)}, bf16[64,6144]{1,0:T(8,128)(2,1)S(1)}, u32[]{:S(2)}, u32[]{:S(2)}) %collective-permute-start.19) | collective-permute-done | bytes 786464 | tf_op jit(solution)/shard_map/ppermute | solution.py:33
  193.5 2.4 %fusion.75 = bf16[1,64,6144]{2,1,0:T(8,128)(2,1)} fusion(bf16[64,6144]{1,0:T(8,128)(2,1)S(1)} %collective-permute-done.19, bf16[64,6144]{1,0:T(8,128)(2,1)S(1)} %collective-permute-done.17, bf16[64,6144]{1,0:T(8,128)(2,1)S(1)} %copy-done.2, bf16[64,6144]{1,0:T(8,128)(2,1)} %collective-permute-done.13), kind=kLoop, calls=%fused_computation.89 | loop fusion | flops 3145728 | bytes 3932160 | tf_op jit(solution)/shard_map/broadcast_in_dim | solution.py:133
  (54 shorter events, 24.7 us)
Async XLA Ops:
  1.5 4.5 %collective-permute-start = (f32[2,64]{1,0:T(2,128)S(1)}, f32[2,64]{1,0:T(2,128)S(1)}, u32[]{:S(2)}, u32[]{:S(2)}) collective-permute-start(f32[2,64]{1,0:T(2,128)S(1)} %pad_maximum_fusion), channel_id=1, source_target_pairs={{0,8},{8,0},{1,9},{9,1},{2,10},{10,2},{3,11},{11,3},{4,12},{12,4},... | collective-permute-start | bytes 1544 | tf_op jit(solution)/shard_map/ppermute | solution.py:42
  7.6 24.2 %copy-start = (bf16[1,64,6144]{2,1,0:T(8,128)(2,1)S(1)}, bf16[1,64,6144]{2,1,0:T(8,128)(2,1)}, u32[]{:S(2)}) copy-start(bf16[1,64,6144]{2,1,0:T(8,128)(2,1)} %param.7) | copy-start | bytes 2359300
  7.6 3.3 %collective-permute-start.2 = (bf16[64,6144]{1,0:T(8,128)(2,1)S(1)}, bf16[64,6144]{1,0:T(8,128)(2,1)S(1)}, u32[]{:S(2)}, u32[]{:S(2)}) collective-permute-start(bf16[64,6144]{1,0:T(8,128)(2,1)S(1)} %fusion.17), channel_id=1, source_target_pairs={{0,1},{1,0},{2,3},{3,2},{4,5},{5,4},{6,7},{7,6},{8,9},{9,8},{10,11... | collective-permute-start | bytes 2359304 | tf_op jit(solution)/shard_map/ppermute | solution.py:36
  7.7 20.6 %collective-permute-start.1 = (bf16[64,6144]{1,0:T(8,128)(2,1)S(1)}, bf16[64,6144]{1,0:T(8,128)(2,1)}, u32[]{:S(2)}, u32[]{:S(2)}) collective-permute-start(bf16[64,6144]{1,0:T(8,128)(2,1)S(1)} %fusion.17), channel_id=1, source_target_pairs={{0,4},{1,5},{4,6},{5,7},{6,2},{7,3},{2,0},{3,1},{8,12},{9,13},{12,... | collective-permute-start | bytes 2359304 | tf_op jit(solution)/shard_map/ppermute | solution.py:29
  28.3 6.5 %collective-permute-start.4 = (bf16[64,6144]{1,0:T(8,128)(2,1)}, bf16[64,6144]{1,0:T(8,128)(2,1)}, u32[]{:S(2)}, u32[]{:S(2)}) collective-permute-start(bf16[64,6144]{1,0:T(8,128)(2,1)} %collective-permute-done.1), channel_id=1, source_target_pairs={{0,1},{1,0},{2,3},{3,2},{4,5},{5,4},{6,7},{7,6},{8,9},{9,8},{10,11... | collective-permute-start | bytes 2359304 | tf_op jit(solution)/shard_map/ppermute | solution.py:36
  28.3 22.2 %collective-permute-start.3 = (bf16[64,6144]{1,0:T(8,128)(2,1)}, bf16[64,6144]{1,0:T(8,128)(2,1)S(1)}, u32[]{:S(2)}, u32[]{:S(2)}) collective-permute-start(bf16[64,6144]{1,0:T(8,128)(2,1)} %collective-permute-done.1), channel_id=1, source_target_pairs={{0,4},{1,5},{4,6},{5,7},{6,2},{7,3},{2,0},{3,1},{8,12},{9,13},{12,... | collective-permute-start | bytes 2359304 | tf_op jit(solution)/shard_map/ppermute | solution.py:29
  31.7 19.7 %collective-permute-start.6 = (bf16[64,6144]{1,0:T(8,128)(2,1)S(1)}, bf16[64,6144]{1,0:T(8,128)(2,1)S(1)}, u32[]{:S(2)}, u32[]{:S(2)}) collective-permute-start(bf16[64,6144]{1,0:T(8,128)(2,1)S(1)} %bitcast.45), channel_id=1, source_target_pairs={{0,16},{16,0},{1,17},{17,1},{2,18},{18,2},{3,19},{19,3},{4,20},{20... | collective-permute-start | bytes 2359304 | tf_op jit(solution)/shard_map/ppermute | solution.py:81
  33.3 19.4 %collective-permute-start.5 = (bf16[128,3072]{1,0:T(8,128)(2,1)S(1)}, bf16[128,3072]{1,0:T(8,128)(2,1)S(1)}, u32[]{:S(2)}, u32[]{:S(2)}) collective-permute-start(bf16[128,3072]{1,0:T(8,128)(2,1)S(1)} %get-tuple-element.35), channel_id=1, source_target_pairs={{0,8},{8,0},{1,9},{9,1},{2,10},{10,2},{3,11},{11,3},{4,12},{12,4},... | collective-permute-start | bytes 2359304 | tf_op jit(solution)/shard_map/ppermute | solution.py:42
  52.7 17.9 %copy-start.3 = (bf16[128,3072]{1,0:T(8,128)(2,1)}, bf16[128,3072]{1,0:T(8,128)(2,1)S(1)}, u32[]{:S(2)}) copy-start(bf16[128,3072]{1,0:T(8,128)(2,1)S(1)} %collective-permute-done.5) | copy-start | bytes 2359300
  52.7 2.4 %collective-permute-start.7 = (bf16[64,6144]{1,0:T(8,128)(2,1)S(1)}, bf16[64,6144]{1,0:T(8,128)(2,1)}, u32[]{:S(2)}, u32[]{:S(2)}) collective-permute-start(bf16[64,6144]{1,0:T(8,128)(2,1)S(1)} %collective-permute-done.3), channel_id=1, source_target_pairs={{0,1},{1,0},{2,3},{3,2},{4,5},{5,4},{6,7},{7,6},{8,9},{9,8},{10,11... | collective-permute-start | bytes 2359304 | tf_op jit(solution)/shard_map/ppermute | solution.py:36
  52.7 21.0 %collective-permute-start.9 = (bf16[64,6144]{1,0:T(8,128)(2,1)S(1)}, bf16[64,6144]{1,0:T(8,128)(2,1)}, u32[]{:S(2)}, u32[]{:S(2)}) collective-permute-start(bf16[64,6144]{1,0:T(8,128)(2,1)S(1)} %fusion.17), channel_id=1, source_target_pairs={{0,2},{1,3},{4,0},{5,1},{6,4},{7,5},{2,6},{3,7},{8,10},{9,11},{12,... | collective-permute-start | bytes 2359304 | tf_op jit(solution)/shard_map/ppermute | solution.py:29
  52.7 21.0 %collective-permute-start.10 = (bf16[128,3072]{1,0:T(8,128)(2,1)}, bf16[128,3072]{1,0:T(8,128)(2,1)S(1)}, u32[]{:S(2)}, u32[]{:S(2)}) collective-permute-start(bf16[128,3072]{1,0:T(8,128)(2,1)} %get-tuple-element.39), channel_id=1, source_target_pairs={{0,8},{8,0},{1,9},{9,1},{2,10},{10,2},{3,11},{11,3},{4,12},{12,4},... | collective-permute-start | bytes 2359304 | tf_op jit(solution)/shard_map/ppermute | solution.py:42
  73.6 2.5 %collective-permute-start.11 = (bf16[64,6144]{1,0:T(8,128)(2,1)}, bf16[64,6144]{1,0:T(8,128)(2,1)S(1)}, u32[]{:S(2)}, u32[]{:S(2)}) collective-permute-start(bf16[64,6144]{1,0:T(8,128)(2,1)} %collective-permute-done.9), channel_id=1, source_target_pairs={{0,1},{1,0},{2,3},{3,2},{4,5},{5,4},{6,7},{7,6},{8,9},{9,8},{10,11... | collective-permute-start | bytes 2359304 | tf_op jit(solution)/shard_map/ppermute | solution.py:36
  73.6 21.1 %copy-start.6 = (f32[1,3072]{1,0:T(1,128)S(1)}, f32[1,3072]{1,0:T(1,128)}, u32[]{:S(2)}) copy-start(f32[1,3072]{1,0:T(1,128)} %param.11) | copy-start | bytes 36868
  73.6 20.2 %collective-permute-start.8 = (bf16[128,3072]{1,0:T(8,128)(2,1)}, bf16[128,3072]{1,0:T(8,128)(2,1)S(1)}, u32[]{:S(2)}, u32[]{:S(2)}) collective-permute-start(bf16[128,3072]{1,0:T(8,128)(2,1)} %get-tuple-element.37), channel_id=1, source_target_pairs={{0,8},{8,0},{1,9},{9,1},{2,10},{10,2},{3,11},{11,3},{4,12},{12,4},... | collective-permute-start | bytes 2359304 | tf_op jit(solution)/shard_map/ppermute | solution.py:42
  119.4 3.5 %collective-permute-start.12 = (bf16[128,6144]{1,0:T(8,128)(2,1)S(1)}, bf16[128,6144]{1,0:T(8,128)(2,1)S(1)}, u32[]{:S(2)}, u32[]{:S(2)}) collective-permute-start(bf16[128,6144]{1,0:T(8,128)(2,1)S(1)} %slice.89), channel_id=1, source_target_pairs={{0,1},{1,0},{2,3},{3,2},{4,5},{5,4},{6,7},{7,6},{8,9},{9,8},{10,11... | collective-permute-start | bytes 4718600 | tf_op jit(solution)/shard_map/ppermute | solution.py:36
  119.5 23.2 %collective-permute-start.15 = (bf16[128,3072]{1,0:T(8,128)(2,1)}, bf16[128,3072]{1,0:T(8,128)(2,1)}, u32[]{:S(2)}, u32[]{:S(2)}) collective-permute-start(bf16[128,3072]{1,0:T(8,128)(2,1)} %get-tuple-element.41), channel_id=1, source_target_pairs={{0,8},{8,0},{1,9},{9,1},{2,10},{10,2},{3,11},{11,3},{4,12},{12,4},... | collective-permute-start | bytes 2359304 | tf_op jit(solution)/shard_map/ppermute | solution.py:42
  125.2 19.8 %collective-permute-start.13 = (bf16[64,6144]{1,0:T(8,128)(2,1)S(1)}, bf16[64,6144]{1,0:T(8,128)(2,1)}, u32[]{:S(2)}, u32[]{:S(2)}) collective-permute-start(bf16[64,6144]{1,0:T(8,128)(2,1)S(1)} %get-tuple-element.27), channel_id=1, source_target_pairs={{0,16},{16,0},{1,17},{17,1},{2,18},{18,2},{3,19},{19,3},{4,20},{20... | collective-permute-start | bytes 2359304 | tf_op jit(solution)/shard_map/ppermute | solution.py:129
  125.8 19.5 %collective-permute-start.14 = (bf16[64,6144]{1,0:T(8,128)(2,1)S(1)}, bf16[64,6144]{1,0:T(8,128)(2,1)}, u32[]{:S(2)}, u32[]{:S(2)}) collective-permute-start(bf16[64,6144]{1,0:T(8,128)(2,1)S(1)} %get-tuple-element.28), channel_id=1, source_target_pairs={{0,4},{1,5},{4,6},{5,7},{6,2},{7,3},{2,0},{3,1},{8,12},{9,13},{12,... | collective-permute-start | bytes 2359304 | tf_op jit(solution)/shard_map/ppermute | solution.py:29
  145.3 2.3 %collective-permute-start.16 = (bf16[64,6144]{1,0:T(8,128)(2,1)S(1)}, bf16[64,6144]{1,0:T(8,128)(2,1)S(1)}, u32[]{:S(2)}, u32[]{:S(2)}) collective-permute-start(bf16[64,6144]{1,0:T(8,128)(2,1)S(1)} %slice.91), channel_id=1, source_target_pairs={{0,1},{1,0},{2,3},{3,2},{4,5},{5,4},{6,7},{7,6},{8,9},{9,8},{10,11... | collective-permute-start | bytes 2359304 | tf_op jit(solution)/shard_map/ppermute | solution.py:36
  147.7 21.5 %collective-permute-start.17 = (bf16[64,6144]{1,0:T(8,128)(2,1)S(1)}, bf16[64,6144]{1,0:T(8,128)(2,1)S(1)}, u32[]{:S(2)}, u32[]{:S(2)}) collective-permute-start(bf16[64,6144]{1,0:T(8,128)(2,1)S(1)} %fusion.52), channel_id=1, source_target_pairs={{0,18},{1,19},{4,16},{5,17},{6,20},{7,21},{2,22},{3,23},{16,2},{17... | collective-permute-start | bytes 2359304 | tf_op jit(solution)/shard_map/ppermute | solution.py:33
  165.4 28.0 %copy-start.2 = (bf16[64,6144]{1,0:T(8,128)(2,1)S(1)}, bf16[64,6144]{1,0:T(8,128)(2,1)}, u32[]{:S(2)}) copy-start(bf16[64,6144]{1,0:T(8,128)(2,1)} %copy-done.1) | copy-start | bytes 2359300
  169.2 2.3 %collective-permute-start.18 = (bf16[64,6144]{1,0:T(8,128)(2,1)S(1)}, bf16[64,6144]{1,0:T(8,128)(2,1)S(1)}, u32[]{:S(2)}, u32[]{:S(2)}) collective-permute-start(bf16[64,6144]{1,0:T(8,128)(2,1)S(1)} %slice.90), channel_id=1, source_target_pairs={{0,1},{1,0},{2,3},{3,2},{4,5},{5,4},{6,7},{7,6},{8,9},{9,8},{10,11... | collective-permute-start | bytes 2359304 | tf_op jit(solution)/shard_map/ppermute | solution.py:36
  172.9 20.5 %collective-permute-start.19 = (bf16[64,6144]{1,0:T(8,128)(2,1)S(1)}, bf16[64,6144]{1,0:T(8,128)(2,1)S(1)}, u32[]{:S(2)}, u32[]{:S(2)}) collective-permute-start(bf16[64,6144]{1,0:T(8,128)(2,1)S(1)} %fusion.51), channel_id=1, source_target_pairs={{0,20},{1,21},{4,22},{5,23},{6,18},{7,19},{2,16},{3,17},{16,4},{17... | collective-permute-start | bytes 2359304 | tf_op jit(solution)/shard_map/ppermute | solution.py:33
  (4 other events, 10.9 us)

commit v6 on v5

--- a/solution.py
+++ b/solution.py
@@ -63,70 +63,78 @@
         def tie(values, done):
             return lax.optimization_barrier((values, done))[0]
 
-        def up(offset, block):
-            both = jnp.concatenate([block, sibling(block)], axis=0)
-            pre = jnp.dot(both, up_weight[0], preferred_element_type=F32)
-            pres[offset] = (pre, from_others(pre.astype(BF16)))
-            return pre
+        def up(held):
+            both = jnp.concatenate([half for block in held for half in (block, sibling(block))])
+            return jnp.dot(both, up_weight[0], preferred_element_type=F32)
 
-        def act(offset, done=None):
+        def act(offset, done):
             pre, other = pres[offset]
-            if done is not None:
-                other = tie(other, done)
+            other = tie(other, done)
             return jax.nn.gelu(pre + other.astype(F32) + up_bias[0], approximate=True).astype(BF16)
 
-        ups = [(chips - k, 1) for k in range(1, ahead + 1)]
-        ups += [(k, -1) for k in range(1, chips - ahead)]
-        done = up(0, normed)
-        residual = lax.ppermute(tie(incoming[0], done), "section", turn)
-        carried, before = {1: normed, -1: normed}, None
-        for offset, way in ups:
-            block = shift(carried[way], way)
-            extra = () if before is None else (pres[before][1], residual)
-            block = tie(block, (done, extra))
-            carried[way] = block
-            before = 0 if before is None else last
-            last = offset
-            done = up(offset, block)
+        def down(offset, done, over):
+            part = jnp.dot(act(offset, done), down_weight[0], preferred_element_type=F32)
+            theirs = tie(part[rows:].astype(BF16), over)
+            return part[:rows] + sibling(theirs).astype(F32)
+
+        pre = up([normed])
+        pres[0] = (pre, from_others(pre.astype(BF16)))
+        block = tie(shift(normed, 1), pre)
+        ahead_blocks, back_blocks = {}, {}
+        back = tie(normed, pre)
+        for k in range(1, chips - ahead):
+            back_blocks[k] = back = shift(back, -1)
+        pre = up([block])
+        front = tie(block, pre)
+        for k in range(2, ahead + 1):
+            ahead_blocks[chips - k] = front = shift(front, 1)
+        pres[chips - 1] = (pre, from_others(pre.astype(BF16)))
+        residual = lax.ppermute(tie(incoming[0], pre), "section", turn)
+
+        own = down(0, (pre, back_blocks), (ahead_blocks, pres[chips - 1][1], residual))
+        own = (own + down_bias[0]).astype(BF16)
+        done = own
+        own = lax.ppermute(own, "section", turn)
 
         along = [(k, 1) for k in range(ahead, 0, -1)]
         against = [(chips - k, -1) for k in range(chips - ahead - 1, 0, -1)]
-        downs = [along.pop(0)]
+        downs = []
         while along or against:
-            downs.append(against.pop(0) if against else along.pop(0))
-            if along and len(downs) % 2 == 0:
-                downs.append(along.pop(0))
+            for offsets in (against, along):
+                if offsets:
+                    downs.append(offsets.pop(0))
+        held = {**ahead_blocks, **back_blocks}
+        rest = [offset for offset, _ in downs if offset in held]
+        if rest:
+            held = tie(held, done)
+            done = pre = up([held[offset] for offset in rest])
+            for place, offset in enumerate(rest):
+                pres[offset] = (pre[2 * rows * place : 2 * rows * (place + 1)], None)
 
-        sums, arrived = {}, []
-        own = sent = None
+        def exchange(place, done=None):
+            if place < len(downs):
+                pre, other = pres[downs[place][0]]
+                if other is None:
+                    sent = pre.astype(BF16)
+                    other = from_others(sent if done is None else tie(sent, done))
+                    pres[downs[place][0]] = (pre, other)
+                return other
+            return ()
+
+        exchange(0)
+        coming = exchange(1)
+        sums, arrived, over = {}, [], own
         for place, (offset, way) in enumerate(downs):
-            active = act(offset, done)
-            if place == 0:
-                mine = act(0)
-                active = jnp.concatenate(
-                    [active[:rows], mine[:rows], active[rows:], mine[rows:]], axis=0
-                )
-            part = jnp.dot(active, down_weight[0], preferred_element_type=F32)
-            half = part.shape[0] // 2
-            theirs = part[half:].astype(BF16)
-            if place:
-                over = pres[downs[place + 1][0]][1] if place + 1 < len(downs) else ()
-                theirs = tie(theirs, (sent, over, own))
-            got = sibling(theirs)
-            summed = part[:rows] + got[:rows].astype(F32)
+            summed = down(offset, done, (over, coming))
             if way in sums:
                 summed = summed + sums[way].astype(F32)
-            summed = summed.astype(BF16)
+            done = summed = summed.astype(BF16)
             if offset == way % chips:
-                sent = shift_and_turn(summed, way)
-                arrived.append(sent)
+                over = shift_and_turn(summed, way)
+                arrived.append(over)
             else:
-                sent = sums[way] = shift(summed, way)
-            done = summed
-            if place == 0:
-                own = (part[rows:half] + got[rows:].astype(F32) + down_bias[0]).astype(BF16)
-                done = (summed, own)
-                own = lax.ppermute(own, "section", turn)
+                over = sums[way] = shift(summed, way)
+            coming = exchange(place + 2, summed)
         result = own.astype(F32) + residual.astype(F32)
         for value in arrived:
             result = result + value.astype(F32)

time: 196 us -> 191 us (0.974)
  waiting for transfers between devices: 44.4 us -> 49.9 us
  other arithmetic: 12 us -> 8.15 us
  matrix products: 110 us -> 107 us
  starting transfers between devices: 25.3 us -> 22.5 us
    ppermute x5, waiting for transfers between devices: 5.02 us -> 9.66 us  [from_others(): got = lax.ppermute(sent, 'dp', route)]
    convert_element_type x4, other arithmetic: 6.56 us -> 2.49 us  [the longest x3 1.42 us: per_device(): done = summed = summed.astype(BF16)]
    ppermute x4, waiting for transfers between devices: 6.36 us -> 9.35 us  [shift(): return lax.ppermute(block, 'tensor', hops(way))]
    dot_general x7, matrix products: 110 us -> 107 us  [the longest x4 60 us: down(): jnp.dot(act(offset, done), down_weight[0], preferred_element_type=F32)]
    ppermute x7 -> x8, waiting for transfers between devices: 8.17 us -> 10.8 us  [sibling(): return lax.ppermute(block, 'tensor', swap)]
    ppermute x1, waiting for transfers between devices: 2.25 us -> 0.01 us  [per_device(): own = lax.ppermute(own, 'section', turn)]
    ppermute x2, waiting for transfers between devices: 21.6 us -> 19.4 us  [shift_and_turn(): return lax.ppermute(block, ('section', 'tensor'), route)]
  transfers between devices with their start and end apart: 20 -> 21, of which waited for: 15 -> 17; matrix products, arithmetic and copies ran while one was open for 48% -> 57% of each run, Pallas kernels for 0% -> 0%
where the time goes in v6:
time: 191 us; the launch traced here: 190 us
  matrix products  107 us (56%)
  waiting for transfers between devices  49.9 us (26%)
  starting transfers between devices  22.5 us (12%)
  other arithmetic  8.15 us (4%)
  local copies, waits for them, and re-layouts  2.64 us (1%)
    dot_general x4, matrix products, down(): jnp.dot(act(offset, done), down_weight[0], preferred_element_type=F32)  60 us
    dot_general x3, matrix products, up(): return jnp.dot(both, up_weight[0], preferred_element_type=F32)  46.9 us
    ppermute x2, waiting for transfers between devices, shift_and_turn(): return lax.ppermute(block, ('section', 'tensor'), route)  19.4 us
    ppermute x8, waiting for transfers between devices, sibling(): return lax.ppermute(block, 'tensor', swap)  10.8 us
    ppermute x5, waiting for transfers between devices, from_others(): got = lax.ppermute(sent, 'dp', route)  9.66 us
    ppermute x4, waiting for transfers between devices, shift(): return lax.ppermute(block, 'tensor', hops(way))  9.35 us
    ppermute x5, starting transfers between devices, from_others(): got = lax.ppermute(sent, 'dp', route)  8.97 us
    ppermute x4, starting transfers between devices, shift(): return lax.ppermute(block, 'tensor', hops(way))  7.49 us
  transfers between devices with their start and end apart: 21, of which 17 were waited for; matrix products, arithmetic and copies ran while one was open for 57% of the time, Pallas kernels for 0%

profile of v6, /device:TPU:0, one launch (start us, length us, event | category | flops | bytes accessed | tf_op | source)
XLA Modules:
  0.0 190.3 jit_solution(8990843138159898930)
XLA Ops:
  1.5 3.0 %collective-permute-start = (f32[2,64]{1,0:T(2,128)S(1)}, f32[2,64]{1,0:T(2,128)S(1)}, u32[]{:S(2)}, u32[]{:S(2)}) collective-permute-start(f32[2,64]{1,0:T(2,128)S(1)} %pad_maximum_fusion), channel_id=1, source_target_pairs={{0,8},{8,0},{1,9},{9,1},{2,10},{10,2},{3,11},{11,3},{4,12},{12,4},... | collective-permute-start | bytes 1544 | tf_op jit(solution)/shard_map/ppermute | solution.py:42
  4.5 1.5 collective-permute-done
  7.7 3.2 %collective-permute-start.3 = (bf16[64,6144]{1,0:T(8,128)(2,1)S(1)}, bf16[64,6144]{1,0:T(8,128)(2,1)S(1)}, u32[]{:S(2)}, u32[]{:S(2)}) collective-permute-start(bf16[64,6144]{1,0:T(8,128)(2,1)S(1)} %fusion.24), channel_id=1, source_target_pairs={{0,4},{1,5},{4,6},{5,7},{6,2},{7,3},{2,0},{3,1},{8,12},{9,13},{12,... | collective-permute-start | bytes 2359304 | tf_op jit(solution)/shard_map/ppermute | solution.py:29
  10.8 14.4 %fusion.117 = (bf16[128,3072]{1,0:T(8,128)(2,1)S(1)}, f32[128,3072]{1,0:T(8,128)S(1)}) fusion(bf16[1,6144,3072]{2,1,0:T(8,128)(2,1)} %param.10, bf16[64,6144]{1,0:T(8,128)(2,1)S(1)} %collective-permute-done.1, bf16[64,6144]{1,0:T(8,128)(2,1)S(1)} %fusion.24), kind=kOutput, calls=%fused_computation.133 | convolution fusion | flops 4835377152 | bytes 41680896 | tf_op jit(solution)/shard_map/dot_general | solution.py:68
  25.2 3.0 %collective-permute-done.3 = bf16[64,6144]{1,0:T(8,128)(2,1)S(1)} collective-permute-done((bf16[64,6144]{1,0:T(8,128)(2,1)S(1)}, bf16[64,6144]{1,0:T(8,128)(2,1)S(1)}, u32[]{:S(2)}, u32[]{:S(2)}) %collective-permute-start.3) | collective-permute-done | bytes 786464 | tf_op jit(solution)/shard_map/ppermute | solution.py:29
  28.2 2.4 %collective-permute-start.5 = (bf16[64,6144]{1,0:T(8,128)(2,1)S(1)}, bf16[64,6144]{1,0:T(8,128)(2,1)S(1)}, u32[]{:S(2)}, u32[]{:S(2)}) collective-permute-start(bf16[64,6144]{1,0:T(8,128)(2,1)S(1)} %fusion.24), channel_id=1, source_target_pairs={{0,2},{1,3},{4,0},{5,1},{6,4},{7,5},{2,6},{3,7},{8,10},{9,11},{12,... | collective-permute-start | bytes 2359304 | tf_op jit(solution)/shard_map/ppermute | solution.py:29
  32.1 15.3 %fusion.118 = (bf16[128,3072]{1,0:T(8,128)(2,1)}, f32[128,3072]{1,0:T(8,128)}) fusion(bf16[1,6144,3072]{2,1,0:T(8,128)(2,1)} %param.10, bf16[64,6144]{1,0:T(8,128)(2,1)S(1)} %collective-permute-done.4, bf16[64,6144]{1,0:T(8,128)(2,1)S(1)} %collective-permute-done.3), kind=kOutput, calls=%fused_computation.134 | convolution fusion | flops 4835377152 | bytes 41680896 | tf_op jit(solution)/shard_map/dot_general | solution.py:68
  47.4 2.4 %collective-permute-done.5 = bf16[64,6144]{1,0:T(8,128)(2,1)S(1)} collective-permute-done((bf16[64,6144]{1,0:T(8,128)(2,1)S(1)}, bf16[64,6144]{1,0:T(8,128)(2,1)S(1)}, u32[]{:S(2)}, u32[]{:S(2)}) %collective-permute-start.5) | collective-permute-done | bytes 786464 | tf_op jit(solution)/shard_map/ppermute | solution.py:29
  51.7 1.5 collective-permute-start.8
  54.7 15.0 %fusion.6 = f32[128,6144]{1,0:T(8,128)S(1)} fusion(bf16[1,3072,6144]{2,1,0:T(8,128)(2,1)} %param.12, f32[128,3072]{1,0:T(8,128)S(1)} %get-tuple-element.42, bf16[128,3072]{1,0:T(8,128)(2,1)} %collective-permute-done.2, f32[3072]{0:T(1024)S(1)} %bitcast.42), kind=kOutput, calls=%fused_computation.6 | convolution fusion | flops 4836556800 | bytes 43266048 | tf_op jit(solution)/shard_map/dot_general | solution.py:76
  72.0 2.3 %collective-permute-done.9 = bf16[64,6144]{1,0:T(8,128)(2,1)S(1)} collective-permute-done((bf16[64,6144]{1,0:T(8,128)(2,1)S(1)}, bf16[64,6144]{1,0:T(8,128)(2,1)S(1)}, u32[]{:S(2)}, u32[]{:S(2)}) %collective-permute-start.9) | collective-permute-done | bytes 786464 | tf_op jit(solution)/shard_map/ppermute | solution.py:36
  78.9 17.3 %fusion.8 = f32[256,3072]{1,0:T(8,128)S(1)} fusion(bf16[1,6144,3072]{2,1,0:T(8,128)(2,1)} %param.10, bf16[64,6144]{1,0:T(8,128)(2,1)} %collective-permute-done.12, bf16[64,6144]{1,0:T(8,128)(2,1)} %copy-done.8, bf16[64,6144]{1,0:T(8,128)(2,1)} %copy-done.10, bf16[64,6144]{1,0:T(8,128)(2,1)} %collective-permute-done.6), kind=kOutput, calls=%fused_computation.8 | convolution fusion | flops 9676259328 | bytes 44040192 | tf_op jit(solution)/shard_map/dot_general | solution.py:68
  99.1 15.0 %fusion.4 = f32[128,6144]{1,0:T(8,128)S(1)} fusion(bf16[1,3072,6144]{2,1,0:T(8,128)(2,1)} %param.12, f32[128,3072]{1,0:T(8,128)S(1)} %copy-done, bf16[128,3072]{1,0:T(8,128)(2,1)} %copy-done.6, f32[3072]{0:T(1024)S(1)} %bitcast.43), kind=kOutput, calls=%fused_computation.4 | convolution fusion | flops 4836556800 | bytes 43266048 | tf_op jit(solution)/shard_map/dot_general | solution.py:76
  114.2 3.3 %collective-permute-done.13 = bf16[128,3072]{1,0:T(8,128)(2,1)} collective-permute-done((bf16[128,3072]{1,0:T(8,128)(2,1)}, bf16[128,3072]{1,0:T(8,128)(2,1)}, u32[]{:S(2)}, u32[]{:S(2)}) %collective-permute-start.13) | collective-permute-done | bytes 786464 | tf_op jit(solution)/shard_map/ppermute | solution.py:42
  117.5 2.3 %collective-permute-done.14 = bf16[64,6144]{1,0:T(8,128)(2,1)S(1)} collective-permute-done((bf16[64,6144]{1,0:T(8,128)(2,1)S(1)}, bf16[64,6144]{1,0:T(8,128)(2,1)S(1)}, u32[]{:S(2)}, u32[]{:S(2)}) %collective-permute-start.14) | collective-permute-done | bytes 786464 | tf_op jit(solution)/shard_map/ppermute | solution.py:36
  123.3 15.0 %fusion.2 = f32[128,6144]{1,0:T(8,128)S(1)} fusion(bf16[1,3072,6144]{2,1,0:T(8,128)(2,1)} %param.12, bf16[128,3072]{1,0:T(8,128)(2,1)} %collective-permute-done.13, f32[256,3072]{1,0:T(8,128)S(1)} %fusion.8, f32[3072]{0:T(1024)S(1)} %bitcast.44), kind=kOutput, calls=%fused_computation.2 | convolution fusion | flops 4836556800 | bytes 43266048 | tf_op jit(solution)/shard_map/dot_general | solution.py:76
  138.4 2.8 %collective-permute-done.16 = bf16[128,3072]{1,0:T(8,128)(2,1)} collective-permute-done((bf16[128,3072]{1,0:T(8,128)(2,1)S(1)}, bf16[128,3072]{1,0:T(8,128)(2,1)}, u32[]{:S(2)}, u32[]{:S(2)}) %collective-permute-start.16) | collective-permute-done | bytes 786464 | tf_op jit(solution)/shard_map/ppermute | solution.py:42
  142.5 2.3 %collective-permute-done.17 = bf16[64,6144]{1,0:T(8,128)(2,1)S(1)} collective-permute-done((bf16[64,6144]{1,0:T(8,128)(2,1)S(1)}, bf16[64,6144]{1,0:T(8,128)(2,1)S(1)}, u32[]{:S(2)}, u32[]{:S(2)}) %collective-permute-start.17) | collective-permute-done | bytes 786464 | tf_op jit(solution)/shard_map/ppermute | solution.py:36
  145.6 15.0 %fusion = f32[128,6144]{1,0:T(8,128)S(1)} fusion(bf16[1,3072,6144]{2,1,0:T(8,128)(2,1)} %param.12, bf16[128,3072]{1,0:T(8,128)(2,1)} %collective-permute-done.16, f32[256,3072]{1,0:T(8,128)S(1)} %fusion.8, f32[3072]{0:T(1024)S(1)} %bitcast.45), kind=kOutput, calls=%fused_computation | convolution fusion | flops 4836556800 | bytes 43266048 | tf_op jit(solution)/shard_map/dot_general | solution.py:76
  160.7 3.9 %collective-permute-done.18 = bf16[64,6144]{1,0:T(8,128)(2,1)S(1)} collective-permute-done((bf16[64,6144]{1,0:T(8,128)(2,1)S(1)}, bf16[64,6144]{1,0:T(8,128)(2,1)S(1)}, u32[]{:S(2)}, u32[]{:S(2)}) %collective-permute-start.18) | collective-permute-done | bytes 786464 | tf_op jit(solution)/shard_map/ppermute | solution.py:29
  164.6 2.3 %collective-permute-done.19 = bf16[64,6144]{1,0:T(8,128)(2,1)S(1)} collective-permute-done((bf16[64,6144]{1,0:T(8,128)(2,1)S(1)}, bf16[64,6144]{1,0:T(8,128)(2,1)S(1)}, u32[]{:S(2)}, u32[]{:S(2)}) %collective-permute-start.19) | collective-permute-done | bytes 786464 | tf_op jit(solution)/shard_map/ppermute | solution.py:36
  167.1 2.5 %collective-permute-start.20 = (bf16[64,6144]{1,0:T(8,128)(2,1)S(1)}, bf16[64,6144]{1,0:T(8,128)(2,1)S(1)}, u32[]{:S(2)}, u32[]{:S(2)}) collective-permute-start(bf16[64,6144]{1,0:T(8,128)(2,1)S(1)} %fusion.58), channel_id=1, source_target_pairs={{0,20},{1,21},{4,22},{5,23},{6,18},{7,19},{2,16},{3,17},{16,4},{17... | collective-permute-start | bytes 2359304 | tf_op jit(solution)/shard_map/ppermute | solution.py:33
  169.6 18.0 %collective-permute-done.20 = bf16[64,6144]{1,0:T(8,128)(2,1)S(1)} collective-permute-done((bf16[64,6144]{1,0:T(8,128)(2,1)S(1)}, bf16[64,6144]{1,0:T(8,128)(2,1)S(1)}, u32[]{:S(2)}, u32[]{:S(2)}) %collective-permute-start.20) | collective-permute-done | bytes 786464 | tf_op jit(solution)/shard_map/ppermute | solution.py:33
  187.7 2.6 %fusion.69 = bf16[1,64,6144]{2,1,0:T(8,128)(2,1)} fusion(bf16[64,6144]{1,0:T(8,128)(2,1)S(1)} %collective-permute-done.20, bf16[64,6144]{1,0:T(8,128)(2,1)} %collective-permute-done.15, bf16[64,6144]{1,0:T(8,128)(2,1)S(1)} %copy-done.5, bf16[64,6144]{1,0:T(8,128)(2,1)} %collective-permute-done.10), kind=kLoop, calls=%fused_computation.86 | loop fusion | flops 3145728 | bytes 3932160 | tf_op jit(solution)/shard_map/broadcast_in_dim | solution.py:141
  (63 shorter events, 23.8 us)
Async XLA Ops:
  1.5 4.5 %collective-permute-start = (f32[2,64]{1,0:T(2,128)S(1)}, f32[2,64]{1,0:T(2,128)S(1)}, u32[]{:S(2)}, u32[]{:S(2)}) collective-permute-start(f32[2,64]{1,0:T(2,128)S(1)} %pad_maximum_fusion), channel_id=1, source_target_pairs={{0,8},{8,0},{1,9},{9,1},{2,10},{10,2},{3,11},{11,3},{4,12},{12,4},... | collective-permute-start | bytes 1544 | tf_op jit(solution)/shard_map/ppermute | solution.py:42
  7.6 3.3 %collective-permute-start.1 = (bf16[64,6144]{1,0:T(8,128)(2,1)S(1)}, bf16[64,6144]{1,0:T(8,128)(2,1)S(1)}, u32[]{:S(2)}, u32[]{:S(2)}) collective-permute-start(bf16[64,6144]{1,0:T(8,128)(2,1)S(1)} %fusion.24), channel_id=1, source_target_pairs={{0,1},{1,0},{2,3},{3,2},{4,5},{5,4},{6,7},{7,6},{8,9},{9,8},{10,11... | collective-permute-start | bytes 2359304 | tf_op jit(solution)/shard_map/ppermute | solution.py:36
  7.7 20.6 %collective-permute-start.3 = (bf16[64,6144]{1,0:T(8,128)(2,1)S(1)}, bf16[64,6144]{1,0:T(8,128)(2,1)S(1)}, u32[]{:S(2)}, u32[]{:S(2)}) collective-permute-start(bf16[64,6144]{1,0:T(8,128)(2,1)S(1)} %fusion.24), channel_id=1, source_target_pairs={{0,4},{1,5},{4,6},{5,7},{6,2},{7,3},{2,0},{3,1},{8,12},{9,13},{12,... | collective-permute-start | bytes 2359304 | tf_op jit(solution)/shard_map/ppermute | solution.py:29
  28.2 3.9 %collective-permute-start.4 = (bf16[64,6144]{1,0:T(8,128)(2,1)S(1)}, bf16[64,6144]{1,0:T(8,128)(2,1)S(1)}, u32[]{:S(2)}, u32[]{:S(2)}) collective-permute-start(bf16[64,6144]{1,0:T(8,128)(2,1)S(1)} %collective-permute-done.3), channel_id=1, source_target_pairs={{0,1},{1,0},{2,3},{3,2},{4,5},{5,4},{6,7},{7,6},{8,9},{9,8},{10,11... | collective-permute-start | bytes 2359304 | tf_op jit(solution)/shard_map/ppermute | solution.py:36
  28.2 21.6 %collective-permute-start.5 = (bf16[64,6144]{1,0:T(8,128)(2,1)S(1)}, bf16[64,6144]{1,0:T(8,128)(2,1)S(1)}, u32[]{:S(2)}, u32[]{:S(2)}) collective-permute-start(bf16[64,6144]{1,0:T(8,128)(2,1)S(1)} %fusion.24), channel_id=1, source_target_pairs={{0,2},{1,3},{4,0},{5,1},{6,4},{7,5},{2,6},{3,7},{8,10},{9,11},{12,... | collective-permute-start | bytes 2359304 | tf_op jit(solution)/shard_map/ppermute | solution.py:29
  30.6 21.1 %copy-start.1 = (bf16[1,64,6144]{2,1,0:T(8,128)(2,1)S(1)}, bf16[1,64,6144]{2,1,0:T(8,128)(2,1)}, u32[]{:S(2)}) copy-start(bf16[1,64,6144]{2,1,0:T(8,128)(2,1)} %param.7) | copy-start | bytes 2359300
  30.6 24.1 %copy-start.2 = (f32[1,3072]{1,0:T(1,128)S(1)}, f32[1,3072]{1,0:T(1,128)}, u32[]{:S(2)}) copy-start(f32[1,3072]{1,0:T(1,128)} %param.11) | copy-start | bytes 36868
  30.6 19.8 %collective-permute-start.2 = (bf16[128,3072]{1,0:T(8,128)(2,1)S(1)}, bf16[128,3072]{1,0:T(8,128)(2,1)}, u32[]{:S(2)}, u32[]{:S(2)}) collective-permute-start(bf16[128,3072]{1,0:T(8,128)(2,1)S(1)} %get-tuple-element.41), channel_id=1, source_target_pairs={{0,8},{8,0},{1,9},{9,1},{2,10},{10,2},{3,11},{11,3},{4,12},{12,4},... | collective-permute-start | bytes 2359304 | tf_op jit(solution)/shard_map/ppermute | solution.py:42
  50.4 19.5 %collective-permute-start.6 = (bf16[64,6144]{1,0:T(8,128)(2,1)S(1)}, bf16[64,6144]{1,0:T(8,128)(2,1)}, u32[]{:S(2)}, u32[]{:S(2)}) collective-permute-start(bf16[64,6144]{1,0:T(8,128)(2,1)S(1)} %collective-permute-done.3), channel_id=1, source_target_pairs={{0,4},{1,5},{4,6},{5,7},{6,2},{7,3},{2,0},{3,1},{8,12},{9,13},{12,... | collective-permute-start | bytes 2359304 | tf_op jit(solution)/shard_map/ppermute | solution.py:29
  51.7 18.9 %collective-permute-start.8 = (bf16[64,6144]{1,0:T(8,128)(2,1)S(1)}, bf16[64,6144]{1,0:T(8,128)(2,1)S(1)}, u32[]{:S(2)}, u32[]{:S(2)}) collective-permute-start(bf16[64,6144]{1,0:T(8,128)(2,1)S(1)} %bitcast.41), channel_id=1, source_target_pairs={{0,16},{16,0},{1,17},{17,1},{2,18},{18,2},{3,19},{19,3},{4,20},{20... | collective-permute-start | bytes 2359304 | tf_op jit(solution)/shard_map/ppermute | solution.py:92
  53.2 18.8 %collective-permute-start.7 = (bf16[128,3072]{1,0:T(8,128)(2,1)}, bf16[128,3072]{1,0:T(8,128)(2,1)S(1)}, u32[]{:S(2)}, u32[]{:S(2)}) collective-permute-start(bf16[128,3072]{1,0:T(8,128)(2,1)} %get-tuple-element.43), channel_id=1, source_target_pairs={{0,8},{8,0},{1,9},{9,1},{2,10},{10,2},{3,11},{11,3},{4,12},{12,4},... | collective-permute-start | bytes 2359304 | tf_op jit(solution)/shard_map/ppermute | solution.py:42
  72.0 2.3 %collective-permute-start.9 = (bf16[64,6144]{1,0:T(8,128)(2,1)S(1)}, bf16[64,6144]{1,0:T(8,128)(2,1)S(1)}, u32[]{:S(2)}, u32[]{:S(2)}) collective-permute-start(bf16[64,6144]{1,0:T(8,128)(2,1)S(1)} %slice.83), channel_id=1, source_target_pairs={{0,1},{1,0},{2,3},{3,2},{4,5},{5,4},{6,7},{7,6},{8,9},{9,8},{10,11... | collective-permute-start | bytes 2359304 | tf_op jit(solution)/shard_map/ppermute | solution.py:36
  75.4 2.5 %collective-permute-start.11 = (bf16[64,6144]{1,0:T(8,128)(2,1)}, bf16[64,6144]{1,0:T(8,128)(2,1)S(1)}, u32[]{:S(2)}, u32[]{:S(2)}) collective-permute-start(bf16[64,6144]{1,0:T(8,128)(2,1)} %collective-permute-done.6), channel_id=1, source_target_pairs={{0,1},{1,0},{2,3},{3,2},{4,5},{5,4},{6,7},{7,6},{8,9},{9,8},{10,11... | collective-permute-start | bytes 2359304 | tf_op jit(solution)/shard_map/ppermute | solution.py:36
  75.6 3.4 %collective-permute-start.12 = (bf16[64,6144]{1,0:T(8,128)(2,1)S(1)}, bf16[64,6144]{1,0:T(8,128)(2,1)}, u32[]{:S(2)}, u32[]{:S(2)}) collective-permute-start(bf16[64,6144]{1,0:T(8,128)(2,1)S(1)} %copy-done.9), channel_id=1, source_target_pairs={{0,1},{1,0},{2,3},{3,2},{4,5},{5,4},{6,7},{7,6},{8,9},{9,8},{10,11... | collective-permute-start | bytes 2359304 | tf_op jit(solution)/shard_map/ppermute | solution.py:36
  75.9 38.3 %collective-permute-start.10 = (bf16[64,6144]{1,0:T(8,128)(2,1)}, bf16[64,6144]{1,0:T(8,128)(2,1)}, u32[]{:S(2)}, u32[]{:S(2)}) collective-permute-start(bf16[64,6144]{1,0:T(8,128)(2,1)} %fusion.62), channel_id=1, source_target_pairs={{0,16},{16,0},{1,17},{17,1},{2,18},{18,2},{3,19},{19,3},{4,20},{20... | collective-permute-start | bytes 2359304 | tf_op jit(solution)/shard_map/ppermute | solution.py:97
  97.6 19.9 %collective-permute-start.13 = (bf16[128,3072]{1,0:T(8,128)(2,1)}, bf16[128,3072]{1,0:T(8,128)(2,1)}, u32[]{:S(2)}, u32[]{:S(2)}) collective-permute-start(bf16[128,3072]{1,0:T(8,128)(2,1)} %get-tuple-element.39), channel_id=1, source_target_pairs={{0,8},{8,0},{1,9},{9,1},{2,10},{10,2},{3,11},{11,3},{4,12},{12,4},... | collective-permute-start | bytes 2359304 | tf_op jit(solution)/shard_map/ppermute | solution.py:42
  117.5 2.3 %collective-permute-start.14 = (bf16[64,6144]{1,0:T(8,128)(2,1)S(1)}, bf16[64,6144]{1,0:T(8,128)(2,1)S(1)}, u32[]{:S(2)}, u32[]{:S(2)}) collective-permute-start(bf16[64,6144]{1,0:T(8,128)(2,1)S(1)} %slice.82), channel_id=1, source_target_pairs={{0,1},{1,0},{2,3},{3,2},{4,5},{5,4},{6,7},{7,6},{8,9},{9,8},{10,11... | collective-permute-start | bytes 2359304 | tf_op jit(solution)/shard_map/ppermute | solution.py:36
  120.8 21.7 %collective-permute-start.15 = (bf16[64,6144]{1,0:T(8,128)(2,1)}, bf16[64,6144]{1,0:T(8,128)(2,1)}, u32[]{:S(2)}, u32[]{:S(2)}) collective-permute-start(bf16[64,6144]{1,0:T(8,128)(2,1)} %fusion.60), channel_id=1, source_target_pairs={{0,18},{1,19},{4,16},{5,17},{6,20},{7,21},{2,22},{3,23},{16,2},{17... | collective-permute-start | bytes 2359304 | tf_op jit(solution)/shard_map/ppermute | solution.py:33
  121.8 19.4 %collective-permute-start.16 = (bf16[128,3072]{1,0:T(8,128)(2,1)S(1)}, bf16[128,3072]{1,0:T(8,128)(2,1)}, u32[]{:S(2)}, u32[]{:S(2)}) collective-permute-start(bf16[128,3072]{1,0:T(8,128)(2,1)S(1)} %copy-done.3), channel_id=1, source_target_pairs={{0,8},{8,0},{1,9},{9,1},{2,10},{10,2},{3,11},{11,3},{4,12},{12,4},... | collective-permute-start | bytes 2359304 | tf_op jit(solution)/shard_map/ppermute | solution.py:42
  142.5 2.3 %collective-permute-start.17 = (bf16[64,6144]{1,0:T(8,128)(2,1)S(1)}, bf16[64,6144]{1,0:T(8,128)(2,1)S(1)}, u32[]{:S(2)}, u32[]{:S(2)}) collective-permute-start(bf16[64,6144]{1,0:T(8,128)(2,1)S(1)} %slice.81), channel_id=1, source_target_pairs={{0,1},{1,0},{2,3},{3,2},{4,5},{5,4},{6,7},{7,6},{8,9},{9,8},{10,11... | collective-permute-start | bytes 2359304 | tf_op jit(solution)/shard_map/ppermute | solution.py:36
  145.0 19.6 %collective-permute-start.18 = (bf16[64,6144]{1,0:T(8,128)(2,1)S(1)}, bf16[64,6144]{1,0:T(8,128)(2,1)S(1)}, u32[]{:S(2)}, u32[]{:S(2)}) collective-permute-start(bf16[64,6144]{1,0:T(8,128)(2,1)S(1)} %fusion.59), channel_id=1, source_target_pairs={{0,4},{1,5},{4,6},{5,7},{6,2},{7,3},{2,0},{3,1},{8,12},{9,13},{12,... | collective-permute-start | bytes 2359304 | tf_op jit(solution)/shard_map/ppermute | solution.py:29
  160.7 27.0 %copy-start.5 = (bf16[64,6144]{1,0:T(8,128)(2,1)S(1)}, bf16[64,6144]{1,0:T(8,128)(2,1)}, u32[]{:S(2)}) copy-start(bf16[64,6144]{1,0:T(8,128)(2,1)} %copy-done.4) | copy-start | bytes 2359300
  164.6 2.3 %collective-permute-start.19 = (bf16[64,6144]{1,0:T(8,128)(2,1)S(1)}, bf16[64,6144]{1,0:T(8,128)(2,1)S(1)}, u32[]{:S(2)}, u32[]{:S(2)}) collective-permute-start(bf16[64,6144]{1,0:T(8,128)(2,1)S(1)} %slice.80), channel_id=1, source_target_pairs={{0,1},{1,0},{2,3},{3,2},{4,5},{5,4},{6,7},{7,6},{8,9},{9,8},{10,11... | collective-permute-start | bytes 2359304 | tf_op jit(solution)/shard_map/ppermute | solution.py:36
  167.1 20.5 %collective-permute-start.20 = (bf16[64,6144]{1,0:T(8,128)(2,1)S(1)}, bf16[64,6144]{1,0:T(8,128)(2,1)S(1)}, u32[]{:S(2)}, u32[]{:S(2)}) collective-permute-start(bf16[64,6144]{1,0:T(8,128)(2,1)S(1)} %fusion.58), channel_id=1, source_target_pairs={{0,20},{1,21},{4,22},{5,23},{6,18},{7,19},{2,16},{3,17},{16,4},{17... | collective-permute-start | bytes 2359304 | tf_op jit(solution)/shard_map/ppermute | solution.py:33
  (8 other events, 32.7 us)

commit v7 on v6

--- a/solution.py
+++ b/solution.py
@@ -75,7 +75,7 @@
         def down(offset, done, over):
             part = jnp.dot(act(offset, done), down_weight[0], preferred_element_type=F32)
             theirs = tie(part[rows:].astype(BF16), over)
-            return part[:rows] + sibling(theirs).astype(F32)
+            return part[:rows] + sibling(theirs).astype(F32), theirs
 
         pre = up([normed])
         pres[0] = (pre, from_others(pre.astype(BF16)))
@@ -89,12 +89,8 @@
         for k in range(2, ahead + 1):
             ahead_blocks[chips - k] = front = shift(front, 1)
         pres[chips - 1] = (pre, from_others(pre.astype(BF16)))
-        residual = lax.ppermute(tie(incoming[0], pre), "section", turn)
-
-        own = down(0, (pre, back_blocks), (ahead_blocks, pres[chips - 1][1], residual))
-        own = (own + down_bias[0]).astype(BF16)
-        done = own
-        own = lax.ppermute(own, "section", turn)
+        own, done = down(0, (pre, back_blocks), (ahead_blocks, pres[chips - 1][1]))
+        own = lax.ppermute((own + down_bias[0] + x).astype(BF16), "section", turn)
 
         along = [(k, 1) for k in range(ahead, 0, -1)]
         against = [(chips - k, -1) for k in range(chips - ahead - 1, 0, -1)]
@@ -125,7 +121,7 @@
         coming = exchange(1)
         sums, arrived, over = {}, [], own
         for place, (offset, way) in enumerate(downs):
-            summed = down(offset, done, (over, coming))
+            summed, _ = down(offset, done, (over, coming))
             if way in sums:
                 summed = summed + sums[way].astype(F32)
             done = summed = summed.astype(BF16)
@@ -134,8 +130,8 @@
                 arrived.append(over)
             else:
                 over = sums[way] = shift(summed, way)
-            coming = exchange(place + 2, summed)
-        result = own.astype(F32) + residual.astype(F32)
+            coming = exchange(place + 2, coming)
+        result = own.astype(F32)
         for value in arrived:
             result = result + value.astype(F32)
         return result.astype(BF16)[None]

time: 191 us -> 190 us (level)
    ppermute x2, waiting for transfers between devices: 19.4 us -> 23.6 us  [shift_and_turn(): return lax.ppermute(block, ('section', 'tensor'), route)]
    ppermute x5, waiting for transfers between devices: 9.66 us -> 6.84 us  [from_others(): got = lax.ppermute(sent, 'dp', route)]
    ppermute x8, waiting for transfers between devices: 10.8 us -> 8.22 us  [sibling(): return lax.ppermute(block, 'tensor', swap)]
  transfers between devices with their start and end apart: 21 -> 20, of which waited for: 17 -> 15; matrix products, arithmetic and copies ran while one was open for 57% -> 58% of each run, Pallas kernels for 0% -> 0%
where the time goes in v7:
time: 190 us; the launch traced here: 189 us
  matrix products  107 us (56%)
  waiting for transfers between devices  49.6 us (26%)
  starting transfers between devices  21.4 us (11%)
  other arithmetic  9.06 us (5%)
  local copies, waits for them, and re-layouts  2.59 us (1%)
    dot_general x4, matrix products, down(): jnp.dot(act(offset, done), down_weight[0], preferred_element_type=F32)  59.9 us
    dot_general x3, matrix products, up(): return jnp.dot(both, up_weight[0], preferred_element_type=F32)  46.7 us
    ppermute x2, waiting for transfers between devices, shift_and_turn(): return lax.ppermute(block, ('section', 'tensor'), route)  23.6 us
    ppermute x4, waiting for transfers between devices, shift(): return lax.ppermute(block, 'tensor', hops(way))  11 us
    ppermute x5, starting transfers between devices, from_others(): got = lax.ppermute(sent, 'dp', route)  8.96 us
    ppermute x8, waiting for transfers between devices, sibling(): return lax.ppermute(block, 'tensor', swap)  8.22 us
    ppermute x4, starting transfers between devices, shift(): return lax.ppermute(block, 'tensor', hops(way))  7.67 us
    ppermute x5, waiting for transfers between devices, from_others(): got = lax.ppermute(sent, 'dp', route)  6.84 us
  transfers between devices with their start and end apart: 20, of which 15 were waited for; matrix products, arithmetic and copies ran while one was open for 58% of the time, Pallas kernels for 0%

profile of v7, /device:TPU:0, one launch (start us, length us, event | category | flops | bytes accessed | tf_op | source)
XLA Modules:
  0.0 189.4 jit_solution(2167301695673753415)
XLA Ops:
  1.5 3.0 %collective-permute-start = (f32[2,64]{1,0:T(2,128)S(1)}, f32[2,64]{1,0:T(2,128)S(1)}, u32[]{:S(2)}, u32[]{:S(2)}) collective-permute-start(f32[2,64]{1,0:T(2,128)S(1)} %pad_maximum_fusion), channel_id=1, source_target_pairs={{0,8},{8,0},{1,9},{9,1},{2,10},{10,2},{3,11},{11,3},{4,12},{12,4},... | collective-permute-start | bytes 1544 | tf_op jit(solution)/shard_map/ppermute | solution.py:42
  4.5 1.5 collective-permute-done
  6.1 1.5 fusion.56
  7.6 3.2 %collective-permute-start.3 = (bf16[64,6144]{1,0:T(8,128)(2,1)S(1)}, bf16[64,6144]{1,0:T(8,128)(2,1)S(1)}, u32[]{:S(2)}, u32[]{:S(2)}) collective-permute-start(bf16[64,6144]{1,0:T(8,128)(2,1)S(1)} %fusion.56), channel_id=1, source_target_pairs={{0,4},{1,5},{4,6},{5,7},{6,2},{7,3},{2,0},{3,1},{8,12},{9,13},{12,... | collective-permute-start | bytes 2359304 | tf_op jit(solution)/shard_map/ppermute | solution.py:29
  10.8 14.4 %fusion.117 = (bf16[128,3072]{1,0:T(8,128)(2,1)S(1)}, f32[128,3072]{1,0:T(8,128)S(1)}) fusion(bf16[1,6144,3072]{2,1,0:T(8,128)(2,1)} %param.10, bf16[64,6144]{1,0:T(8,128)(2,1)S(1)} %collective-permute-done.1, bf16[64,6144]{1,0:T(8,128)(2,1)S(1)} %fusion.56), kind=kOutput, calls=%fused_computation.135 | convolution fusion | flops 4835377152 | bytes 41680896 | tf_op jit(solution)/shard_map/dot_general | solution.py:68
  25.2 3.0 %collective-permute-done.3 = bf16[64,6144]{1,0:T(8,128)(2,1)S(1)} collective-permute-done((bf16[64,6144]{1,0:T(8,128)(2,1)S(1)}, bf16[64,6144]{1,0:T(8,128)(2,1)S(1)}, u32[]{:S(2)}, u32[]{:S(2)}) %collective-permute-start.3) | collective-permute-done | bytes 786464 | tf_op jit(solution)/shard_map/ppermute | solution.py:29
  28.2 2.4 %collective-permute-start.5 = (bf16[64,6144]{1,0:T(8,128)(2,1)S(1)}, bf16[64,6144]{1,0:T(8,128)(2,1)}, u32[]{:S(2)}, u32[]{:S(2)}) collective-permute-start(bf16[64,6144]{1,0:T(8,128)(2,1)S(1)} %fusion.56), channel_id=1, source_target_pairs={{0,2},{1,3},{4,0},{5,1},{6,4},{7,5},{2,6},{3,7},{8,10},{9,11},{12,... | collective-permute-start | bytes 2359304 | tf_op jit(solution)/shard_map/ppermute | solution.py:29
  32.1 15.1 %fusion.118 = (bf16[128,3072]{1,0:T(8,128)(2,1)S(1)}, f32[128,3072]{1,0:T(8,128)}) fusion(bf16[1,6144,3072]{2,1,0:T(8,128)(2,1)} %param.10, bf16[64,6144]{1,0:T(8,128)(2,1)S(1)} %collective-permute-done.4, bf16[64,6144]{1,0:T(8,128)(2,1)S(1)} %collective-permute-done.3), kind=kOutput, calls=%fused_computation.136 | convolution fusion | flops 4835377152 | bytes 41680896 | tf_op jit(solution)/shard_map/dot_general | solution.py:68
  47.2 2.8 %collective-permute-done.5 = bf16[64,6144]{1,0:T(8,128)(2,1)} collective-permute-done((bf16[64,6144]{1,0:T(8,128)(2,1)S(1)}, bf16[64,6144]{1,0:T(8,128)(2,1)}, u32[]{:S(2)}, u32[]{:S(2)}) %collective-permute-start.5) | collective-permute-done | bytes 786464 | tf_op jit(solution)/shard_map/ppermute | solution.py:29
  53.2 14.8 %fusion.6 = f32[128,6144]{1,0:T(8,128)S(1)} fusion(bf16[1,3072,6144]{2,1,0:T(8,128)(2,1)} %param.12, f32[128,3072]{1,0:T(8,128)S(1)} %get-tuple-element.40, bf16[128,3072]{1,0:T(8,128)(2,1)S(1)} %collective-permute-done.2, f32[3072]{0:T(1024)S(1)} %bitcast.43), kind=kOutput, calls=%fused_computation.6 | convolution fusion | flops 4836556800 | bytes 43266048 | tf_op jit(solution)/shard_map/dot_general | solution.py:76
  71.1 2.9 %collective-permute-done.8 = bf16[64,6144]{1,0:T(8,128)(2,1)S(1)} collective-permute-done((bf16[64,6144]{1,0:T(8,128)(2,1)S(1)}, bf16[64,6144]{1,0:T(8,128)(2,1)S(1)}, u32[]{:S(2)}, u32[]{:S(2)}) %collective-permute-start.8) | collective-permute-done | bytes 786464 | tf_op jit(solution)/shard_map/ppermute | solution.py:36
  75.1 1.5 collective-permute-start.9
  77.5 17.3 %fusion.8 = f32[256,3072]{1,0:T(8,128)S(1)} fusion(bf16[1,6144,3072]{2,1,0:T(8,128)(2,1)} %param.10, bf16[64,6144]{1,0:T(8,128)(2,1)} %collective-permute-done.11, bf16[64,6144]{1,0:T(8,128)(2,1)} %collective-permute-done.5, bf16[64,6144]{1,0:T(8,128)(2,1)} %copy-done.5, bf16[64,6144]{1,0:T(8,128)(2,1)} %collective-permute-done.6), kind=kOutput, calls=%fused_computation.8 | convolution fusion | flops 9676259328 | bytes 44040192 | tf_op jit(solution)/shard_map/dot_general | solution.py:68
  97.7 15.1 %fusion.4 = f32[128,6144]{1,0:T(8,128)S(1)} fusion(bf16[1,3072,6144]{2,1,0:T(8,128)(2,1)} %param.12, f32[128,3072]{1,0:T(8,128)S(1)} %copy-done.1, bf16[128,3072]{1,0:T(8,128)(2,1)} %copy-done.3, f32[3072]{0:T(1024)S(1)} %bitcast.44), kind=kOutput, calls=%fused_computation.4 | convolution fusion | flops 4836556800 | bytes 43266048 | tf_op jit(solution)/shard_map/dot_general | solution.py:76
  112.8 3.0 %collective-permute-done.12 = bf16[128,3072]{1,0:T(8,128)(2,1)} collective-permute-done((bf16[128,3072]{1,0:T(8,128)(2,1)}, bf16[128,3072]{1,0:T(8,128)(2,1)}, u32[]{:S(2)}, u32[]{:S(2)}) %collective-permute-start.12) | collective-permute-done | bytes 786464 | tf_op jit(solution)/shard_map/ppermute | solution.py:42
  120.1 15.0 %fusion.2 = f32[128,6144]{1,0:T(8,128)S(1)} fusion(bf16[1,3072,6144]{2,1,0:T(8,128)(2,1)} %param.12, bf16[128,3072]{1,0:T(8,128)(2,1)} %collective-permute-done.12, f32[256,3072]{1,0:T(8,128)S(1)} %fusion.8, f32[3072]{0:T(1024)S(1)} %bitcast.45), kind=kOutput, calls=%fused_computation.2 | convolution fusion | flops 4836556800 | bytes 43266048 | tf_op jit(solution)/shard_map/dot_general | solution.py:76
  136.1 4.6 %collective-permute-done.14 = bf16[64,6144]{1,0:T(8,128)(2,1)S(1)} collective-permute-done((bf16[64,6144]{1,0:T(8,128)(2,1)}, bf16[64,6144]{1,0:T(8,128)(2,1)S(1)}, u32[]{:S(2)}, u32[]{:S(2)}) %collective-permute-start.14) | collective-permute-done | bytes 786464 | tf_op jit(solution)/shard_map/ppermute | solution.py:33
  140.7 2.3 %collective-permute-done.16 = bf16[64,6144]{1,0:T(8,128)(2,1)S(1)} collective-permute-done((bf16[64,6144]{1,0:T(8,128)(2,1)S(1)}, bf16[64,6144]{1,0:T(8,128)(2,1)S(1)}, u32[]{:S(2)}, u32[]{:S(2)}) %collective-permute-start.16) | collective-permute-done | bytes 786464 | tf_op jit(solution)/shard_map/ppermute | solution.py:36
  143.9 15.0 %fusion = f32[128,6144]{1,0:T(8,128)S(1)} fusion(bf16[1,3072,6144]{2,1,0:T(8,128)(2,1)} %param.12, bf16[128,3072]{1,0:T(8,128)(2,1)} %collective-permute-done.15, f32[256,3072]{1,0:T(8,128)S(1)} %fusion.8, f32[3072]{0:T(1024)S(1)} %bitcast.46), kind=kOutput, calls=%fused_computation | convolution fusion | flops 4836556800 | bytes 43266048 | tf_op jit(solution)/shard_map/dot_general | solution.py:76
  159.0 3.9 %collective-permute-done.17 = bf16[64,6144]{1,0:T(8,128)(2,1)} collective-permute-done((bf16[64,6144]{1,0:T(8,128)(2,1)S(1)}, bf16[64,6144]{1,0:T(8,128)(2,1)}, u32[]{:S(2)}, u32[]{:S(2)}) %collective-permute-start.17) | collective-permute-done | bytes 786464 | tf_op jit(solution)/shard_map/ppermute | solution.py:29
  162.9 2.3 %collective-permute-done.18 = bf16[64,6144]{1,0:T(8,128)(2,1)S(1)} collective-permute-done((bf16[64,6144]{1,0:T(8,128)(2,1)S(1)}, bf16[64,6144]{1,0:T(8,128)(2,1)S(1)}, u32[]{:S(2)}, u32[]{:S(2)}) %collective-permute-start.18) | collective-permute-done | bytes 786464 | tf_op jit(solution)/shard_map/ppermute | solution.py:36
  166.6 1.6 collective-permute-start.19
  168.2 19.0 %collective-permute-done.19 = bf16[64,6144]{1,0:T(8,128)(2,1)S(1)} collective-permute-done((bf16[64,6144]{1,0:T(8,128)(2,1)S(1)}, bf16[64,6144]{1,0:T(8,128)(2,1)S(1)}, u32[]{:S(2)}, u32[]{:S(2)}) %collective-permute-start.19) | collective-permute-done | bytes 786464 | tf_op jit(solution)/shard_map/ppermute | solution.py:33
  187.1 2.3 %fusion.69 = bf16[1,64,6144]{2,1,0:T(8,128)(2,1)} fusion(bf16[64,6144]{1,0:T(8,128)(2,1)S(1)} %collective-permute-done.19, bf16[64,6144]{1,0:T(8,128)(2,1)S(1)} %collective-permute-done.14, bf16[64,6144]{1,0:T(8,128)(2,1)} %collective-permute-done.9), kind=kLoop, calls=%fused_computation.88 | loop fusion | flops 2359296 | bytes 3145728 | tf_op jit(solution)/shard_map/broadcast_in_dim | solution.py:137
  (51 shorter events, 22.0 us)
Async XLA Ops:
  1.5 4.5 %collective-permute-start = (f32[2,64]{1,0:T(2,128)S(1)}, f32[2,64]{1,0:T(2,128)S(1)}, u32[]{:S(2)}, u32[]{:S(2)}) collective-permute-start(f32[2,64]{1,0:T(2,128)S(1)} %pad_maximum_fusion), channel_id=1, source_target_pairs={{0,8},{8,0},{1,9},{9,1},{2,10},{10,2},{3,11},{11,3},{4,12},{12,4},... | collective-permute-start | bytes 1544 | tf_op jit(solution)/shard_map/ppermute | solution.py:42
  7.6 3.3 %collective-permute-start.1 = (bf16[64,6144]{1,0:T(8,128)(2,1)S(1)}, bf16[64,6144]{1,0:T(8,128)(2,1)S(1)}, u32[]{:S(2)}, u32[]{:S(2)}) collective-permute-start(bf16[64,6144]{1,0:T(8,128)(2,1)S(1)} %fusion.56), channel_id=1, source_target_pairs={{0,1},{1,0},{2,3},{3,2},{4,5},{5,4},{6,7},{7,6},{8,9},{9,8},{10,11... | collective-permute-start | bytes 2359304 | tf_op jit(solution)/shard_map/ppermute | solution.py:36
  7.6 20.6 %collective-permute-start.3 = (bf16[64,6144]{1,0:T(8,128)(2,1)S(1)}, bf16[64,6144]{1,0:T(8,128)(2,1)S(1)}, u32[]{:S(2)}, u32[]{:S(2)}) collective-permute-start(bf16[64,6144]{1,0:T(8,128)(2,1)S(1)} %fusion.56), channel_id=1, source_target_pairs={{0,4},{1,5},{4,6},{5,7},{6,2},{7,3},{2,0},{3,1},{8,12},{9,13},{12,... | collective-permute-start | bytes 2359304 | tf_op jit(solution)/shard_map/ppermute | solution.py:29
  28.2 3.9 %collective-permute-start.4 = (bf16[64,6144]{1,0:T(8,128)(2,1)S(1)}, bf16[64,6144]{1,0:T(8,128)(2,1)S(1)}, u32[]{:S(2)}, u32[]{:S(2)}) collective-permute-start(bf16[64,6144]{1,0:T(8,128)(2,1)S(1)} %collective-permute-done.3), channel_id=1, source_target_pairs={{0,1},{1,0},{2,3},{3,2},{4,5},{5,4},{6,7},{7,6},{8,9},{9,8},{10,11... | collective-permute-start | bytes 2359304 | tf_op jit(solution)/shard_map/ppermute | solution.py:36
  28.2 21.7 %collective-permute-start.5 = (bf16[64,6144]{1,0:T(8,128)(2,1)S(1)}, bf16[64,6144]{1,0:T(8,128)(2,1)}, u32[]{:S(2)}, u32[]{:S(2)}) collective-permute-start(bf16[64,6144]{1,0:T(8,128)(2,1)S(1)} %fusion.56), channel_id=1, source_target_pairs={{0,2},{1,3},{4,0},{5,1},{6,4},{7,5},{2,6},{3,7},{8,10},{9,11},{12,... | collective-permute-start | bytes 2359304 | tf_op jit(solution)/shard_map/ppermute | solution.py:29
  30.6 22.6 %copy-start.2 = (f32[1,3072]{1,0:T(1,128)S(1)}, f32[1,3072]{1,0:T(1,128)}, u32[]{:S(2)}) copy-start(f32[1,3072]{1,0:T(1,128)} %param.11) | copy-start | bytes 36868
  30.6 19.7 %collective-permute-start.2 = (bf16[128,3072]{1,0:T(8,128)(2,1)S(1)}, bf16[128,3072]{1,0:T(8,128)(2,1)S(1)}, u32[]{:S(2)}, u32[]{:S(2)}) collective-permute-start(bf16[128,3072]{1,0:T(8,128)(2,1)S(1)} %get-tuple-element.39), channel_id=1, source_target_pairs={{0,8},{8,0},{1,9},{9,1},{2,10},{10,2},{3,11},{11,3},{4,12},{12,4},... | collective-permute-start | bytes 2359304 | tf_op jit(solution)/shard_map/ppermute | solution.py:42
  50.3 19.1 %collective-permute-start.6 = (bf16[64,6144]{1,0:T(8,128)(2,1)S(1)}, bf16[64,6144]{1,0:T(8,128)(2,1)}, u32[]{:S(2)}, u32[]{:S(2)}) collective-permute-start(bf16[64,6144]{1,0:T(8,128)(2,1)S(1)} %collective-permute-done.3), channel_id=1, source_target_pairs={{0,4},{1,5},{4,6},{5,7},{6,2},{7,3},{2,0},{3,1},{8,12},{9,13},{12,... | collective-permute-start | bytes 2359304 | tf_op jit(solution)/shard_map/ppermute | solution.py:29
  51.7 18.9 %collective-permute-start.7 = (bf16[128,3072]{1,0:T(8,128)(2,1)S(1)}, bf16[128,3072]{1,0:T(8,128)(2,1)S(1)}, u32[]{:S(2)}, u32[]{:S(2)}) collective-permute-start(bf16[128,3072]{1,0:T(8,128)(2,1)S(1)} %get-tuple-element.41), channel_id=1, source_target_pairs={{0,8},{8,0},{1,9},{9,1},{2,10},{10,2},{3,11},{11,3},{4,12},{12,4},... | collective-permute-start | bytes 2359304 | tf_op jit(solution)/shard_map/ppermute | solution.py:42
  68.0 6.0 %copy-start = (bf16[1,64,6144]{2,1,0:T(8,128)(2,1)S(1)}, bf16[1,64,6144]{2,1,0:T(8,128)(2,1)}, u32[]{:S(2)}) copy-start(bf16[1,64,6144]{2,1,0:T(8,128)(2,1)} %param.7) | copy-start | bytes 2359300
  68.0 6.0 %copy-start.4 = (f32[1,6144]{1,0:T(1,128)S(1)}, f32[1,6144]{1,0:T(1,128)}, u32[]{:S(2)}) copy-start(f32[1,6144]{1,0:T(1,128)} %param.13) | copy-start | bytes 73732
  70.6 4.6 %copy-start.3 = (bf16[128,3072]{1,0:T(8,128)(2,1)}, bf16[128,3072]{1,0:T(8,128)(2,1)S(1)}, u32[]{:S(2)}) copy-start(bf16[128,3072]{1,0:T(8,128)(2,1)S(1)} %collective-permute-done.7) | copy-start | bytes 2359300
  70.6 3.4 %collective-permute-start.8 = (bf16[64,6144]{1,0:T(8,128)(2,1)S(1)}, bf16[64,6144]{1,0:T(8,128)(2,1)S(1)}, u32[]{:S(2)}, u32[]{:S(2)}) collective-permute-start(bf16[64,6144]{1,0:T(8,128)(2,1)S(1)} %slice.83), channel_id=1, source_target_pairs={{0,1},{1,0},{2,3},{3,2},{4,5},{5,4},{6,7},{7,6},{8,9},{9,8},{10,11... | collective-permute-start | bytes 2359304 | tf_op jit(solution)/shard_map/ppermute | solution.py:36
  70.6 6.1 %collective-permute-start.10 = (bf16[64,6144]{1,0:T(8,128)(2,1)}, bf16[64,6144]{1,0:T(8,128)(2,1)S(1)}, u32[]{:S(2)}, u32[]{:S(2)}) collective-permute-start(bf16[64,6144]{1,0:T(8,128)(2,1)} %collective-permute-done.6), channel_id=1, source_target_pairs={{0,1},{1,0},{2,3},{3,2},{4,5},{5,4},{6,7},{7,6},{8,9},{9,8},{10,11... | collective-permute-start | bytes 2359304 | tf_op jit(solution)/shard_map/ppermute | solution.py:36
  71.1 6.4 %collective-permute-start.11 = (bf16[64,6144]{1,0:T(8,128)(2,1)}, bf16[64,6144]{1,0:T(8,128)(2,1)}, u32[]{:S(2)}, u32[]{:S(2)}) collective-permute-start(bf16[64,6144]{1,0:T(8,128)(2,1)} %collective-permute-done.5), channel_id=1, source_target_pairs={{0,1},{1,0},{2,3},{3,2},{4,5},{5,4},{6,7},{7,6},{8,9},{9,8},{10,11... | collective-permute-start | bytes 2359304 | tf_op jit(solution)/shard_map/ppermute | solution.py:36
  75.1 37.7 %collective-permute-start.9 = (bf16[64,6144]{1,0:T(8,128)(2,1)}, bf16[64,6144]{1,0:T(8,128)(2,1)}, u32[]{:S(2)}, u32[]{:S(2)}) collective-permute-start(bf16[64,6144]{1,0:T(8,128)(2,1)} %fusion.57), channel_id=1, source_target_pairs={{0,16},{16,0},{1,17},{17,1},{2,18},{18,2},{3,19},{19,3},{4,20},{20... | collective-permute-start | bytes 2359304 | tf_op jit(solution)/shard_map/ppermute | solution.py:93
  96.2 19.6 %collective-permute-start.12 = (bf16[128,3072]{1,0:T(8,128)(2,1)}, bf16[128,3072]{1,0:T(8,128)(2,1)}, u32[]{:S(2)}, u32[]{:S(2)}) collective-permute-start(bf16[128,3072]{1,0:T(8,128)(2,1)} %get-tuple-element.37), channel_id=1, source_target_pairs={{0,8},{8,0},{1,9},{9,1},{2,10},{10,2},{3,11},{11,3},{4,12},{12,4},... | collective-permute-start | bytes 2359304 | tf_op jit(solution)/shard_map/ppermute | solution.py:42
  115.8 2.3 %collective-permute-start.13 = (bf16[64,6144]{1,0:T(8,128)(2,1)S(1)}, bf16[64,6144]{1,0:T(8,128)(2,1)S(1)}, u32[]{:S(2)}, u32[]{:S(2)}) collective-permute-start(bf16[64,6144]{1,0:T(8,128)(2,1)S(1)} %slice.82), channel_id=1, source_target_pairs={{0,1},{1,0},{2,3},{3,2},{4,5},{5,4},{6,7},{7,6},{8,9},{9,8},{10,11... | collective-permute-start | bytes 2359304 | tf_op jit(solution)/shard_map/ppermute | solution.py:36
  115.8 20.3 %collective-permute-start.15 = (bf16[128,3072]{1,0:T(8,128)(2,1)}, bf16[128,3072]{1,0:T(8,128)(2,1)}, u32[]{:S(2)}, u32[]{:S(2)}) collective-permute-start(bf16[128,3072]{1,0:T(8,128)(2,1)} %get-tuple-element.32), channel_id=1, source_target_pairs={{0,8},{8,0},{1,9},{9,1},{2,10},{10,2},{3,11},{11,3},{4,12},{12,4},... | collective-permute-start | bytes 2359304 | tf_op jit(solution)/shard_map/ppermute | solution.py:42
  119.1 21.6 %collective-permute-start.14 = (bf16[64,6144]{1,0:T(8,128)(2,1)}, bf16[64,6144]{1,0:T(8,128)(2,1)S(1)}, u32[]{:S(2)}, u32[]{:S(2)}) collective-permute-start(bf16[64,6144]{1,0:T(8,128)(2,1)} %fusion.61), channel_id=1, source_target_pairs={{0,18},{1,19},{4,16},{5,17},{6,20},{7,21},{2,22},{3,23},{16,2},{17... | collective-permute-start | bytes 2359304 | tf_op jit(solution)/shard_map/ppermute | solution.py:33
  140.7 2.3 %collective-permute-start.16 = (bf16[64,6144]{1,0:T(8,128)(2,1)S(1)}, bf16[64,6144]{1,0:T(8,128)(2,1)S(1)}, u32[]{:S(2)}, u32[]{:S(2)}) collective-permute-start(bf16[64,6144]{1,0:T(8,128)(2,1)S(1)} %slice.81), channel_id=1, source_target_pairs={{0,1},{1,0},{2,3},{3,2},{4,5},{5,4},{6,7},{7,6},{8,9},{9,8},{10,11... | collective-permute-start | bytes 2359304 | tf_op jit(solution)/shard_map/ppermute | solution.py:36
  143.1 19.7 %collective-permute-start.17 = (bf16[64,6144]{1,0:T(8,128)(2,1)S(1)}, bf16[64,6144]{1,0:T(8,128)(2,1)}, u32[]{:S(2)}, u32[]{:S(2)}) collective-permute-start(bf16[64,6144]{1,0:T(8,128)(2,1)S(1)} %fusion.60), channel_id=1, source_target_pairs={{0,4},{1,5},{4,6},{5,7},{6,2},{7,3},{2,0},{3,1},{8,12},{9,13},{12,... | collective-permute-start | bytes 2359304 | tf_op jit(solution)/shard_map/ppermute | solution.py:29
  162.9 2.3 %collective-permute-start.18 = (bf16[64,6144]{1,0:T(8,128)(2,1)S(1)}, bf16[64,6144]{1,0:T(8,128)(2,1)S(1)}, u32[]{:S(2)}, u32[]{:S(2)}) collective-permute-start(bf16[64,6144]{1,0:T(8,128)(2,1)S(1)} %slice.80), channel_id=1, source_target_pairs={{0,1},{1,0},{2,3},{3,2},{4,5},{5,4},{6,7},{7,6},{8,9},{9,8},{10,11... | collective-permute-start | bytes 2359304 | tf_op jit(solution)/shard_map/ppermute | solution.py:36
  166.6 20.5 %collective-permute-start.19 = (bf16[64,6144]{1,0:T(8,128)(2,1)S(1)}, bf16[64,6144]{1,0:T(8,128)(2,1)S(1)}, u32[]{:S(2)}, u32[]{:S(2)}) collective-permute-start(bf16[64,6144]{1,0:T(8,128)(2,1)S(1)} %fusion.59), channel_id=1, source_target_pairs={{0,20},{1,21},{4,22},{5,23},{6,18},{7,19},{2,16},{3,17},{16,4},{17... | collective-permute-start | bytes 2359304 | tf_op jit(solution)/shard_map/ppermute | solution.py:33
  (2 other events, 3.8 us)

commit v8 on v4

--- a/solution.py
+++ b/solution.py
@@ -81,11 +81,10 @@
             return lax.ppermute(value, ("section", "tensor"), along_and_turn)
 
         up(0)
-        residual = lax.ppermute(tie(incoming[0], pres[0][0]), "section", turn)
         for k in range(1, chips):
             if k == 1:
                 up(1)
-                done = (pres[1][0], pres[0][1], residual)
+                done = (pres[1][0], pres[0][1])
                 if chips > 2:
                     blocks[2] = tie(blocks[2], done)
                     done = up(2)
@@ -97,20 +96,28 @@
                 summed = (part[:rows] + sibling(theirs).astype(F32)).astype(BF16)
                 running = send(1, summed)
                 theirs = tie(part[3 * rows :].astype(BF16), summed)
-                own = part[2 * rows : 3 * rows] + sibling(theirs).astype(F32)
-                own = lax.ppermute((own + down_bias[0]).astype(BF16), "section", turn)
+                mine, got = part[2 * rows : 3 * rows], sibling(theirs)
+                own, residual = None, lax.ppermute(tie(incoming[0], done), "section", turn)
                 continue
             if k + 1 < chips:
                 blocks[k + 1] = tie(blocks[k + 1], summed)
-                done = (up(k + 1), running)
+                pre = up(k + 1)
+                done = (pre, running)
+                if k == 2:
+                    residual = lax.ppermute(tie(incoming[0], pre), "section", turn)
             else:
                 done = summed
             part = jnp.dot(act(k, done), down_weight[0], preferred_element_type=F32)
             theirs = part[rows:].astype(BF16)
-            theirs = tie(theirs, pres[k + 1][1] if k + 1 < chips else (running, own))
+            theirs = tie(theirs, (pres[k + 1][1], residual) if k + 1 < chips else (running, own))
             summed = part[:rows] + sibling(theirs).astype(F32) + running.astype(F32)
             summed = summed.astype(BF16)
             running = send(k, summed)
+            if own is None:
+                own = mine + tie(got, summed).astype(F32) + down_bias[0]
+                own = lax.ppermute(own.astype(BF16), "section", turn)
+        if own is None:
+            own = lax.ppermute((mine + got.astype(F32) + down_bias[0]).astype(BF16), "section", turn)
         result = running.astype(F32) + own.astype(F32) + residual.astype(F32)
         return result.astype(BF16)[None]
 

time: 187 us -> 191 us (1.021)
  waiting for transfers between devices: 38.4 us -> 42.9 us
    ppermute x2, waiting for transfers between devices: 1.56 us -> 5.06 us  [the longest x1 3.68 us: per_device(): own = lax.ppermute(own.astype(BF16), 'section', turn)]
    convert_element_type x2, other arithmetic: 1.42 us -> 3.69 us  [per_device(): summed = summed.astype(BF16)]
    ppermute x5, waiting for transfers between devices: 7.59 us -> 5.41 us  [forward(): return lax.ppermute(block, 'tensor', along)]
    ppermute x8, waiting for transfers between devices: 5.29 us -> 7.22 us  [sibling(): return lax.ppermute(block, 'tensor', swap)]
  transfers between devices with their start and end apart: 21 -> 21, of which waited for: 12 -> 14; matrix products, arithmetic and copies ran while one was open for 64% -> 63% of each run, Pallas kernels for 0% -> 0%
where the time goes in v8:
time: 191 us; the launch traced here: 190 us
  matrix products  110 us (58%)
  waiting for transfers between devices  42.9 us (22%)
  starting transfers between devices  22.5 us (12%)
  other arithmetic  12.4 us (6%)
  local copies, waits for them, and re-layouts  2.57 us (1%)
    dot_general x4, matrix products, up(): pre = jnp.dot(both, up_weight[0], preferred_element_type=F32)  59.8 us
    dot_general x2, matrix products, per_device(): part = jnp.dot(act(k, done), down_weight[0], preferred_element_type=F32)  30 us
    dot_general x1, matrix products, per_device(): part = jnp.dot(both, down_weight[0], preferred_element_type=F32)  20.2 us
    ppermute x1, waiting for transfers between devices, send(): return lax.ppermute(value, ('section', 'tensor'), along_and_turn)  19.2 us
    ppermute x5, starting transfers between devices, forward(): return lax.ppermute(block, 'tensor', along)  10 us
    ppermute x5, starting transfers between devices, from_others(): got = lax.ppermute(sent, 'dp', route)  8.01 us
    ppermute x8, waiting for transfers between devices, sibling(): return lax.ppermute(block, 'tensor', swap)  7.22 us
    ppermute x5, waiting for transfers between devices, from_others(): got = lax.ppermute(sent, 'dp', route)  5.98 us
  transfers between devices with their start and end apart: 21, of which 14 were waited for; matrix products, arithmetic and copies ran while one was open for 63% of the time, Pallas kernels for 0%

profile of v8, /device:TPU:0, one launch (start us, length us, event | category | flops | bytes accessed | tf_op | source)
XLA Modules:
  0.0 190.5 jit_solution(13098055017675508741)
XLA Ops:
  1.5 3.0 %collective-permute-start = (f32[2,64]{1,0:T(2,128)S(1)}, f32[2,64]{1,0:T(2,128)S(1)}, u32[]{:S(2)}, u32[]{:S(2)}) collective-permute-start(f32[2,64]{1,0:T(2,128)S(1)} %pad_maximum_fusion), channel_id=1, source_target_pairs={{0,8},{8,0},{1,9},{9,1},{2,10},{10,2},{3,11},{11,3},{4,12},{12,4},... | collective-permute-start | bytes 1544 | tf_op jit(solution)/shard_map/ppermute | solution.py:36
  7.7 3.2 %collective-permute-start.1 = (bf16[64,6144]{1,0:T(8,128)(2,1)S(1)}, bf16[64,6144]{1,0:T(8,128)(2,1)S(1)}, u32[]{:S(2)}, u32[]{:S(2)}) collective-permute-start(bf16[64,6144]{1,0:T(8,128)(2,1)S(1)} %fusion.17), channel_id=1, source_target_pairs={{0,4},{1,5},{4,6},{5,7},{6,2},{7,3},{2,0},{3,1},{8,12},{9,13},{12,... | collective-permute-start | bytes 2359304 | tf_op jit(solution)/shard_map/ppermute | solution.py:27
  10.8 14.4 %fusion.103 = (bf16[128,3072]{1,0:T(8,128)(2,1)S(1)}, f32[128,3072]{1,0:T(8,128)S(1)}) fusion(bf16[1,6144,3072]{2,1,0:T(8,128)(2,1)} %param.10, bf16[64,6144]{1,0:T(8,128)(2,1)S(1)} %collective-permute-done.2, bf16[64,6144]{1,0:T(8,128)(2,1)S(1)} %fusion.17), kind=kOutput, calls=%fused_computation.117 | convolution fusion | flops 4835377152 | bytes 41680896 | tf_op jit(solution)/shard_map/dot_general | solution.py:64
  25.2 3.0 %collective-permute-done.1 = bf16[64,6144]{1,0:T(8,128)(2,1)S(1)} collective-permute-done((bf16[64,6144]{1,0:T(8,128)(2,1)S(1)}, bf16[64,6144]{1,0:T(8,128)(2,1)S(1)}, u32[]{:S(2)}, u32[]{:S(2)}) %collective-permute-start.1) | collective-permute-done | bytes 786464 | tf_op jit(solution)/shard_map/ppermute | solution.py:27
  28.2 3.4 %collective-permute-start.3 = (bf16[64,6144]{1,0:T(8,128)(2,1)S(1)}, bf16[64,6144]{1,0:T(8,128)(2,1)}, u32[]{:S(2)}, u32[]{:S(2)}) collective-permute-start(bf16[64,6144]{1,0:T(8,128)(2,1)S(1)} %collective-permute-done.1), channel_id=1, source_target_pairs={{0,4},{1,5},{4,6},{5,7},{6,2},{7,3},{2,0},{3,1},{8,12},{9,13},{12,... | collective-permute-start | bytes 2359304 | tf_op jit(solution)/shard_map/ppermute | solution.py:27
  33.1 14.4 %fusion.102 = (bf16[128,3072]{1,0:T(8,128)(2,1)S(1)}, f32[128,3072]{1,0:T(8,128)S(1)}) fusion(bf16[1,6144,3072]{2,1,0:T(8,128)(2,1)} %param.10, bf16[64,6144]{1,0:T(8,128)(2,1)S(1)} %collective-permute-done.4, bf16[64,6144]{1,0:T(8,128)(2,1)S(1)} %collective-permute-done.1), kind=kOutput, calls=%fused_computation.116 | convolution fusion | flops 4835377152 | bytes 41680896 | tf_op jit(solution)/shard_map/dot_general | solution.py:64
  47.5 1.6 collective-permute-done.3
  49.1 2.2 %collective-permute-done.5 = bf16[128,3072]{1,0:T(8,128)(2,1)S(1)} collective-permute-done((bf16[128,3072]{1,0:T(8,128)(2,1)S(1)}, bf16[128,3072]{1,0:T(8,128)(2,1)S(1)}, u32[]{:S(2)}, u32[]{:S(2)}) %collective-permute-start.5) | collective-permute-done | bytes 786464 | tf_op jit(solution)/shard_map/ppermute | solution.py:36
  55.1 15.5 %fusion.105 = (bf16[128,3072]{1,0:T(8,128)(2,1)}, f32[128,3072]{1,0:T(8,128)S(1)}) fusion(bf16[1,6144,3072]{2,1,0:T(8,128)(2,1)} %param.10, bf16[64,6144]{1,0:T(8,128)(2,1)S(1)} %collective-permute-done.6, bf16[64,6144]{1,0:T(8,128)(2,1)} %collective-permute-done.3), kind=kOutput, calls=%fused_computation.119 | convolution fusion | flops 4835377152 | bytes 41680896 | tf_op jit(solution)/shard_map/dot_general | solution.py:64
  74.0 20.2 %fusion.104 = (bf16[256,6144]{1,0:T(8,128)(2,1)}, f32[256,6144]{1,0:T(8,128)}) fusion(bf16[1,3072,6144]{2,1,0:T(8,128)(2,1)} %param.12, bf16[128,3072]{1,0:T(8,128)(2,1)S(1)} %get-tuple-element.44, bf16[128,3072]{1,0:T(8,128)(2,1)S(1)} %get-tuple-element.43), kind=kOutput, calls=%fused_computation.118 | convolution fusion | flops 9668395008 | bytes 48758784 | tf_op jit(solution)/shard_map/dot_general | solution.py:92
  94.2 2.4 %fusion.101 = (bf16[64,6144]{1,0:T(8,128)(2,1)}, bf16[64,6144]{1,0:T(8,128)(2,1)S(1)}) fusion(bf16[256,6144]{1,0:T(8,128)(2,1)} %get-tuple-element.49), kind=kLoop, calls=%fused_computation.115 | loop fusion | bytes 3145728 | tf_op jit(solution)/shard_map/slice | solution.py:98
  97.1 2.2 %collective-permute-done.11 = bf16[64,6144]{1,0:T(8,128)(2,1)S(1)} collective-permute-done((bf16[64,6144]{1,0:T(8,128)(2,1)S(1)}, bf16[64,6144]{1,0:T(8,128)(2,1)S(1)}, u32[]{:S(2)}, u32[]{:S(2)}) %collective-permute-start.11) | collective-permute-done | bytes 786464 | tf_op jit(solution)/shard_map/ppermute | solution.py:30
  99.3 1.6 fusion.56
  100.9 1.6 collective-permute-start.13
  102.4 15.6 %fusion.106 = (bf16[128,3072]{1,0:T(8,128)(2,1)}, f32[128,3072]{1,0:T(8,128)S(1)}) fusion(bf16[1,6144,3072]{2,1,0:T(8,128)(2,1)} %param.10, bf16[64,6144]{1,0:T(8,128)(2,1)S(1)} %collective-permute-done.8, bf16[64,6144]{1,0:T(8,128)(2,1)} %collective-permute-done.7), kind=kOutput, calls=%fused_computation.120 | convolution fusion | flops 4835377152 | bytes 41680896 | tf_op jit(solution)/shard_map/dot_general | solution.py:64
  120.8 15.0 %fusion.2 = f32[128,6144]{1,0:T(8,128)S(1)} fusion(bf16[1,3072,6144]{2,1,0:T(8,128)(2,1)} %param.12, f32[128,3072]{1,0:T(8,128)S(1)} %get-tuple-element.52, bf16[128,3072]{1,0:T(8,128)(2,1)} %collective-permute-done.10, f32[3072]{0:T(1024)S(1)} %bitcast.49), kind=kOutput, calls=%fused_computation.2 | convolution fusion | flops 4836556800 | bytes 43266048 | tf_op jit(solution)/shard_map/dot_general | solution.py:110
  137.3 1.6 collective-permute-done.12
  139.4 1.8 collective-permute-done.15
  141.2 2.3 %fusion.55 = bf16[64,6144]{1,0:T(8,128)(2,1)} fusion(f32[128,6144]{1,0:T(8,128)S(1)} %fusion.2, bf16[64,6144]{1,0:T(8,128)(2,1)} %collective-permute-done.13, bf16[64,6144]{1,0:T(8,128)(2,1)S(1)} %collective-permute-done.15), kind=kLoop, calls=%fused_computation.66 | loop fusion | flops 1966080 | bytes 3932160 | tf_op jit(solution)/shard_map/convert_element_type | solution.py:114
  144.1 1.6 fusion.51
  146.3 15.0 %fusion = f32[128,6144]{1,0:T(8,128)S(1)} fusion(bf16[1,3072,6144]{2,1,0:T(8,128)(2,1)} %param.12, f32[128,3072]{1,0:T(8,128)S(1)} %get-tuple-element.54, bf16[128,3072]{1,0:T(8,128)(2,1)} %collective-permute-done.12, f32[3072]{0:T(1024)S(1)} %bitcast.50), kind=kOutput, calls=%fused_computation | convolution fusion | flops 4836556800 | bytes 43266048 | tf_op jit(solution)/shard_map/dot_general | solution.py:110
  161.4 3.7 %collective-permute-done.18 = bf16[64,6144]{1,0:T(8,128)(2,1)S(1)} collective-permute-done((bf16[64,6144]{1,0:T(8,128)(2,1)S(1)}, bf16[64,6144]{1,0:T(8,128)(2,1)S(1)}, u32[]{:S(2)}, u32[]{:S(2)}) %collective-permute-start.18) | collective-permute-done | bytes 786464 | tf_op jit(solution)/shard_map/ppermute | solution.py:118
  165.1 2.3 %collective-permute-done.19 = bf16[64,6144]{1,0:T(8,128)(2,1)S(1)} collective-permute-done((bf16[64,6144]{1,0:T(8,128)(2,1)S(1)}, bf16[64,6144]{1,0:T(8,128)(2,1)S(1)}, u32[]{:S(2)}, u32[]{:S(2)}) %collective-permute-start.19) | collective-permute-done | bytes 786464 | tf_op jit(solution)/shard_map/ppermute | solution.py:30
  170.1 19.2 %collective-permute-done.20 = bf16[64,6144]{1,0:T(8,128)(2,1)S(1)} collective-permute-done((bf16[64,6144]{1,0:T(8,128)(2,1)S(1)}, bf16[64,6144]{1,0:T(8,128)(2,1)S(1)}, u32[]{:S(2)}, u32[]{:S(2)}) %collective-permute-start.20) | collective-permute-done | bytes 786464 | tf_op jit(solution)/shard_map/ppermute | solution.py:81
  (48 shorter events, 23.8 us)
Async XLA Ops:
  1.5 4.5 %collective-permute-start = (f32[2,64]{1,0:T(2,128)S(1)}, f32[2,64]{1,0:T(2,128)S(1)}, u32[]{:S(2)}, u32[]{:S(2)}) collective-permute-start(f32[2,64]{1,0:T(2,128)S(1)} %pad_maximum_fusion), channel_id=1, source_target_pairs={{0,8},{8,0},{1,9},{9,1},{2,10},{10,2},{3,11},{11,3},{4,12},{12,4},... | collective-permute-start | bytes 1544 | tf_op jit(solution)/shard_map/ppermute | solution.py:36
  7.6 3.3 %collective-permute-start.2 = (bf16[64,6144]{1,0:T(8,128)(2,1)S(1)}, bf16[64,6144]{1,0:T(8,128)(2,1)S(1)}, u32[]{:S(2)}, u32[]{:S(2)}) collective-permute-start(bf16[64,6144]{1,0:T(8,128)(2,1)S(1)} %fusion.17), channel_id=1, source_target_pairs={{0,1},{1,0},{2,3},{3,2},{4,5},{5,4},{6,7},{7,6},{8,9},{9,8},{10,11... | collective-permute-start | bytes 2359304 | tf_op jit(solution)/shard_map/ppermute | solution.py:30
  7.7 20.6 %collective-permute-start.1 = (bf16[64,6144]{1,0:T(8,128)(2,1)S(1)}, bf16[64,6144]{1,0:T(8,128)(2,1)S(1)}, u32[]{:S(2)}, u32[]{:S(2)}) collective-permute-start(bf16[64,6144]{1,0:T(8,128)(2,1)S(1)} %fusion.17), channel_id=1, source_target_pairs={{0,4},{1,5},{4,6},{5,7},{6,2},{7,3},{2,0},{3,1},{8,12},{9,13},{12,... | collective-permute-start | bytes 2359304 | tf_op jit(solution)/shard_map/ppermute | solution.py:27
  28.2 4.9 %collective-permute-start.4 = (bf16[64,6144]{1,0:T(8,128)(2,1)S(1)}, bf16[64,6144]{1,0:T(8,128)(2,1)S(1)}, u32[]{:S(2)}, u32[]{:S(2)}) collective-permute-start(bf16[64,6144]{1,0:T(8,128)(2,1)S(1)} %collective-permute-done.1), channel_id=1, source_target_pairs={{0,1},{1,0},{2,3},{3,2},{4,5},{5,4},{6,7},{7,6},{8,9},{9,8},{10,11... | collective-permute-start | bytes 2359304 | tf_op jit(solution)/shard_map/ppermute | solution.py:30
  28.2 20.9 %collective-permute-start.3 = (bf16[64,6144]{1,0:T(8,128)(2,1)S(1)}, bf16[64,6144]{1,0:T(8,128)(2,1)}, u32[]{:S(2)}, u32[]{:S(2)}) collective-permute-start(bf16[64,6144]{1,0:T(8,128)(2,1)S(1)} %collective-permute-done.1), channel_id=1, source_target_pairs={{0,4},{1,5},{4,6},{5,7},{6,2},{7,3},{2,0},{3,1},{8,12},{9,13},{12,... | collective-permute-start | bytes 2359304 | tf_op jit(solution)/shard_map/ppermute | solution.py:27
  31.6 19.7 %collective-permute-start.5 = (bf16[128,3072]{1,0:T(8,128)(2,1)S(1)}, bf16[128,3072]{1,0:T(8,128)(2,1)S(1)}, u32[]{:S(2)}, u32[]{:S(2)}) collective-permute-start(bf16[128,3072]{1,0:T(8,128)(2,1)S(1)} %get-tuple-element.47), channel_id=1, source_target_pairs={{0,8},{8,0},{1,9},{9,1},{2,10},{10,2},{3,11},{11,3},{4,12},{12,4},... | collective-permute-start | bytes 2359304 | tf_op jit(solution)/shard_map/ppermute | solution.py:36
  51.3 2.5 %collective-permute-start.6 = (bf16[64,6144]{1,0:T(8,128)(2,1)}, bf16[64,6144]{1,0:T(8,128)(2,1)S(1)}, u32[]{:S(2)}, u32[]{:S(2)}) collective-permute-start(bf16[64,6144]{1,0:T(8,128)(2,1)} %collective-permute-done.3), channel_id=1, source_target_pairs={{0,1},{1,0},{2,3},{3,2},{4,5},{5,4},{6,7},{7,6},{8,9},{9,8},{10,11... | collective-permute-start | bytes 2359304 | tf_op jit(solution)/shard_map/ppermute | solution.py:30
  51.3 21.4 %copy-start.2 = (f32[1,3072]{1,0:T(1,128)S(1)}, f32[1,3072]{1,0:T(1,128)}, u32[]{:S(2)}) copy-start(f32[1,3072]{1,0:T(1,128)} %param.11) | copy-start | bytes 36868
  51.3 20.0 %collective-permute-start.9 = (bf16[128,3072]{1,0:T(8,128)(2,1)S(1)}, bf16[128,3072]{1,0:T(8,128)(2,1)S(1)}, u32[]{:S(2)}, u32[]{:S(2)}) collective-permute-start(bf16[128,3072]{1,0:T(8,128)(2,1)S(1)} %get-tuple-element.45), channel_id=1, source_target_pairs={{0,8},{8,0},{1,9},{9,1},{2,10},{10,2},{3,11},{11,3},{4,12},{12,4},... | collective-permute-start | bytes 2359304 | tf_op jit(solution)/shard_map/ppermute | solution.py:36
  53.8 42.8 %collective-permute-start.7 = (bf16[64,6144]{1,0:T(8,128)(2,1)}, bf16[64,6144]{1,0:T(8,128)(2,1)}, u32[]{:S(2)}, u32[]{:S(2)}) collective-permute-start(bf16[64,6144]{1,0:T(8,128)(2,1)} %collective-permute-done.3), channel_id=1, source_target_pairs={{0,4},{1,5},{4,6},{5,7},{6,2},{7,3},{2,0},{3,1},{8,12},{9,13},{12,... | collective-permute-start | bytes 2359304 | tf_op jit(solution)/shard_map/ppermute | solution.py:27
  71.3 25.4 %collective-permute-start.10 = (bf16[128,3072]{1,0:T(8,128)(2,1)}, bf16[128,3072]{1,0:T(8,128)(2,1)}, u32[]{:S(2)}, u32[]{:S(2)}) collective-permute-start(bf16[128,3072]{1,0:T(8,128)(2,1)} %get-tuple-element.51), channel_id=1, source_target_pairs={{0,8},{8,0},{1,9},{9,1},{2,10},{10,2},{3,11},{11,3},{4,12},{12,4},... | collective-permute-start | bytes 2359304 | tf_op jit(solution)/shard_map/ppermute | solution.py:36
  96.6 2.7 %collective-permute-start.11 = (bf16[64,6144]{1,0:T(8,128)(2,1)S(1)}, bf16[64,6144]{1,0:T(8,128)(2,1)S(1)}, u32[]{:S(2)}, u32[]{:S(2)}) collective-permute-start(bf16[64,6144]{1,0:T(8,128)(2,1)S(1)} %get-tuple-element.31), channel_id=1, source_target_pairs={{0,1},{1,0},{2,3},{3,2},{4,5},{5,4},{6,7},{7,6},{8,9},{9,8},{10,11... | collective-permute-start | bytes 2359304 | tf_op jit(solution)/shard_map/ppermute | solution.py:30
  96.6 5.8 %collective-permute-start.8 = (bf16[64,6144]{1,0:T(8,128)(2,1)}, bf16[64,6144]{1,0:T(8,128)(2,1)S(1)}, u32[]{:S(2)}, u32[]{:S(2)}) collective-permute-start(bf16[64,6144]{1,0:T(8,128)(2,1)} %collective-permute-done.7), channel_id=1, source_target_pairs={{0,1},{1,0},{2,3},{3,2},{4,5},{5,4},{6,7},{7,6},{8,9},{9,8},{10,11... | collective-permute-start | bytes 2359304 | tf_op jit(solution)/shard_map/ppermute | solution.py:30
  100.9 17.1 %copy-start = (bf16[1,64,6144]{2,1,0:T(8,128)(2,1)S(1)}, bf16[1,64,6144]{2,1,0:T(8,128)(2,1)}, u32[]{:S(2)}) copy-start(bf16[1,64,6144]{2,1,0:T(8,128)(2,1)} %param.7) | copy-start | bytes 2359300
  100.9 20.0 %collective-permute-start.13 = (bf16[64,6144]{1,0:T(8,128)(2,1)S(1)}, bf16[64,6144]{1,0:T(8,128)(2,1)}, u32[]{:S(2)}, u32[]{:S(2)}) collective-permute-start(bf16[64,6144]{1,0:T(8,128)(2,1)S(1)} %fusion.56), channel_id=1, source_target_pairs={{0,4},{1,5},{4,6},{5,7},{6,2},{7,3},{2,0},{3,1},{8,12},{9,13},{12,... | collective-permute-start | bytes 2359304 | tf_op jit(solution)/shard_map/ppermute | solution.py:27
  118.0 19.3 %collective-permute-start.14 = (bf16[64,6144]{1,0:T(8,128)(2,1)S(1)}, bf16[64,6144]{1,0:T(8,128)(2,1)S(1)}, u32[]{:S(2)}, u32[]{:S(2)}) collective-permute-start(bf16[64,6144]{1,0:T(8,128)(2,1)S(1)} %bitcast.47), channel_id=1, source_target_pairs={{0,16},{16,0},{1,17},{17,1},{2,18},{18,2},{3,19},{19,3},{4,20},{20... | collective-permute-start | bytes 2359304 | tf_op jit(solution)/shard_map/ppermute | solution.py:107
  119.5 19.3 %collective-permute-start.12 = (bf16[128,3072]{1,0:T(8,128)(2,1)}, bf16[128,3072]{1,0:T(8,128)(2,1)}, u32[]{:S(2)}, u32[]{:S(2)}) collective-permute-start(bf16[128,3072]{1,0:T(8,128)(2,1)} %get-tuple-element.53), channel_id=1, source_target_pairs={{0,8},{8,0},{1,9},{9,1},{2,10},{10,2},{3,11},{11,3},{4,12},{12,4},... | collective-permute-start | bytes 2359304 | tf_op jit(solution)/shard_map/ppermute | solution.py:36
  138.9 2.3 %collective-permute-start.15 = (bf16[64,6144]{1,0:T(8,128)(2,1)S(1)}, bf16[64,6144]{1,0:T(8,128)(2,1)S(1)}, u32[]{:S(2)}, u32[]{:S(2)}) collective-permute-start(bf16[64,6144]{1,0:T(8,128)(2,1)S(1)} %slice.65), channel_id=1, source_target_pairs={{0,1},{1,0},{2,3},{3,2},{4,5},{5,4},{6,7},{7,6},{8,9},{9,8},{10,11... | collective-permute-start | bytes 2359304 | tf_op jit(solution)/shard_map/ppermute | solution.py:30
  138.9 5.2 %copy-start.3 = (f32[1,6144]{1,0:T(1,128)S(1)}, f32[1,6144]{1,0:T(1,128)}, u32[]{:S(2)}) copy-start(f32[1,6144]{1,0:T(1,128)} %param.13) | copy-start | bytes 73732
  138.9 5.2 %collective-permute-start.17 = (bf16[64,6144]{1,0:T(8,128)(2,1)S(1)}, bf16[64,6144]{1,0:T(8,128)(2,1)S(1)}, u32[]{:S(2)}, u32[]{:S(2)}) collective-permute-start(bf16[64,6144]{1,0:T(8,128)(2,1)S(1)} %copy-done.1), channel_id=1, source_target_pairs={{0,1},{1,0},{2,3},{3,2},{4,5},{5,4},{6,7},{7,6},{8,9},{9,8},{10,11... | collective-permute-start | bytes 2359304 | tf_op jit(solution)/shard_map/ppermute | solution.py:30
  143.4 21.6 %collective-permute-start.16 = (bf16[64,6144]{1,0:T(8,128)(2,1)}, bf16[64,6144]{1,0:T(8,128)(2,1)}, u32[]{:S(2)}, u32[]{:S(2)}) collective-permute-start(bf16[64,6144]{1,0:T(8,128)(2,1)} %fusion.55), channel_id=1, source_target_pairs={{0,4},{1,5},{4,6},{5,7},{6,2},{7,3},{2,0},{3,1},{8,12},{9,13},{12,... | collective-permute-start | bytes 2359304 | tf_op jit(solution)/shard_map/ppermute | solution.py:27
  145.7 19.4 %collective-permute-start.18 = (bf16[64,6144]{1,0:T(8,128)(2,1)S(1)}, bf16[64,6144]{1,0:T(8,128)(2,1)S(1)}, u32[]{:S(2)}, u32[]{:S(2)}) collective-permute-start(bf16[64,6144]{1,0:T(8,128)(2,1)S(1)} %fusion.51), channel_id=1, source_target_pairs={{0,16},{16,0},{1,17},{17,1},{2,18},{18,2},{3,19},{19,3},{4,20},{20... | collective-permute-start | bytes 2359304 | tf_op jit(solution)/shard_map/ppermute | solution.py:118
  165.1 2.3 %collective-permute-start.19 = (bf16[64,6144]{1,0:T(8,128)(2,1)S(1)}, bf16[64,6144]{1,0:T(8,128)(2,1)S(1)}, u32[]{:S(2)}, u32[]{:S(2)}) collective-permute-start(bf16[64,6144]{1,0:T(8,128)(2,1)S(1)} %slice.64), channel_id=1, source_target_pairs={{0,1},{1,0},{2,3},{3,2},{4,5},{5,4},{6,7},{7,6},{8,9},{9,8},{10,11... | collective-permute-start | bytes 2359304 | tf_op jit(solution)/shard_map/ppermute | solution.py:30
  168.8 20.5 %collective-permute-start.20 = (bf16[64,6144]{1,0:T(8,128)(2,1)S(1)}, bf16[64,6144]{1,0:T(8,128)(2,1)S(1)}, u32[]{:S(2)}, u32[]{:S(2)}) collective-permute-start(bf16[64,6144]{1,0:T(8,128)(2,1)S(1)} %fusion.53), channel_id=1, source_target_pairs={{0,20},{1,21},{4,22},{5,23},{6,18},{7,19},{2,16},{3,17},{16,4},{17... | collective-permute-start | bytes 2359304 | tf_op jit(solution)/shard_map/ppermute | solution.py:81
  (1 other events, 3.0 us)

commit v9 on v4

--- a/solution.py
+++ b/solution.py
@@ -81,11 +81,10 @@
             return lax.ppermute(value, ("section", "tensor"), along_and_turn)
 
         up(0)
-        residual = lax.ppermute(tie(incoming[0], pres[0][0]), "section", turn)
         for k in range(1, chips):
             if k == 1:
                 up(1)
-                done = (pres[1][0], pres[0][1], residual)
+                done = (pres[1][0], pres[0][1])
                 if chips > 2:
                     blocks[2] = tie(blocks[2], done)
                     done = up(2)
@@ -98,7 +97,7 @@
                 running = send(1, summed)
                 theirs = tie(part[3 * rows :].astype(BF16), summed)
                 own = part[2 * rows : 3 * rows] + sibling(theirs).astype(F32)
-                own = lax.ppermute((own + down_bias[0]).astype(BF16), "section", turn)
+                own = lax.ppermute((own + down_bias[0] + x).astype(BF16), "section", turn)
                 continue
             if k + 1 < chips:
                 blocks[k + 1] = tie(blocks[k + 1], summed)
@@ -111,7 +110,7 @@
             summed = part[:rows] + sibling(theirs).astype(F32) + running.astype(F32)
             summed = summed.astype(BF16)
             running = send(k, summed)
-        result = running.astype(F32) + own.astype(F32) + residual.astype(F32)
+        result = running.astype(F32) + own.astype(F32)
         return result.astype(BF16)[None]
 
     return per_device

time: 187 us -> 186 us (level)
  waiting for transfers between devices: 38.4 us -> 42 us
    ppermute x5, waiting for transfers between devices: 7.59 us -> 9.5 us  [forward(): return lax.ppermute(block, 'tensor', along)]
  transfers between devices with their start and end apart: 21 -> 20, of which waited for: 12 -> 13; matrix products, arithmetic and copies ran while one was open for 64% -> 63% of each run, Pallas kernels for 0% -> 0%
where the time goes in v9:
time: 186 us
  matrix products  110 us (59%)
  waiting for transfers between devices  42 us (23%)
  starting transfers between devices  22 us (12%)
  other arithmetic  10.2 us (5%)
    dot_general x4, matrix products, up(): pre = jnp.dot(both, up_weight[0], preferred_element_type=F32)  59.7 us
    dot_general x2, matrix products, per_device(): part = jnp.dot(act(k, done), down_weight[0], preferred_element_type=F32)  30 us
    dot_general x1, matrix products, per_device(): part = jnp.dot(both, down_weight[0], preferred_element_type=F32)  20.2 us
    ppermute x1, waiting for transfers between devices, send(): return lax.ppermute(value, ('section', 'tensor'), along_and_turn)  19 us
    ppermute x5, starting transfers between devices, forward(): return lax.ppermute(block, 'tensor', along)  10.2 us
    ppermute x5, waiting for transfers between devices, forward(): return lax.ppermute(block, 'tensor', along)  9.5 us
    ppermute x5, starting transfers between devices, from_others(): got = lax.ppermute(sent, 'dp', route)  8.01 us
    ppermute x5, waiting for transfers between devices, from_others(): got = lax.ppermute(sent, 'dp', route)  6.81 us
  transfers between devices with their start and end apart: 20, of which 13 were waited for; matrix products, arithmetic and copies ran while one was open for 63% of the time, Pallas kernels for 0%

profile of v9, /device:TPU:0, one launch (start us, length us, event | category | flops | bytes accessed | tf_op | source)
XLA Modules:
  0.0 185.8 jit_solution(6989254123963229182)
XLA Ops:
  1.5 3.0 %collective-permute-start = (f32[2,64]{1,0:T(2,128)S(1)}, f32[2,64]{1,0:T(2,128)S(1)}, u32[]{:S(2)}, u32[]{:S(2)}) collective-permute-start(f32[2,64]{1,0:T(2,128)S(1)} %pad_maximum_fusion), channel_id=1, source_target_pairs={{0,8},{8,0},{1,9},{9,1},{2,10},{10,2},{3,11},{11,3},{4,12},{12,4},... | collective-permute-start | bytes 1544 | tf_op jit(solution)/shard_map/ppermute | solution.py:36
  4.5 1.5 collective-permute-done
  7.6 3.2 %collective-permute-start.1 = (bf16[64,6144]{1,0:T(8,128)(2,1)S(1)}, bf16[64,6144]{1,0:T(8,128)(2,1)S(1)}, u32[]{:S(2)}, u32[]{:S(2)}) collective-permute-start(bf16[64,6144]{1,0:T(8,128)(2,1)S(1)} %fusion.49), channel_id=1, source_target_pairs={{0,4},{1,5},{4,6},{5,7},{6,2},{7,3},{2,0},{3,1},{8,12},{9,13},{12,... | collective-permute-start | bytes 2359304 | tf_op jit(solution)/shard_map/ppermute | solution.py:27
  10.8 14.4 %fusion.103 = (bf16[128,3072]{1,0:T(8,128)(2,1)S(1)}, f32[128,3072]{1,0:T(8,128)S(1)}) fusion(bf16[1,6144,3072]{2,1,0:T(8,128)(2,1)} %param.10, bf16[64,6144]{1,0:T(8,128)(2,1)S(1)} %collective-permute-done.2, bf16[64,6144]{1,0:T(8,128)(2,1)S(1)} %fusion.49), kind=kOutput, calls=%fused_computation.119 | convolution fusion | flops 4835377152 | bytes 41680896 | tf_op jit(solution)/shard_map/dot_general | solution.py:64
  25.2 3.0 %collective-permute-done.1 = bf16[64,6144]{1,0:T(8,128)(2,1)S(1)} collective-permute-done((bf16[64,6144]{1,0:T(8,128)(2,1)S(1)}, bf16[64,6144]{1,0:T(8,128)(2,1)S(1)}, u32[]{:S(2)}, u32[]{:S(2)}) %collective-permute-start.1) | collective-permute-done | bytes 786464 | tf_op jit(solution)/shard_map/ppermute | solution.py:27
  28.2 3.4 %collective-permute-start.3 = (bf16[64,6144]{1,0:T(8,128)(2,1)S(1)}, bf16[64,6144]{1,0:T(8,128)(2,1)}, u32[]{:S(2)}, u32[]{:S(2)}) collective-permute-start(bf16[64,6144]{1,0:T(8,128)(2,1)S(1)} %collective-permute-done.1), channel_id=1, source_target_pairs={{0,4},{1,5},{4,6},{5,7},{6,2},{7,3},{2,0},{3,1},{8,12},{9,13},{12,... | collective-permute-start | bytes 2359304 | tf_op jit(solution)/shard_map/ppermute | solution.py:27
  33.1 14.4 %fusion.102 = (bf16[128,3072]{1,0:T(8,128)(2,1)S(1)}, f32[128,3072]{1,0:T(8,128)S(1)}) fusion(bf16[1,6144,3072]{2,1,0:T(8,128)(2,1)} %param.10, bf16[64,6144]{1,0:T(8,128)(2,1)S(1)} %collective-permute-done.4, bf16[64,6144]{1,0:T(8,128)(2,1)S(1)} %collective-permute-done.1), kind=kOutput, calls=%fused_computation.118 | convolution fusion | flops 4835377152 | bytes 41680896 | tf_op jit(solution)/shard_map/dot_general | solution.py:64
  47.5 1.6 collective-permute-done.3
  49.1 2.2 %collective-permute-done.5 = bf16[128,3072]{1,0:T(8,128)(2,1)S(1)} collective-permute-done((bf16[128,3072]{1,0:T(8,128)(2,1)S(1)}, bf16[128,3072]{1,0:T(8,128)(2,1)S(1)}, u32[]{:S(2)}, u32[]{:S(2)}) %collective-permute-start.5) | collective-permute-done | bytes 786464 | tf_op jit(solution)/shard_map/ppermute | solution.py:36
  55.1 15.5 %fusion.105 = (bf16[128,3072]{1,0:T(8,128)(2,1)}, f32[128,3072]{1,0:T(8,128)S(1)}) fusion(bf16[1,6144,3072]{2,1,0:T(8,128)(2,1)} %param.10, bf16[64,6144]{1,0:T(8,128)(2,1)S(1)} %collective-permute-done.6, bf16[64,6144]{1,0:T(8,128)(2,1)} %collective-permute-done.3), kind=kOutput, calls=%fused_computation.121 | convolution fusion | flops 4835377152 | bytes 41680896 | tf_op jit(solution)/shard_map/dot_general | solution.py:64
  74.0 20.2 %fusion.104 = (bf16[256,6144]{1,0:T(8,128)(2,1)}, f32[256,6144]{1,0:T(8,128)}) fusion(bf16[1,3072,6144]{2,1,0:T(8,128)(2,1)} %param.12, bf16[128,3072]{1,0:T(8,128)(2,1)S(1)} %get-tuple-element.40, bf16[128,3072]{1,0:T(8,128)(2,1)S(1)} %get-tuple-element.39), kind=kOutput, calls=%fused_computation.120 | convolution fusion | flops 9668395008 | bytes 48758784 | tf_op jit(solution)/shard_map/dot_general | solution.py:92
  96.3 2.0 %collective-permute-done.11 = bf16[64,6144]{1,0:T(8,128)(2,1)S(1)} collective-permute-done((bf16[64,6144]{1,0:T(8,128)(2,1)S(1)}, bf16[64,6144]{1,0:T(8,128)(2,1)S(1)}, u32[]{:S(2)}, u32[]{:S(2)}) %collective-permute-start.11) | collective-permute-done | bytes 786464 | tf_op jit(solution)/shard_map/ppermute | solution.py:30
  98.3 1.6 fusion.56
  99.9 1.6 collective-permute-start.13
  101.4 15.5 %fusion.106 = (bf16[128,3072]{1,0:T(8,128)(2,1)}, f32[128,3072]{1,0:T(8,128)S(1)}) fusion(bf16[1,6144,3072]{2,1,0:T(8,128)(2,1)} %param.10, bf16[64,6144]{1,0:T(8,128)(2,1)S(1)} %collective-permute-done.8, bf16[64,6144]{1,0:T(8,128)(2,1)} %collective-permute-done.7), kind=kOutput, calls=%fused_computation.122 | convolution fusion | flops 4835377152 | bytes 41680896 | tf_op jit(solution)/shard_map/dot_general | solution.py:64
  117.5 2.3 %collective-permute-done.13 = bf16[64,6144]{1,0:T(8,128)(2,1)S(1)} collective-permute-done((bf16[64,6144]{1,0:T(8,128)(2,1)S(1)}, bf16[64,6144]{1,0:T(8,128)(2,1)S(1)}, u32[]{:S(2)}, u32[]{:S(2)}) %collective-permute-start.13) | collective-permute-done | bytes 786464 | tf_op jit(solution)/shard_map/ppermute | solution.py:27
  119.7 15.0 %fusion.2 = f32[128,6144]{1,0:T(8,128)S(1)} fusion(bf16[1,3072,6144]{2,1,0:T(8,128)(2,1)} %param.12, f32[128,3072]{1,0:T(8,128)S(1)} %get-tuple-element.48, bf16[128,3072]{1,0:T(8,128)(2,1)} %collective-permute-done.10, f32[3072]{0:T(1024)S(1)} %bitcast.50), kind=kOutput, calls=%fused_computation.2 | convolution fusion | flops 4836556800 | bytes 43266048 | tf_op jit(solution)/shard_map/dot_general | solution.py:107
  134.8 2.3 %collective-permute-done.12 = bf16[128,3072]{1,0:T(8,128)(2,1)} collective-permute-done((bf16[128,3072]{1,0:T(8,128)(2,1)}, bf16[128,3072]{1,0:T(8,128)(2,1)}, u32[]{:S(2)}, u32[]{:S(2)}) %collective-permute-start.12) | collective-permute-done | bytes 786464 | tf_op jit(solution)/shard_map/ppermute | solution.py:36
  137.2 1.9 %fusion.50 = bf16[64,6144]{1,0:T(8,128)(2,1)S(1)} fusion(f32[256,6144]{1,0:T(8,128)} %get-tuple-element.46, bf16[64,6144]{1,0:T(8,128)(2,1)} %collective-permute-done.16, bf16[1,64,6144]{2,1,0:T(8,128)(2,1)S(1)} %copy-done, f32[6144]{0:T(1024)S(1)} %bitcast.52), kind=kLoop, calls=%fused_computation.58 | loop fusion | flops 2359296 | bytes 3956736 | tf_op jit(solution)/shard_map/convert_element_type | solution.py:100
  139.1 1.6 collective-permute-start.17
  142.7 15.0 %fusion = f32[128,6144]{1,0:T(8,128)S(1)} fusion(bf16[1,3072,6144]{2,1,0:T(8,128)(2,1)} %param.12, f32[128,3072]{1,0:T(8,128)S(1)} %get-tuple-element.50, bf16[128,3072]{1,0:T(8,128)(2,1)} %collective-permute-done.12, f32[3072]{0:T(1024)S(1)} %bitcast.51), kind=kOutput, calls=%fused_computation | convolution fusion | flops 4836556800 | bytes 43266048 | tf_op jit(solution)/shard_map/dot_general | solution.py:107
  159.1 2.6 %collective-permute-done.15 = bf16[64,6144]{1,0:T(8,128)(2,1)S(1)} collective-permute-done((bf16[64,6144]{1,0:T(8,128)(2,1)}, bf16[64,6144]{1,0:T(8,128)(2,1)S(1)}, u32[]{:S(2)}, u32[]{:S(2)}) %collective-permute-start.15) | collective-permute-done | bytes 786464 | tf_op jit(solution)/shard_map/ppermute | solution.py:27
  161.7 2.3 %collective-permute-done.18 = bf16[64,6144]{1,0:T(8,128)(2,1)S(1)} collective-permute-done((bf16[64,6144]{1,0:T(8,128)(2,1)S(1)}, bf16[64,6144]{1,0:T(8,128)(2,1)S(1)}, u32[]{:S(2)}, u32[]{:S(2)}) %collective-permute-start.18) | collective-permute-done | bytes 786464 | tf_op jit(solution)/shard_map/ppermute | solution.py:30
  165.8 19.0 %collective-permute-done.19 = bf16[64,6144]{1,0:T(8,128)(2,1)S(1)} collective-permute-done((bf16[64,6144]{1,0:T(8,128)(2,1)S(1)}, bf16[64,6144]{1,0:T(8,128)(2,1)S(1)}, u32[]{:S(2)}, u32[]{:S(2)}) %collective-permute-start.19) | collective-permute-done | bytes 786464 | tf_op jit(solution)/shard_map/ppermute | solution.py:81
  (44 shorter events, 20.7 us)
Async XLA Ops:
  1.5 4.5 %collective-permute-start = (f32[2,64]{1,0:T(2,128)S(1)}, f32[2,64]{1,0:T(2,128)S(1)}, u32[]{:S(2)}, u32[]{:S(2)}) collective-permute-start(f32[2,64]{1,0:T(2,128)S(1)} %pad_maximum_fusion), channel_id=1, source_target_pairs={{0,8},{8,0},{1,9},{9,1},{2,10},{10,2},{3,11},{11,3},{4,12},{12,4},... | collective-permute-start | bytes 1544 | tf_op jit(solution)/shard_map/ppermute | solution.py:36
  7.6 3.3 %collective-permute-start.2 = (bf16[64,6144]{1,0:T(8,128)(2,1)S(1)}, bf16[64,6144]{1,0:T(8,128)(2,1)S(1)}, u32[]{:S(2)}, u32[]{:S(2)}) collective-permute-start(bf16[64,6144]{1,0:T(8,128)(2,1)S(1)} %fusion.49), channel_id=1, source_target_pairs={{0,1},{1,0},{2,3},{3,2},{4,5},{5,4},{6,7},{7,6},{8,9},{9,8},{10,11... | collective-permute-start | bytes 2359304 | tf_op jit(solution)/shard_map/ppermute | solution.py:30
  7.6 20.6 %collective-permute-start.1 = (bf16[64,6144]{1,0:T(8,128)(2,1)S(1)}, bf16[64,6144]{1,0:T(8,128)(2,1)S(1)}, u32[]{:S(2)}, u32[]{:S(2)}) collective-permute-start(bf16[64,6144]{1,0:T(8,128)(2,1)S(1)} %fusion.49), channel_id=1, source_target_pairs={{0,4},{1,5},{4,6},{5,7},{6,2},{7,3},{2,0},{3,1},{8,12},{9,13},{12,... | collective-permute-start | bytes 2359304 | tf_op jit(solution)/shard_map/ppermute | solution.py:27
  28.2 4.9 %collective-permute-start.4 = (bf16[64,6144]{1,0:T(8,128)(2,1)S(1)}, bf16[64,6144]{1,0:T(8,128)(2,1)S(1)}, u32[]{:S(2)}, u32[]{:S(2)}) collective-permute-start(bf16[64,6144]{1,0:T(8,128)(2,1)S(1)} %collective-permute-done.1), channel_id=1, source_target_pairs={{0,1},{1,0},{2,3},{3,2},{4,5},{5,4},{6,7},{7,6},{8,9},{9,8},{10,11... | collective-permute-start | bytes 2359304 | tf_op jit(solution)/shard_map/ppermute | solution.py:30
  28.2 20.9 %collective-permute-start.3 = (bf16[64,6144]{1,0:T(8,128)(2,1)S(1)}, bf16[64,6144]{1,0:T(8,128)(2,1)}, u32[]{:S(2)}, u32[]{:S(2)}) collective-permute-start(bf16[64,6144]{1,0:T(8,128)(2,1)S(1)} %collective-permute-done.1), channel_id=1, source_target_pairs={{0,4},{1,5},{4,6},{5,7},{6,2},{7,3},{2,0},{3,1},{8,12},{9,13},{12,... | collective-permute-start | bytes 2359304 | tf_op jit(solution)/shard_map/ppermute | solution.py:27
  31.6 19.7 %collective-permute-start.5 = (bf16[128,3072]{1,0:T(8,128)(2,1)S(1)}, bf16[128,3072]{1,0:T(8,128)(2,1)S(1)}, u32[]{:S(2)}, u32[]{:S(2)}) collective-permute-start(bf16[128,3072]{1,0:T(8,128)(2,1)S(1)} %get-tuple-element.43), channel_id=1, source_target_pairs={{0,8},{8,0},{1,9},{9,1},{2,10},{10,2},{3,11},{11,3},{4,12},{12,4},... | collective-permute-start | bytes 2359304 | tf_op jit(solution)/shard_map/ppermute | solution.py:36
  51.3 2.5 %collective-permute-start.6 = (bf16[64,6144]{1,0:T(8,128)(2,1)}, bf16[64,6144]{1,0:T(8,128)(2,1)S(1)}, u32[]{:S(2)}, u32[]{:S(2)}) collective-permute-start(bf16[64,6144]{1,0:T(8,128)(2,1)} %collective-permute-done.3), channel_id=1, source_target_pairs={{0,1},{1,0},{2,3},{3,2},{4,5},{5,4},{6,7},{7,6},{8,9},{9,8},{10,11... | collective-permute-start | bytes 2359304 | tf_op jit(solution)/shard_map/ppermute | solution.py:30
  51.3 21.4 %copy-start.1 = (f32[1,3072]{1,0:T(1,128)S(1)}, f32[1,3072]{1,0:T(1,128)}, u32[]{:S(2)}) copy-start(f32[1,3072]{1,0:T(1,128)} %param.11) | copy-start | bytes 36868
  51.3 20.0 %collective-permute-start.9 = (bf16[128,3072]{1,0:T(8,128)(2,1)S(1)}, bf16[128,3072]{1,0:T(8,128)(2,1)S(1)}, u32[]{:S(2)}, u32[]{:S(2)}) collective-permute-start(bf16[128,3072]{1,0:T(8,128)(2,1)S(1)} %get-tuple-element.41), channel_id=1, source_target_pairs={{0,8},{8,0},{1,9},{9,1},{2,10},{10,2},{3,11},{11,3},{4,12},{12,4},... | collective-permute-start | bytes 2359304 | tf_op jit(solution)/shard_map/ppermute | solution.py:36
  53.8 42.0 %collective-permute-start.7 = (bf16[64,6144]{1,0:T(8,128)(2,1)}, bf16[64,6144]{1,0:T(8,128)(2,1)}, u32[]{:S(2)}, u32[]{:S(2)}) collective-permute-start(bf16[64,6144]{1,0:T(8,128)(2,1)} %collective-permute-done.3), channel_id=1, source_target_pairs={{0,4},{1,5},{4,6},{5,7},{6,2},{7,3},{2,0},{3,1},{8,12},{9,13},{12,... | collective-permute-start | bytes 2359304 | tf_op jit(solution)/shard_map/ppermute | solution.py:27
  71.2 24.5 %collective-permute-start.10 = (bf16[128,3072]{1,0:T(8,128)(2,1)}, bf16[128,3072]{1,0:T(8,128)(2,1)}, u32[]{:S(2)}, u32[]{:S(2)}) collective-permute-start(bf16[128,3072]{1,0:T(8,128)(2,1)} %get-tuple-element.47), channel_id=1, source_target_pairs={{0,8},{8,0},{1,9},{9,1},{2,10},{10,2},{3,11},{11,3},{4,12},{12,4},... | collective-permute-start | bytes 2359304 | tf_op jit(solution)/shard_map/ppermute | solution.py:36
  95.7 2.6 %collective-permute-start.11 = (bf16[64,6144]{1,0:T(8,128)(2,1)S(1)}, bf16[64,6144]{1,0:T(8,128)(2,1)S(1)}, u32[]{:S(2)}, u32[]{:S(2)}) collective-permute-start(bf16[64,6144]{1,0:T(8,128)(2,1)S(1)} %get-tuple-element.29), channel_id=1, source_target_pairs={{0,1},{1,0},{2,3},{3,2},{4,5},{5,4},{6,7},{7,6},{8,9},{9,8},{10,11... | collective-permute-start | bytes 2359304 | tf_op jit(solution)/shard_map/ppermute | solution.py:30
  95.8 5.6 %collective-permute-start.8 = (bf16[64,6144]{1,0:T(8,128)(2,1)}, bf16[64,6144]{1,0:T(8,128)(2,1)S(1)}, u32[]{:S(2)}, u32[]{:S(2)}) collective-permute-start(bf16[64,6144]{1,0:T(8,128)(2,1)} %collective-permute-done.7), channel_id=1, source_target_pairs={{0,1},{1,0},{2,3},{3,2},{4,5},{5,4},{6,7},{7,6},{8,9},{9,8},{10,11... | collective-permute-start | bytes 2359304 | tf_op jit(solution)/shard_map/ppermute | solution.py:30
  99.9 19.9 %collective-permute-start.13 = (bf16[64,6144]{1,0:T(8,128)(2,1)S(1)}, bf16[64,6144]{1,0:T(8,128)(2,1)S(1)}, u32[]{:S(2)}, u32[]{:S(2)}) collective-permute-start(bf16[64,6144]{1,0:T(8,128)(2,1)S(1)} %fusion.56), channel_id=1, source_target_pairs={{0,4},{1,5},{4,6},{5,7},{6,2},{7,3},{2,0},{3,1},{8,12},{9,13},{12,... | collective-permute-start | bytes 2359304 | tf_op jit(solution)/shard_map/ppermute | solution.py:27
  101.4 35.7 %collective-permute-start.16 = (bf16[64,6144]{1,0:T(8,128)(2,1)S(1)}, bf16[64,6144]{1,0:T(8,128)(2,1)}, u32[]{:S(2)}, u32[]{:S(2)}) collective-permute-start(bf16[64,6144]{1,0:T(8,128)(2,1)S(1)} %get-tuple-element.35), channel_id=1, source_target_pairs={{0,1},{1,0},{2,3},{3,2},{4,5},{5,4},{6,7},{7,6},{8,9},{9,8},{10,11... | collective-permute-start | bytes 2359304 | tf_op jit(solution)/shard_map/ppermute | solution.py:30
  116.9 20.3 %collective-permute-start.12 = (bf16[128,3072]{1,0:T(8,128)(2,1)}, bf16[128,3072]{1,0:T(8,128)(2,1)}, u32[]{:S(2)}, u32[]{:S(2)}) collective-permute-start(bf16[128,3072]{1,0:T(8,128)(2,1)} %get-tuple-element.49), channel_id=1, source_target_pairs={{0,8},{8,0},{1,9},{9,1},{2,10},{10,2},{3,11},{11,3},{4,12},{12,4},... | collective-permute-start | bytes 2359304 | tf_op jit(solution)/shard_map/ppermute | solution.py:36
  134.7 2.5 %copy-start = (bf16[1,64,6144]{2,1,0:T(8,128)(2,1)S(1)}, bf16[1,64,6144]{2,1,0:T(8,128)(2,1)}, u32[]{:S(2)}) copy-start(bf16[1,64,6144]{2,1,0:T(8,128)(2,1)} %param.7) | copy-start | bytes 2359300
  134.7 2.5 %copy-start.2 = (f32[1,6144]{1,0:T(1,128)S(1)}, f32[1,6144]{1,0:T(1,128)}, u32[]{:S(2)}) copy-start(f32[1,6144]{1,0:T(1,128)} %param.13) | copy-start | bytes 73732
  137.2 3.5 %collective-permute-start.14 = (bf16[64,6144]{1,0:T(8,128)(2,1)S(1)}, bf16[64,6144]{1,0:T(8,128)(2,1)S(1)}, u32[]{:S(2)}, u32[]{:S(2)}) collective-permute-start(bf16[64,6144]{1,0:T(8,128)(2,1)S(1)} %slice.65), channel_id=1, source_target_pairs={{0,1},{1,0},{2,3},{3,2},{4,5},{5,4},{6,7},{7,6},{8,9},{9,8},{10,11... | collective-permute-start | bytes 2359304 | tf_op jit(solution)/shard_map/ppermute | solution.py:30
  139.1 20.0 %collective-permute-start.17 = (bf16[64,6144]{1,0:T(8,128)(2,1)S(1)}, bf16[64,6144]{1,0:T(8,128)(2,1)S(1)}, u32[]{:S(2)}, u32[]{:S(2)}) collective-permute-start(bf16[64,6144]{1,0:T(8,128)(2,1)S(1)} %fusion.50), channel_id=1, source_target_pairs={{0,16},{16,0},{1,17},{17,1},{2,18},{18,2},{3,19},{19,3},{4,20},{20... | collective-permute-start | bytes 2359304 | tf_op jit(solution)/shard_map/ppermute | solution.py:100
  141.8 19.9 %collective-permute-start.15 = (bf16[64,6144]{1,0:T(8,128)(2,1)}, bf16[64,6144]{1,0:T(8,128)(2,1)S(1)}, u32[]{:S(2)}, u32[]{:S(2)}) collective-permute-start(bf16[64,6144]{1,0:T(8,128)(2,1)} %fusion.55), channel_id=1, source_target_pairs={{0,4},{1,5},{4,6},{5,7},{6,2},{7,3},{2,0},{3,1},{8,12},{9,13},{12,... | collective-permute-start | bytes 2359304 | tf_op jit(solution)/shard_map/ppermute | solution.py:27
  161.7 2.3 %collective-permute-start.18 = (bf16[64,6144]{1,0:T(8,128)(2,1)S(1)}, bf16[64,6144]{1,0:T(8,128)(2,1)S(1)}, u32[]{:S(2)}, u32[]{:S(2)}) collective-permute-start(bf16[64,6144]{1,0:T(8,128)(2,1)S(1)} %slice.64), channel_id=1, source_target_pairs={{0,1},{1,0},{2,3},{3,2},{4,5},{5,4},{6,7},{7,6},{8,9},{9,8},{10,11... | collective-permute-start | bytes 2359304 | tf_op jit(solution)/shard_map/ppermute | solution.py:30
  164.2 20.5 %collective-permute-start.19 = (bf16[64,6144]{1,0:T(8,128)(2,1)S(1)}, bf16[64,6144]{1,0:T(8,128)(2,1)S(1)}, u32[]{:S(2)}, u32[]{:S(2)}) collective-permute-start(bf16[64,6144]{1,0:T(8,128)(2,1)S(1)} %fusion.53), channel_id=1, source_target_pairs={{0,20},{1,21},{4,22},{5,23},{6,18},{7,19},{2,16},{3,17},{16,4},{17... | collective-permute-start | bytes 2359304 | tf_op jit(solution)/shard_map/ppermute | solution.py:81
